TPU v7x, 32 devices: a whole 2x2x4 slice. The times are simulated.
32 devices in a mesh: member: 2 (over y), gx: 4 (over z), gy: 2 (over x), tracer: 2 (over core).
Axes of the slice: x: 2, y: 2, z: 4, core: 2. Of those that a mesh axis runs over, the one named last changes fastest.
Arguments:
- tracers: bfloat16 [128, 32, 512], P(('member', 'tracer'), 'gx', 'gy'), parts along dimension 0, may hold values from 0.5 to 2
- cotangent: bfloat16 [128, 32, 512], P(('member', 'tracer'), 'gx', 'gy'), parts along dimension 0, may hold values from -6 to 6
- winds: float32 [8, 32, 512], P('member', 'gx', 'gy'), parts along dimension 0, may hold values from -1 to 1
- levels: int32 [128], P(('member', 'tracer')), parts along dimension 0, may hold values from 0 to 1
- conv1: float32 [32, 36], replicated, may hold values from -1 to 1
- bias1: float32 [32], replicated, may hold values from -0.5 to 0.5
- conv2: float32 [32, 288], replicated, may hold values from -0.375 to 0.375
- bias2: float32 [32], replicated, may hold values from -0.5 to 0.5
- head: float32 [18, 32], replicated, may hold values from -1 to 1
Outputs:
- tracer_grad: bfloat16 [128, 32, 512], P(('member', 'tracer'), 'gx', 'gy'), parts along dimension 0
- wind_grad: float32 [8, 32, 512], P('member', 'gx', 'gy'), parts along dimension 0
- conv1_grad: float32 [64, 36], P('member'), parts along dimension 0
- bias1_grad: float32 [64], P('member'), parts along dimension 0
- conv2_grad: float32 [64, 288], P('member'), parts along dimension 0
- bias2_grad: float32 [64], P('member'), parts along dimension 0
- head_grad: float32 [36, 32], P('member'), parts along dimension 0
There are 2 independent parts, one for each index of `member`. A program takes and returns all parts, laid end to end along the dimension named above; an argument that names none is the same for every part. Nothing has to cross between parts.
All inputs are finite; a program needn't handle non-finite values.
Results may differ from a plain program's by a relative error of at most 0.001.
Values may be sent and summed in bfloat16 or wider, within the bound.
No kernel may reach another device: no remote copies, remote signals or barrier semaphores. Data moves between devices by JAX's collectives and lax.ppermute only.
A program may use at most 64 MiB of HBM per device.

v0:
```python
import jax
import jax.numpy as jnp
from jax import lax
from jax.sharding import PartitionSpec as P

LEVELS = 2


COURANT = 0.5
CORRECTION = 0.2
OFFSETS = tuple(((step_x, step_y) for step_x in (-1, 0, 1) for step_y in (-1, 0, 1)))


def with_halo(array, sides, width, wrap):
    for axis, dim in sides:
        size, length = (lax.axis_size(axis), array.shape[dim])
        up = [(i, (i + 1) % size) for i in range(size if wrap else size - 1)]
        down = [(j, i) for i, j in up]
        last = lax.slice_in_dim(array, length - width, length, axis=dim)
        first = lax.slice_in_dim(array, 0, width, axis=dim)
        before = lax.ppermute(last, axis, up)
        after = lax.ppermute(first, axis, down)
        array = jnp.concatenate([before, array, after], axis=dim)
    return array


def extend(field):
    wider = with_halo(field, (("gx", 1),), 1, True)
    return with_halo(wider, (("gy", 2),), 1, False)


def extend_tracers(field):
    wider = with_halo(field, (("gx", 1),), 1, True)
    return with_halo(wider, (("gy", 2),), 1, False)


def window(field, start_x, start_y, tile_rows, tile_cols):
    return field[:, start_x : start_x + tile_rows, start_y : start_y + tile_cols]


def lax_wendroff(courant):
    return jnp.stack(
        [
            0.5 * courant + 0.5 * courant * courant,
            1.0 - courant * courant,
            0.5 * courant * courant - 0.5 * courant,
        ],
        axis=1,
    )


def coef_cells(winds, hidden, head):
    paired = winds.reshape((LEVELS, 2) + winds.shape[1:]) * COURANT
    along_x = lax_wendroff(paired[:, 0])
    along_y = lax_wendroff(paired[:, 1])
    base = (along_x[:, :, None] * along_y[:, None, :]).reshape((LEVELS, 9) + winds.shape[1:])
    raw = jnp.einsum("kc,cxy->kxy", head, hidden, precision=lax.Precision.HIGHEST)
    raw = raw.reshape((LEVELS, 9) + winds.shape[1:])
    return base + CORRECTION * (raw - jnp.mean(raw, axis=1, keepdims=True))


def convolve_local(padded, weights, biases):
    tile_rows = padded.shape[1] - 2
    tile_cols = padded.shape[2] - 2
    kernel = weights.reshape(weights.shape[0], padded.shape[0], 9)
    total = jnp.zeros((weights.shape[0], tile_rows, tile_cols), jnp.float32) + biases[:, None, None]
    for offset, (step_x, step_y) in enumerate(OFFSETS):
        total = total + jnp.einsum(
            "oi,ixy->oxy",
            kernel[:, :, offset],
            window(padded, 1 + step_x, 1 + step_y, tile_rows, tile_cols),
            precision=lax.Precision.HIGHEST,
        )
    return total


def convolve_back(padded_delta, weights, inputs):
    tile_rows = padded_delta.shape[1] - 2
    tile_cols = padded_delta.shape[2] - 2
    kernel = weights.reshape(weights.shape[0], inputs, 9)
    total = jnp.zeros((inputs, tile_rows, tile_cols), jnp.float32)
    for offset, (step_x, step_y) in enumerate(OFFSETS):
        total = total + jnp.einsum(
            "oi,oxy->ixy",
            kernel[:, :, offset],
            window(padded_delta, 1 - step_x, 1 - step_y, tile_rows, tile_cols),
            precision=lax.Precision.HIGHEST,
        )
    return total


def kernel_grad(delta, padded):
    tile_rows = delta.shape[1]
    tile_cols = delta.shape[2]
    pieces = [
        jnp.einsum(
            "oxy,ixy->oi",
            delta,
            window(padded, 1 + step_x, 1 + step_y, tile_rows, tile_cols),
            precision=lax.Precision.HIGHEST,
        )
        for step_x, step_y in OFFSETS
    ]
    return jnp.stack(pieces, 2).reshape(delta.shape[0], -1)


def body(tracers, cotangent, winds, levels, conv1, bias1, conv2, bias2, head):
    tr_count, tile_rows, tile_cols = tracers.shape
    wind_ext = extend(winds)
    first = jnp.tanh(convolve_local(wind_ext, conv1, bias1))
    first_ext = extend(first)
    second = jnp.tanh(convolve_local(first_ext, conv2, bias2))
    coefs, pullback = jax.vjp(coef_cells, winds, second, head)
    coef_ext = extend(coefs.reshape(9 * LEVELS, tile_rows, tile_cols))
    coef_ext = coef_ext.reshape(LEVELS, 9, tile_rows + 2, tile_cols + 2)
    select = (jnp.arange(LEVELS, dtype=jnp.int32)[:, None] == levels[None, :]).astype(jnp.float32)
    both_ext = extend_tracers(jnp.concatenate([tracers, cotangent], axis=0))
    tracer_ext = both_ext[:tr_count]
    cot_ext = both_ext[tr_count:]
    adjoint = cotangent.astype(jnp.float32)
    terms = []
    for step_x, step_y in OFFSETS:
        moved = window(tracer_ext, 1 + step_x, 1 + step_y, tile_rows, tile_cols).astype(jnp.float32)
        terms.append(
            jnp.einsum("lt,txy->lxy", select, adjoint * moved, precision=lax.Precision.HIGHEST)
        )
    local_terms = jnp.stack(terms, 1)
    coef_grad = lax.psum(local_terms, "tracer")
    tracer_sum = jnp.zeros((tr_count, tile_rows, tile_cols), jnp.float32)
    for offset, (step_x, step_y) in enumerate(OFFSETS):
        chosen = jnp.einsum(
            "lt,lxy->txy",
            select,
            window(coef_ext[:, offset], 1 - step_x, 1 - step_y, tile_rows, tile_cols),
            precision=lax.Precision.HIGHEST,
        )
        earlier = window(cot_ext, 1 - step_x, 1 - step_y, tile_rows, tile_cols).astype(jnp.float32)
        tracer_sum = tracer_sum + chosen * earlier
    tracer_grad = tracer_sum.astype(jnp.bfloat16)
    wind_direct, hidden_grad, head_grad = pullback(coef_grad)
    second_delta = hidden_grad * (1.0 - second * second)
    conv2_grad = kernel_grad(second_delta, first_ext)
    bias2_grad = jnp.sum(second_delta, axis=(1, 2))
    second_ext = extend(second_delta)
    first_delta = convolve_back(second_ext, conv2, first.shape[0]) * (1.0 - first * first)
    conv1_grad = kernel_grad(first_delta, wind_ext)
    bias1_grad = jnp.sum(first_delta, axis=(1, 2))
    first_ext_delta = extend(first_delta)
    wind_grad = wind_direct + convolve_back(first_ext_delta, conv1, winds.shape[0])
    conv1_grad, bias1_grad, conv2_grad, bias2_grad, head_grad = lax.psum(
        (conv1_grad, bias1_grad, conv2_grad, bias2_grad, head_grad), ("gx", "gy")
    )
    return (tracer_grad, wind_grad, conv1_grad, bias1_grad, conv2_grad, bias2_grad, head_grad)


def solution(mesh):
    return jax.shard_map(
        body,
        mesh=mesh,
        in_specs=(
            P(("member", "tracer"), "gx", "gy"),
            P(("member", "tracer"), "gx", "gy"),
            P("member", "gx", "gy"),
            P(("member", "tracer")),
            P(),
            P(),
            P(),
            P(),
            P(),
        ),
        out_specs=(
            P(("member", "tracer"), "gx", "gy"),
            P("member", "gx", "gy"),
            P("member", None),
            P("member"),
            P("member", None),
            P("member"),
            P("member", None),
        ),
        check_vma=False,
    )
```

profile of v0, /device:TPU:0, one launch (start us, length us, event | category | flops | bytes accessed | tf_op | source)
XLA Modules:
  0.0 188.6 jit_solution(15959918718714191005)
XLA Ops:
  7.2 0.8 fusion.255
  8.1 3.1 %collective-permute-start = (f32[4,1,256]{2,0,1:T(4,128)S(1)}, f32[4,1,256]{2,0,1:T(4,128)S(1)}, u32[]{:S(2)}, u32[]{:S(2)}) collective-permute-start(f32[4,1,256]{2,0,1:T(4,128)S(1)} %copy.347), channel_id=1, source_target_pairs={{0,4},{4,8},{8,12},{12,0},{1,5},{5,9},{9,13},{13,1},{2,6},{6,10},{... | collective-permute-start | bytes 12296 | tf_op jit(solution)/shard_map/ppermute | solution.py:21
  11.2 2.1 %collective-permute-start.1 = (f32[4,1,256]{2,0,1:T(4,128)S(1)}, f32[4,1,256]{2,0,1:T(4,128)S(1)}, u32[]{:S(2)}, u32[]{:S(2)}) collective-permute-start(f32[4,1,256]{2,0,1:T(4,128)S(1)} %copy.348), channel_id=1, source_target_pairs={{4,0},{8,4},{12,8},{0,12},{5,1},{9,5},{13,9},{1,13},{6,2},{10,6},{... | collective-permute-start | bytes 12296 | tf_op jit(solution)/shard_map/ppermute | solution.py:22
  13.3 0.9 copy_dynamic-update-slice_fusion
  14.3 3.8 %collective-permute-start.13 = (bf16[64,1,256]{2,0,1:T(8,128)(2,1)S(1)}, bf16[64,1,256]{2,0,1:T(8,128)(2,1)S(1)}, u32[]{:S(2)}, u32[]{:S(2)}) collective-permute-start(bf16[64,1,256]{2,0,1:T(8,128)(2,1)S(1)} %get-tuple-element.72), channel_id=1, source_target_pairs={{4,0},{8,4},{12,8},{0,12},{5,1},{9,5},{13,9},{1,13},{6,2},{10,6},{... | collective-permute-start | bytes 98312 | tf_op jit(solution)/shard_map/ppermute | solution.py:22
  18.8 0.8 copy-done.40
  19.7 0.7 fusion.249
  20.5 0.7 pad_maximum_fusion.14
  21.3 3.5 %collective-permute-start.2 = (f32[4,10,1]{2,0,1:T(4,128)S(1)}, f32[4,10,1]{2,0,1:T(4,128)S(1)}, u32[]{:S(2)}, u32[]{:S(2)}) collective-permute-start(f32[4,10,1]{2,0,1:T(4,128)S(1)} %get-tuple-element.89), channel_id=1, source_target_pairs={{0,2},{1,3},{4,6},{5,7},{8,10},{9,11},{12,14},{13,15},{16,18},{17,... | collective-permute-start | bytes 488 | tf_op jit(solution)/shard_map/ppermute | solution.py:21
  24.8 1.3 collective-permute-start.3
  27.0 3.5 %collective-permute-done.3 = f32[4,10,1]{2,0,1:T(4,128)S(1)} collective-permute-done((f32[4,10,1]{2,0,1:T(4,128)S(1)}, f32[4,10,1]{2,0,1:T(4,128)S(1)}, u32[]{:S(2)}, u32[]{:S(2)}) %collective-permute-start.3) | collective-permute-done | bytes 192 | tf_op jit(solution)/shard_map/ppermute | solution.py:22
  31.4 0.6 copy-done.62
  33.9 0.5 fusion.18
  34.4 3.8 %collective-permute-start.5 = (f32[32,1,256]{2,0,1:T(8,128)S(1)}, f32[32,1,256]{2,0,1:T(8,128)S(1)}, u32[]{:S(2)}, u32[]{:S(2)}) collective-permute-start(f32[32,1,256]{2,0,1:T(8,128)S(1)} %get-tuple-element.83), channel_id=1, source_target_pairs={{4,0},{8,4},{12,8},{0,12},{5,1},{9,5},{13,9},{1,13},{6,2},{10,6},{... | collective-permute-start | bytes 98312 | tf_op jit(solution)/shard_map/ppermute | solution.py:22
  38.4 1.3 collective-permute-start.14
  39.7 4.6 %collective-permute-start.15 = (bf16[64,10,1]{2,0,1:T(8,128)(2,1)S(1)}, bf16[64,10,1]{2,0,1:T(8,128)(2,1)S(1)}, u32[]{:S(2)}, u32[]{:S(2)}) collective-permute-start(bf16[64,10,1]{2,0,1:T(8,128)(2,1)S(1)} %get-tuple-element.62), channel_id=1, source_target_pairs={{0,2},{1,3},{4,6},{5,7},{8,10},{9,11},{12,14},{13,15},{16,18},{17,... | collective-permute-start | bytes 3848 | tf_op jit(solution)/shard_map/ppermute | solution.py:21
  44.7 0.9 collective-permute-done.14
  45.6 1.5 collective-permute-done.15
  47.4 0.6 copy-done.39
  49.1 0.6 copy-done.37
  51.1 0.7 copy-done.35
  52.0 4.4 %collective-permute-start.6 = (f32[32,10,1]{2,0,1:T(8,128)S(1)}, f32[32,10,1]{2,0,1:T(8,128)S(1)}, u32[]{:S(2)}, u32[]{:S(2)}) collective-permute-start(f32[32,10,1]{2,0,1:T(8,128)S(1)} %get-tuple-element.65), channel_id=1, source_target_pairs={{0,2},{1,3},{4,6},{5,7},{8,10},{9,11},{12,14},{13,15},{16,18},{17,... | collective-permute-start | bytes 3848 | tf_op jit(solution)/shard_map/ppermute | solution.py:21
  56.4 1.3 collective-permute-start.7
  58.5 0.7 collective-permute-done.6
  59.2 4.4 %collective-permute-done.7 = f32[32,10,1]{2,0,1:T(8,128)S(1)} collective-permute-done((f32[32,10,1]{2,0,1:T(8,128)S(1)}, f32[32,10,1]{2,0,1:T(8,128)S(1)}, u32[]{:S(2)}, u32[]{:S(2)}) %collective-permute-start.7) | collective-permute-done | bytes 1312 | tf_op jit(solution)/shard_map/ppermute | solution.py:22
  63.8 0.5 copy-done.27
  65.2 0.5 fusion.105
  65.7 0.5 fusion.116
  66.2 0.6 copy-done.63
  67.3 0.5 fusion.23
  68.3 0.6 broadcast_multiply_fusion.2
  69.1 1.1 multiply_reduce_fusion.2
  70.3 1.0 convolution_bitcast_fusion.15
  71.3 1.1 fusion.257
  72.3 0.6 fusion.247
  74.0 1.8 collective-permute-start.16
  75.8 2.1 %collective-permute-start.17 = (f32[32,1,256]{2,0,1:T(8,128)}, f32[32,1,256]{2,0,1:T(8,128)}, u32[]{:S(2)}, u32[]{:S(2)}) collective-permute-start(f32[32,1,256]{2,0,1:T(8,128)} %get-tuple-element.70), channel_id=1, source_target_pairs={{4,0},{8,4},{12,8},{0,12},{5,1},{9,5},{13,9},{1,13},{6,2},{10,6},{... | collective-permute-start | bytes 98312 | tf_op jit(solution)/shard_map/ppermute | solution.py:22
  82.7 3.8 %collective-permute-start.9 = (f32[18,1,256]{2,0,1:T(8,128)S(1)}, f32[18,1,256]{2,0,1:T(8,128)S(1)}, u32[]{:S(2)}, u32[]{:S(2)}) collective-permute-start(f32[18,1,256]{2,0,1:T(8,128)S(1)} %get-tuple-element.87), channel_id=1, source_target_pairs={{4,0},{8,4},{12,8},{0,12},{5,1},{9,5},{13,9},{1,13},{6,2},{10,6},{... | collective-permute-start | bytes 55304 | tf_op jit(solution)/shard_map/ppermute | solution.py:22
  86.6 1.8 collective-permute-done.8
  88.5 3.6 %collective-permute-start.10 = (f32[18,10,1]{2,0,1:T(8,128)S(1)}, f32[18,10,1]{2,0,1:T(8,128)S(1)}, u32[]{:S(2)}, u32[]{:S(2)}) collective-permute-start(f32[18,10,1]{2,0,1:T(8,128)S(1)} %get-tuple-element.84), channel_id=1, source_target_pairs={{0,2},{1,3},{4,6},{5,7},{8,10},{9,11},{12,14},{13,15},{16,18},{17,... | collective-permute-start | bytes 2168 | tf_op jit(solution)/shard_map/ppermute | solution.py:21
  92.1 1.3 collective-permute-start.11
  93.4 0.6 add_multiply_fusion
  94.2 0.7 reshape.81
  94.9 4.0 %collective-permute-done.11 = f32[18,10,1]{2,0,1:T(8,128)S(1)} collective-permute-done((f32[18,10,1]{2,0,1:T(8,128)S(1)}, f32[18,10,1]{2,0,1:T(8,128)S(1)}, u32[]{:S(2)}, u32[]{:S(2)}) %collective-permute-start.11) | collective-permute-done | bytes 752 | tf_op jit(solution)/shard_map/ppermute | solution.py:22
  102.4 0.6 add_convert_fusion
  103.0 0.7 copy.231
  103.7 0.8 pad_maximum_fusion.7
  104.6 1.3 collective-permute-start.18
  105.9 4.6 %collective-permute-start.19 = (f32[32,10,1]{2,0,1:T(8,128)S(1)}, f32[32,10,1]{2,0,1:T(8,128)S(1)}, u32[]{:S(2)}, u32[]{:S(2)}) collective-permute-start(f32[32,10,1]{2,0,1:T(8,128)S(1)} %get-tuple-element.58), channel_id=1, source_target_pairs={{0,2},{1,3},{4,6},{5,7},{8,10},{9,11},{12,14},{13,15},{16,18},{17,... | collective-permute-start | bytes 3848 | tf_op jit(solution)/shard_map/ppermute | solution.py:21
  110.5 1.1 fusion.53
  111.7 1.1 fusion.57
  112.8 0.5 collective-permute-done.19
  113.3 1.0 pad_maximum_fusion.2
  117.2 0.5 fusion.24
  117.8 0.5 fusion.256
  122.4 3.9 %collective-permute-start.21 = (f32[32,1,256]{2,0,1:T(8,128)S(1)}, f32[32,1,256]{2,0,1:T(8,128)S(1)}, u32[]{:S(2)}, u32[]{:S(2)}) collective-permute-start(f32[32,1,256]{2,0,1:T(8,128)S(1)} %get-tuple-element.68), channel_id=1, source_target_pairs={{4,0},{8,4},{12,8},{0,12},{5,1},{9,5},{13,9},{1,13},{6,2},{10,6},{... | collective-permute-start | bytes 98312 | tf_op jit(solution)/shard_map/ppermute | solution.py:22
  127.4 39.4 %all-reduce.2 = (f32[32,36]{0,1:T(8,128)S(1)}, f32[32]{0:T(128)}, f32[32,288]{0,1:T(8,128)S(1)}, f32[32]{0:T(128)}, f32[18,32]{1,0:T(8,128)}) all-reduce(f32[32,36]{0,1:T(8,128)S(1)} %reshape.80, f32[32]{0:T(128)S(1)} %get-tuple-element.117, ...), channel_id=1, replica_groups=mesh['member'=2,'gx'=4,'gy'=2,'tracer'=2] {'gx','gy'}, use_global_device_ids=true, to_apply=%region_5.0 | all-reduce | flops 11008 | bytes 88064 | tf_op jit(solution)/shard_map/psum | solution.py:150
  166.8 0.7 copy.233
  167.4 0.7 copy.234
  168.3 1.3 collective-permute-start.22
  169.6 4.6 %collective-permute-start.23 = (f32[32,10,1]{2,0,1:T(8,128)S(1)}, f32[32,10,1]{2,0,1:T(8,128)S(1)}, u32[]{:S(2)}, u32[]{:S(2)}) collective-permute-start(f32[32,10,1]{2,0,1:T(8,128)S(1)} %get-tuple-element.54), channel_id=1, source_target_pairs={{0,2},{1,3},{4,6},{5,7},{8,10},{9,11},{12,14},{13,15},{16,18},{17,... | collective-permute-start | bytes 3848 | tf_op jit(solution)/shard_map/ppermute | solution.py:21
  174.7 0.8 collective-permute-done.22
  175.5 1.5 collective-permute-done.23
  181.1 0.6 copy.232
  (261 shorter events, 32.8 us)
Async XLA Ops:
  7.2 60.7 %copy-start = (f32[18,32]{1,0:T(8,128)S(1)}, f32[18,32]{1,0:T(8,128)}, u32[]{:S(2)}) copy-start(f32[18,32]{1,0:T(8,128)} %param.17) | copy-start | bytes 6916
  7.2 61.9 %all-reduce.5.cloned.1.call-start = ((), (), s32[]{:S(2)}) async-start(), calls=%async_computation | async-start | bytes 294912 | tf_op jit(solution)/shard_map/psum | solution.py:128
  8.1 13.0 %collective-permute-start = (f32[4,1,256]{2,0,1:T(4,128)S(1)}, f32[4,1,256]{2,0,1:T(4,128)S(1)}, u32[]{:S(2)}, u32[]{:S(2)}) collective-permute-start(f32[4,1,256]{2,0,1:T(4,128)S(1)} %copy.347), channel_id=1, source_target_pairs={{0,4},{4,8},{8,12},{12,0},{1,5},{5,9},{9,13},{13,1},{2,6},{6,10},{... | collective-permute-start | bytes 12296 | tf_op jit(solution)/shard_map/ppermute | solution.py:21
  11.2 3.0 %copy-start.1 = (bf16[32,8,256]{2,1,0:T(8,128)(2,1)S(1)}, bf16[32,8,256]{2,1,0:T(8,128)(2,1)}, u32[]{:S(2)}) copy-start(bf16[32,8,256]{2,1,0:T(8,128)(2,1)} %param.10) | copy-start | bytes 393220
  11.2 10.0 %collective-permute-start.1 = (f32[4,1,256]{2,0,1:T(4,128)S(1)}, f32[4,1,256]{2,0,1:T(4,128)S(1)}, u32[]{:S(2)}, u32[]{:S(2)}) collective-permute-start(f32[4,1,256]{2,0,1:T(4,128)S(1)} %copy.348), channel_id=1, source_target_pairs={{4,0},{8,4},{12,8},{0,12},{5,1},{9,5},{13,9},{1,13},{6,2},{10,6},{... | collective-permute-start | bytes 12296 | tf_op jit(solution)/shard_map/ppermute | solution.py:22
  14.2 3.9 %copy-start.3 = (f32[4,8,256]{2,1,0:T(8,128)S(1)}, f32[4,8,256]{2,1,0:T(8,128)}, u32[]{:S(2)}) copy-start(f32[4,8,256]{2,1,0:T(8,128)} %param.11) | copy-start | bytes 98308
  14.3 24.0 %collective-permute-start.12 = (bf16[64,1,256]{2,0,1:T(8,128)(2,1)S(1)}, bf16[64,1,256]{2,0,1:T(8,128)(2,1)S(1)}, u32[]{:S(2)}, u32[]{:S(2)}) collective-permute-start(bf16[64,1,256]{2,0,1:T(8,128)(2,1)S(1)} %get-tuple-element.71), channel_id=1, source_target_pairs={{0,4},{4,8},{8,12},{12,0},{1,5},{5,9},{9,13},{13,1},{2,6},{6,10},{... | collective-permute-start | bytes 98312 | tf_op jit(solution)/shard_map/ppermute | solution.py:21
  14.3 3.8 %copy-start.60 = (f32[32,36]{1,0:T(8,128)S(1)}, f32[32,36]{1,0:T(8,128)}, u32[]{:S(2)}) copy-start(f32[32,36]{1,0:T(8,128)} %param.13) | copy-start | bytes 13828
  14.3 23.9 %collective-permute-start.13 = (bf16[64,1,256]{2,0,1:T(8,128)(2,1)S(1)}, bf16[64,1,256]{2,0,1:T(8,128)(2,1)S(1)}, u32[]{:S(2)}, u32[]{:S(2)}) collective-permute-start(bf16[64,1,256]{2,0,1:T(8,128)(2,1)S(1)} %get-tuple-element.72), channel_id=1, source_target_pairs={{4,0},{8,4},{12,8},{0,12},{5,1},{9,5},{13,9},{1,13},{6,2},{10,6},{... | collective-permute-start | bytes 98312 | tf_op jit(solution)/shard_map/ppermute | solution.py:22
  18.3 7.8 %copy-start.56 = (f32[32,4,1]{0,2,1:T(1,128)}, f32[32,4,1]{0,2,1:T(1,128)S(1)}, u32[]{:S(2)}) copy-start(f32[32,4,1]{0,2,1:T(1,128)S(1)} %get-tuple-element.95) | copy-start | bytes 1540
  18.3 8.2 %copy-start.54 = (f32[32,4,1]{0,2,1:T(1,128)}, f32[32,4,1]{0,2,1:T(1,128)S(1)}, u32[]{:S(2)}) copy-start(f32[32,4,1]{0,2,1:T(1,128)S(1)} %get-tuple-element.100) | copy-start | bytes 1540
  18.3 12.2 %copy-start.46 = (f32[32,4,1]{0,2,1:T(1,128)}, f32[32,4,1]{0,2,1:T(1,128)S(1)}, u32[]{:S(2)}) copy-start(f32[32,4,1]{0,2,1:T(1,128)S(1)} %get-tuple-element.99) | copy-start | bytes 1540
  18.3 12.6 %copy-start.50 = (f32[32,4,1]{0,2,1:T(1,128)}, f32[32,4,1]{0,2,1:T(1,128)S(1)}, u32[]{:S(2)}) copy-start(f32[32,4,1]{0,2,1:T(1,128)S(1)} %get-tuple-element.98) | copy-start | bytes 1540
  18.3 13.1 %copy-start.44 = (f32[32,4,1]{0,2,1:T(1,128)}, f32[32,4,1]{0,2,1:T(1,128)S(1)}, u32[]{:S(2)}) copy-start(f32[32,4,1]{0,2,1:T(1,128)S(1)} %get-tuple-element.101) | copy-start | bytes 1540
  18.3 14.2 %copy-start.58 = (f32[32,4,1]{0,2,1:T(1,128)}, f32[32,4,1]{0,2,1:T(1,128)S(1)}, u32[]{:S(2)}) copy-start(f32[32,4,1]{0,2,1:T(1,128)S(1)} %get-tuple-element.97) | copy-start | bytes 1540
  18.3 14.6 %copy-start.48 = (f32[32,4,1]{0,2,1:T(1,128)}, f32[32,4,1]{0,2,1:T(1,128)S(1)}, u32[]{:S(2)}) copy-start(f32[32,4,1]{0,2,1:T(1,128)S(1)} %get-tuple-element.94) | copy-start | bytes 1540
  18.4 15.1 %copy-start.52 = (f32[32,4,1]{0,2,1:T(1,128)}, f32[32,4,1]{0,2,1:T(1,128)S(1)}, u32[]{:S(2)}) copy-start(f32[32,4,1]{0,2,1:T(1,128)S(1)} %get-tuple-element.96) | copy-start | bytes 1540
  18.4 15.5 %copy-start.42 = (f32[32,4,1]{0,2,1:T(1,128)}, f32[32,4,1]{0,2,1:T(1,128)S(1)}, u32[]{:S(2)}) copy-start(f32[32,4,1]{0,2,1:T(1,128)S(1)} %get-tuple-element.93) | copy-start | bytes 1540
  20.4 23.9 %copy-start.33 = (f32[32,32,1]{0,2,1:T(1,128)}, f32[32,32,1]{0,2,1:T(1,128)S(1)}, u32[]{:S(2)}) copy-start(f32[32,32,1]{0,2,1:T(1,128)S(1)} %get-tuple-element.76) | copy-start | bytes 12292
  20.4 37.2 %copy-start.29 = (f32[32,32,1]{0,2,1:T(1,128)}, f32[32,32,1]{0,2,1:T(1,128)S(1)}, u32[]{:S(2)}) copy-start(f32[32,32,1]{0,2,1:T(1,128)S(1)} %get-tuple-element.74) | copy-start | bytes 12292
  20.4 37.7 %copy-start.31 = (f32[32,32,1]{0,2,1:T(1,128)}, f32[32,32,1]{0,2,1:T(1,128)S(1)}, u32[]{:S(2)}) copy-start(f32[32,32,1]{0,2,1:T(1,128)S(1)} %get-tuple-element.79) | copy-start | bytes 12292
  20.4 44.3 %copy-start.25 = (f32[32,32,1]{0,2,1:T(1,128)}, f32[32,32,1]{0,2,1:T(1,128)S(1)}, u32[]{:S(2)}) copy-start(f32[32,32,1]{0,2,1:T(1,128)S(1)} %get-tuple-element.77) | copy-start | bytes 12292
  20.4 44.7 %copy-start.23 = (f32[32,32,1]{0,2,1:T(1,128)}, f32[32,32,1]{0,2,1:T(1,128)S(1)}, u32[]{:S(2)}) copy-start(f32[32,32,1]{0,2,1:T(1,128)S(1)} %get-tuple-element.81) | copy-start | bytes 12292
  20.4 45.2 %copy-start.21 = (f32[32,32,1]{0,2,1:T(1,128)}, f32[32,32,1]{0,2,1:T(1,128)S(1)}, u32[]{:S(2)}) copy-start(f32[32,32,1]{0,2,1:T(1,128)S(1)} %get-tuple-element.78) | copy-start | bytes 12292
  20.4 45.7 %copy-start.17 = (f32[32,32,1]{0,2,1:T(1,128)}, f32[32,32,1]{0,2,1:T(1,128)S(1)}, u32[]{:S(2)}) copy-start(f32[32,32,1]{0,2,1:T(1,128)S(1)} %get-tuple-element.80) | copy-start | bytes 12292
  21.1 5.4 %copy-start.19 = (f32[4,9,256]{2,0,1:T(4,128)}, f32[4,9,256]{2,0,1:T(4,128)S(1)}, u32[]{:S(2)}) copy-start(f32[4,9,256]{2,0,1:T(4,128)S(1)} %get-tuple-element.102) | copy-start | bytes 110596
  21.2 4.9 %copy-start.11 = (f32[4,9,256]{2,0,1:T(4,128)}, f32[4,9,256]{2,0,1:T(4,128)S(1)}, u32[]{:S(2)}) copy-start(f32[4,9,256]{2,0,1:T(4,128)S(1)} %get-tuple-element.115) | copy-start | bytes 110596
  21.3 9.7 %collective-permute-start.2 = (f32[4,10,1]{2,0,1:T(4,128)S(1)}, f32[4,10,1]{2,0,1:T(4,128)S(1)}, u32[]{:S(2)}, u32[]{:S(2)}) collective-permute-start(f32[4,10,1]{2,0,1:T(4,128)S(1)} %get-tuple-element.89), channel_id=1, source_target_pairs={{0,2},{1,3},{4,6},{5,7},{8,10},{9,11},{12,14},{13,15},{16,18},{17,... | collective-permute-start | bytes 488 | tf_op jit(solution)/shard_map/ppermute | solution.py:21
  24.8 5.7 %collective-permute-start.3 = (f32[4,10,1]{2,0,1:T(4,128)S(1)}, f32[4,10,1]{2,0,1:T(4,128)S(1)}, u32[]{:S(2)}, u32[]{:S(2)}) collective-permute-start(f32[4,10,1]{2,0,1:T(4,128)S(1)} %get-tuple-element.90), channel_id=1, source_target_pairs={{2,0},{3,1},{6,4},{7,5},{10,8},{11,9},{14,12},{15,13},{18,16},{19,... | collective-permute-start | bytes 488 | tf_op jit(solution)/shard_map/ppermute | solution.py:22
  34.4 17.4 %collective-permute-start.4 = (f32[32,1,256]{2,0,1:T(8,128)S(1)}, f32[32,1,256]{2,0,1:T(8,128)S(1)}, u32[]{:S(2)}, u32[]{:S(2)}) collective-permute-start(f32[32,1,256]{2,0,1:T(8,128)S(1)} %get-tuple-element.82), channel_id=1, source_target_pairs={{0,4},{4,8},{8,12},{12,0},{1,5},{5,9},{9,13},{13,1},{2,6},{6,10},{... | collective-permute-start | bytes 98312 | tf_op jit(solution)/shard_map/ppermute | solution.py:21
  34.4 17.4 %collective-permute-start.5 = (f32[32,1,256]{2,0,1:T(8,128)S(1)}, f32[32,1,256]{2,0,1:T(8,128)S(1)}, u32[]{:S(2)}, u32[]{:S(2)}) collective-permute-start(f32[32,1,256]{2,0,1:T(8,128)S(1)} %get-tuple-element.83), channel_id=1, source_target_pairs={{4,0},{8,4},{12,8},{0,12},{5,1},{9,5},{13,9},{1,13},{6,2},{10,6},{... | collective-permute-start | bytes 98312 | tf_op jit(solution)/shard_map/ppermute | solution.py:22
  38.4 7.2 %collective-permute-start.14 = (bf16[64,10,1]{2,0,1:T(8,128)(2,1)S(1)}, bf16[64,10,1]{2,0,1:T(8,128)(2,1)S(1)}, u32[]{:S(2)}, u32[]{:S(2)}) collective-permute-start(bf16[64,10,1]{2,0,1:T(8,128)(2,1)S(1)} %get-tuple-element.61), channel_id=1, source_target_pairs={{2,0},{3,1},{6,4},{7,5},{10,8},{11,9},{14,12},{15,13},{18,16},{19,... | collective-permute-start | bytes 3848 | tf_op jit(solution)/shard_map/ppermute | solution.py:22
  39.7 7.4 %collective-permute-start.15 = (bf16[64,10,1]{2,0,1:T(8,128)(2,1)S(1)}, bf16[64,10,1]{2,0,1:T(8,128)(2,1)S(1)}, u32[]{:S(2)}, u32[]{:S(2)}) collective-permute-start(bf16[64,10,1]{2,0,1:T(8,128)(2,1)S(1)} %get-tuple-element.62), channel_id=1, source_target_pairs={{0,2},{1,3},{4,6},{5,7},{8,10},{9,11},{12,14},{13,15},{16,18},{17,... | collective-permute-start | bytes 3848 | tf_op jit(solution)/shard_map/ppermute | solution.py:21
  48.8 0.9 copy-start.37
  51.8 11.8 %copy-start.7 = (f32[32,1,256]{2,0,1:T(8,128)}, f32[32,1,256]{2,0,1:T(8,128)S(1)}, u32[]{:S(2)}) copy-start(f32[32,1,256]{2,0,1:T(8,128)S(1)} %collective-permute-done.4) | copy-start | bytes 98308
  51.8 11.8 %copy-start.5 = (f32[32,1,256]{2,0,1:T(8,128)}, f32[32,1,256]{2,0,1:T(8,128)S(1)}, u32[]{:S(2)}) copy-start(f32[32,1,256]{2,0,1:T(8,128)S(1)} %collective-permute-done.5) | copy-start | bytes 98308
  52.0 7.2 %collective-permute-start.6 = (f32[32,10,1]{2,0,1:T(8,128)S(1)}, f32[32,10,1]{2,0,1:T(8,128)S(1)}, u32[]{:S(2)}, u32[]{:S(2)}) collective-permute-start(f32[32,10,1]{2,0,1:T(8,128)S(1)} %get-tuple-element.65), channel_id=1, source_target_pairs={{0,2},{1,3},{4,6},{5,7},{8,10},{9,11},{12,14},{13,15},{16,18},{17,... | collective-permute-start | bytes 3848 | tf_op jit(solution)/shard_map/ppermute | solution.py:21
  56.4 7.2 %collective-permute-start.7 = (f32[32,10,1]{2,0,1:T(8,128)S(1)}, f32[32,10,1]{2,0,1:T(8,128)S(1)}, u32[]{:S(2)}, u32[]{:S(2)}) collective-permute-start(f32[32,10,1]{2,0,1:T(8,128)S(1)} %get-tuple-element.66), channel_id=1, source_target_pairs={{2,0},{3,1},{6,4},{7,5},{10,8},{11,9},{14,12},{15,13},{18,16},{19,... | collective-permute-start | bytes 3848 | tf_op jit(solution)/shard_map/ppermute | solution.py:22
  69.1 1.1 copy-start.2
  73.7 4.2 %copy-start.8 = (f32[32,1,256]{2,0,1:T(8,128)S(1)}, f32[32,1,256]{2,0,1:T(8,128)}, u32[]{:S(2)}) copy-start(f32[32,1,256]{2,0,1:T(8,128)} %copy-done.7) | copy-start | bytes 98308
  74.0 29.7 %collective-permute-start.16 = (f32[32,1,256]{2,0,1:T(8,128)}, f32[32,1,256]{2,0,1:T(8,128)}, u32[]{:S(2)}, u32[]{:S(2)}) collective-permute-start(f32[32,1,256]{2,0,1:T(8,128)} %get-tuple-element.69), channel_id=1, source_target_pairs={{0,4},{4,8},{8,12},{12,0},{1,5},{5,9},{9,13},{13,1},{2,6},{6,10},{... | collective-permute-start | bytes 98312 | tf_op jit(solution)/shard_map/ppermute | solution.py:21
  75.8 27.9 %collective-permute-start.17 = (f32[32,1,256]{2,0,1:T(8,128)}, f32[32,1,256]{2,0,1:T(8,128)}, u32[]{:S(2)}, u32[]{:S(2)}) collective-permute-start(f32[32,1,256]{2,0,1:T(8,128)} %get-tuple-element.70), channel_id=1, source_target_pairs={{4,0},{8,4},{12,8},{0,12},{5,1},{9,5},{13,9},{1,13},{6,2},{10,6},{... | collective-permute-start | bytes 98312 | tf_op jit(solution)/shard_map/ppermute | solution.py:22
  81.0 0.8 copy-start.14
  82.6 3.9 %copy-start.10 = (f32[4,8,256]{2,1,0:T(8,128)S(1)}, f32[4,8,256]{2,1,0:T(8,128)}, u32[]{:S(2)}) copy-start(f32[4,8,256]{2,1,0:T(8,128)} %copy-done.9) | copy-start | bytes 98308
  82.7 5.7 %collective-permute-start.8 = (f32[18,1,256]{2,0,1:T(8,128)S(1)}, f32[18,1,256]{2,0,1:T(8,128)S(1)}, u32[]{:S(2)}, u32[]{:S(2)}) collective-permute-start(f32[18,1,256]{2,0,1:T(8,128)S(1)} %get-tuple-element.86), channel_id=1, source_target_pairs={{0,4},{4,8},{8,12},{12,0},{1,5},{5,9},{9,13},{13,1},{2,6},{6,10},{... | collective-permute-start | bytes 55304 | tf_op jit(solution)/shard_map/ppermute | solution.py:21
  82.7 5.6 %collective-permute-start.9 = (f32[18,1,256]{2,0,1:T(8,128)S(1)}, f32[18,1,256]{2,0,1:T(8,128)S(1)}, u32[]{:S(2)}, u32[]{:S(2)}) collective-permute-start(f32[18,1,256]{2,0,1:T(8,128)S(1)} %get-tuple-element.87), channel_id=1, source_target_pairs={{4,0},{8,4},{12,8},{0,12},{5,1},{9,5},{13,9},{1,13},{6,2},{10,6},{... | collective-permute-start | bytes 55304 | tf_op jit(solution)/shard_map/ppermute | solution.py:22
  88.4 5.7 %copy-start.16 = (f32[32,32,9]{1,0,2:T(8,128)S(1)}, f32[32,32,9]{1,0,2:T(8,128)}, u32[]{:S(2)}) copy-start(f32[32,32,9]{1,0,2:T(8,128)} %copy-done.15) | copy-start | bytes 110596
  88.5 6.4 %collective-permute-start.10 = (f32[18,10,1]{2,0,1:T(8,128)S(1)}, f32[18,10,1]{2,0,1:T(8,128)S(1)}, u32[]{:S(2)}, u32[]{:S(2)}) collective-permute-start(f32[18,10,1]{2,0,1:T(8,128)S(1)} %get-tuple-element.84), channel_id=1, source_target_pairs={{0,2},{1,3},{4,6},{5,7},{8,10},{9,11},{12,14},{13,15},{16,18},{17,... | collective-permute-start | bytes 2168 | tf_op jit(solution)/shard_map/ppermute | solution.py:21
  92.1 6.8 %collective-permute-start.11 = (f32[18,10,1]{2,0,1:T(8,128)S(1)}, f32[18,10,1]{2,0,1:T(8,128)S(1)}, u32[]{:S(2)}, u32[]{:S(2)}) collective-permute-start(f32[18,10,1]{2,0,1:T(8,128)S(1)} %get-tuple-element.85), channel_id=1, source_target_pairs={{2,0},{3,1},{6,4},{7,5},{10,8},{11,9},{14,12},{15,13},{18,16},{19,... | collective-permute-start | bytes 2168 | tf_op jit(solution)/shard_map/ppermute | solution.py:22
  104.5 6.0 %copy-start.32 = (f32[32,32,1]{0,2,1:T(1,128)S(1)}, f32[32,32,1]{0,2,1:T(1,128)}, u32[]{:S(2)}) copy-start(f32[32,32,1]{0,2,1:T(1,128)} %copy-done.31) | copy-start | bytes 12292
  104.6 8.2 %collective-permute-start.18 = (f32[32,10,1]{2,0,1:T(8,128)S(1)}, f32[32,10,1]{2,0,1:T(8,128)S(1)}, u32[]{:S(2)}, u32[]{:S(2)}) collective-permute-start(f32[32,10,1]{2,0,1:T(8,128)S(1)} %get-tuple-element.57), channel_id=1, source_target_pairs={{2,0},{3,1},{6,4},{7,5},{10,8},{11,9},{14,12},{15,13},{18,16},{19,... | collective-permute-start | bytes 3848 | tf_op jit(solution)/shard_map/ppermute | solution.py:22
  105.9 5.7 %copy-start.30 = (f32[32,32,1]{0,2,1:T(1,128)S(1)}, f32[32,32,1]{0,2,1:T(1,128)}, u32[]{:S(2)}) copy-start(f32[32,32,1]{0,2,1:T(1,128)} %copy-done.29) | copy-start | bytes 12292
  105.9 7.4 %collective-permute-start.19 = (f32[32,10,1]{2,0,1:T(8,128)S(1)}, f32[32,10,1]{2,0,1:T(8,128)S(1)}, u32[]{:S(2)}, u32[]{:S(2)}) collective-permute-start(f32[32,10,1]{2,0,1:T(8,128)S(1)} %get-tuple-element.58), channel_id=1, source_target_pairs={{0,2},{1,3},{4,6},{5,7},{8,10},{9,11},{12,14},{13,15},{16,18},{17,... | collective-permute-start | bytes 3848 | tf_op jit(solution)/shard_map/ppermute | solution.py:21
  112.8 1.6 copy-start.28
  121.3 0.8 copy-start.12
  122.4 45.8 %collective-permute-start.20 = (f32[32,1,256]{2,0,1:T(8,128)S(1)}, f32[32,1,256]{2,0,1:T(8,128)S(1)}, u32[]{:S(2)}, u32[]{:S(2)}) collective-permute-start(f32[32,1,256]{2,0,1:T(8,128)S(1)} %get-tuple-element.67), channel_id=1, source_target_pairs={{0,4},{4,8},{8,12},{12,0},{1,5},{5,9},{9,13},{13,1},{2,6},{6,10},{... | collective-permute-start | bytes 98312 | tf_op jit(solution)/shard_map/ppermute | solution.py:21
  122.4 4.3 %copy-start.4 = (f32[32,288]{0,1:T(8,128)S(1)}, f32[32,288]{0,1:T(8,128)}, u32[]{:S(2)}) copy-start(f32[32,288]{0,1:T(8,128)} %reshape.81) | copy-start | bytes 110596
  122.4 45.8 %collective-permute-start.21 = (f32[32,1,256]{2,0,1:T(8,128)S(1)}, f32[32,1,256]{2,0,1:T(8,128)S(1)}, u32[]{:S(2)}, u32[]{:S(2)}) collective-permute-start(f32[32,1,256]{2,0,1:T(8,128)S(1)} %get-tuple-element.68), channel_id=1, source_target_pairs={{4,0},{8,4},{12,8},{0,12},{5,1},{9,5},{13,9},{1,13},{6,2},{10,6},{... | collective-permute-start | bytes 98312 | tf_op jit(solution)/shard_map/ppermute | solution.py:22
  168.3 5.9 %copy-start.57 = (f32[32,4,1]{0,2,1:T(1,128)S(1)}, f32[32,4,1]{0,2,1:T(1,128)}, u32[]{:S(2)}) copy-start(f32[32,4,1]{0,2,1:T(1,128)} %copy-done.56) | copy-start | bytes 1540
  168.3 7.2 %collective-permute-start.22 = (f32[32,10,1]{2,0,1:T(8,128)S(1)}, f32[32,10,1]{2,0,1:T(8,128)S(1)}, u32[]{:S(2)}, u32[]{:S(2)}) collective-permute-start(f32[32,10,1]{2,0,1:T(8,128)S(1)} %get-tuple-element.53), channel_id=1, source_target_pairs={{2,0},{3,1},{6,4},{7,5},{10,8},{11,9},{14,12},{15,13},{18,16},{19,... | collective-permute-start | bytes 3848 | tf_op jit(solution)/shard_map/ppermute | solution.py:22
  169.6 4.9 %copy-start.55 = (f32[32,4,1]{0,2,1:T(1,128)S(1)}, f32[32,4,1]{0,2,1:T(1,128)}, u32[]{:S(2)}) copy-start(f32[32,4,1]{0,2,1:T(1,128)} %copy-done.54) | copy-start | bytes 1540
  169.6 7.4 %collective-permute-start.23 = (f32[32,10,1]{2,0,1:T(8,128)S(1)}, f32[32,10,1]{2,0,1:T(8,128)S(1)}, u32[]{:S(2)}, u32[]{:S(2)}) collective-permute-start(f32[32,10,1]{2,0,1:T(8,128)S(1)} %get-tuple-element.54), channel_id=1, source_target_pairs={{0,2},{1,3},{4,6},{5,7},{8,10},{9,11},{12,14},{13,15},{16,18},{17,... | collective-permute-start | bytes 3848 | tf_op jit(solution)/shard_map/ppermute | solution.py:21
  177.7 1.0 copy-start.49
  179.4 1.0 copy-start.43
  (25 other events, 17.6 us)
Sparse Core Ops, SparseCore 0:
  51.9 17.1 all-reduce.4
where the time goes:
time: 190 us; the launch traced here: 189 us
  starting transfers between devices  57.6 us (30%)
  blocking collectives  39.4 us (21%)
  matrix products  30.2 us (16%)
  local copies, waits for them, and re-layouts  19.8 us (10%)
  waiting for transfers between devices  19.8 us (10%)
  between operations  15.8 us (8%)
  other arithmetic  5.99 us (3%)
    psum x1, blocking collectives, body(): lax.psum((conv1_grad, bias1_grad, conv2_grad, bias2_grad, head_grad), ('g...  39.4 us
    ppermute x12, starting transfers between devices, with_halo(): before = lax.ppermute(last, axis, up)  30.3 us
    ppermute x12, starting transfers between devices, with_halo(): after = lax.ppermute(first, axis, down)  27.3 us
    unnamed x147, local copies, waits for them, and re-layouts  15.9 us
    ppermute x12, waiting for transfers between devices, with_halo(): after = lax.ppermute(first, axis, down)  13.7 us
    dot_general x18, matrix products, convolve_local(): jnp.einsum('oi,ixy->oxy', kernel[:, :, offset], window(padded, 1 + step_x...  7.96 us
    dot_general x18, matrix products, convolve_back(): jnp.einsum('oi,oxy->ixy', kernel[:, :, offset], window(padded_delta, 1 -...  7.82 us
    dot_general x18, matrix products, kernel_grad(): jnp.einsum('oxy,ixy->oi', delta, window(padded, 1 + step_x, 1 + step_y, t...  6.24 us
  transfers between devices with their start and end apart: 25, of which 11 were waited for; matrix products, arithmetic and copies ran while one was open for 15% of the time, Pallas kernels for 0%

commit v1 on v0

v1 whole, which is shorter than its diff:
```python
import functools

import jax
import jax.numpy as jnp
from jax import lax
from jax.experimental import pallas as pl
from jax.experimental.pallas import tpu as pltpu
from jax.sharding import PartitionSpec as P

LEVELS = 2
CH = 32
COURANT = 0.5
CORRECTION = 0.2
STEPS = (-1, 0, 1)
HALO = 4
LANES = 128
F32 = jnp.float32
BF16 = jnp.bfloat16
NT = (((1,), (1,)), ((), ()))


def pieces(array, count):
    parts = []
    for _ in range(count):
        part = lax.reduce_precision(array, 8, 7)
        parts.append(part)
        array = array - part
    return parts


def halves(value):
    high = value.astype(BF16)
    return high, (value - high.astype(F32)).astype(BF16)


def dot3(weights, high, low):
    rows = weights.shape[0] // 2
    both = jnp.dot(weights, high, preferred_element_type=F32)
    rest = jnp.dot(weights[:rows], low, preferred_element_type=F32)
    return both[:rows] + both[rows:] + rest


def dot3_nt(a_high, a_low, b_high, b_low):
    out = lax.dot_general(a_high, b_high, NT, preferred_element_type=F32)
    out = out + lax.dot_general(a_high, b_low, NT, preferred_element_type=F32)
    return out + lax.dot_general(a_low, b_high, NT, preferred_element_type=F32)


def turn(value, step, axis):
    shift = (-step) % value.shape[axis]
    return pltpu.roll(value, shift, axis) if shift else value


def load_field(index, main_ref, below_ref, above_ref):
    strip = jnp.concatenate([below_ref[index].astype(F32), above_ref[index].astype(F32)], axis=0)
    return jnp.concatenate([main_ref[index].astype(F32), strip], axis=0)


def grad_kernel(levels_ref, main_ref, below_ref, above_ref, out_ref, moved_ref, cot_ref):
    count = levels_ref.shape[0]

    def fill(t, carry):
        field = load_field(t, main_ref, below_ref, above_ref)
        for b in range(3):
            moved_ref[b, t] = turn(field, STEPS[b], 1)
        cot_ref[t] = load_field(count + t, main_ref, below_ref, above_ref)
        return carry

    lax.fori_loop(0, count, fill, 0, unroll=4)
    for a in range(3):
        for b in range(3):

            def step(t, sums):
                product = cot_ref[t] * turn(moved_ref[b, t], STEPS[a], 0)
                upper = levels_ref[t].astype(F32)
                return sums[0] + product, sums[1] + upper * product

            zero = jnp.zeros(out_ref.shape[1:], F32)
            total, second = lax.fori_loop(0, count, step, (zero, zero), unroll=4)
            out_ref[3 * a + b] = total - second
            out_ref[9 + 3 * a + b] = second


def put_moved(high_ref, low_ref, row, value, sign):
    width = value.shape[1]
    for b in range(3):
        high, low = halves(turn(value, sign * STEPS[b], 1))
        high_ref[b * CH : (b + 1) * CH, row * width : (row + 1) * width] = high
        low_ref[b * CH : (b + 1) * CH, row * width : (row + 1) * width] = low


def put_winds(wind_ref, stack_ref, first_row, rows):
    width = wind_ref.shape[2]
    count = wind_ref.shape[0]
    for row in range(rows):
        value = wind_ref[:, first_row + row, :]
        for b in range(3):
            stack_ref[b * count : (b + 1) * count, row * width : (row + 1) * width] = turn(value, STEPS[b], 1)


def forward_kernel(wind_ref, inside_ref, w1_ref, b1_ref, w2_ref, b2_ref, head_ref, first_ref, second_ref, corr_ref, stack_ref, high_ref, low_ref):
    rows, width = wind_ref.shape[1:]
    stack_ref[...] = jnp.zeros(stack_ref.shape, F32)
    put_winds(wind_ref, stack_ref, 0, rows)
    bias1, bias2 = b1_ref[...], b2_ref[...]
    inside = jnp.concatenate([inside_ref[...]] * 2, axis=1)
    for row in range(0, rows - 2, 2):
        total = jnp.zeros((CH, 2 * width), F32) + bias1
        for a in range(3):
            high, low = halves(stack_ref[:, (row + a) * width : (row + a + 2) * width])
            total = total + dot3(w1_ref[a], high, low)
        value = jnp.tanh(total) * inside
        first_ref[:, row * width : (row + 2) * width] = value
        for part in range(2):
            put_moved(high_ref, low_ref, row + part, value[:, part * width : (part + 1) * width], 1)
    for row in range(0, rows - 4, 2):
        total = jnp.zeros((CH, 2 * width), F32) + bias2
        for a in range(3):
            where = slice((row + a) * width, (row + a + 2) * width)
            total = total + dot3(w2_ref[a], high_ref[:, where], low_ref[:, where])
        value = jnp.tanh(total)
        second_ref[:, row * width : (row + 2) * width] = value
        high, low = halves(value)
        corr = dot3(head_ref[...], high, low)
        for part in range(2):
            corr_ref[:, 2 + row + part, :] = corr[: corr_ref.shape[0], part * width : (part + 1) * width]


def backward_kernel(
    mine_ref, other_ref, wind_ref, inside_ref, first_ref, second_ref, headt_ref, w2b_ref, w1b_ref,
    wgrad_ref, par_ref,
    sum_ref, g_ref, d2_high, d2_low, own2_high, own2_low, act_high, act_low, d1_high, d1_low, own1_high, own1_low, wind_stack, net_ref,
):
    cells = g_ref.shape[1]
    width = wind_ref.shape[2]
    cols = wgrad_ref.shape[2]
    ring = cells // width
    tile = ring - 4
    sum_ref[...] = mine_ref[...] + other_ref[...]
    wrap = sum_ref.shape[1]
    nine = sum_ref.shape[0]
    g_ref[...] = jnp.zeros(g_ref.shape, F32)
    for row in range(ring):
        g_ref[:nine, row * width : (row + 1) * width] = sum_ref[:, (row - 2) % wrap, :]
    own = lax.broadcasted_iota(jnp.int32, (1, width), 1) < cols
    inside = inside_ref[...]
    for ref in (own2_high, own2_low, own1_high, own1_low):
        ref[...] = jnp.zeros(ref.shape, BF16)
    wind_stack[...] = jnp.zeros(wind_stack.shape, F32)
    put_winds(wind_ref, wind_stack, 3, tile + 2)
    wind_stack[12:13, :] = jnp.ones((1, wind_stack.shape[1]), F32)
    act_high[3 * CH :, :] = jnp.ones((act_high.shape[0] - 3 * CH, act_high.shape[1]), BF16)
    act_low[3 * CH :, :] = jnp.zeros((act_high.shape[0] - 3 * CH, act_high.shape[1]), BF16)

    def put_own(high_ref, low_ref, x, value):
        high, low = halves(jnp.where(own, value, 0.0))
        for a in range(3):
            high_ref[a * CH : (a + 1) * CH, (x + a) * width : (x + a + 1) * width] = high
            low_ref[a * CH : (a + 1) * CH, (x + a) * width : (x + a + 1) * width] = low

    for row in range(0, ring, 2):
        where = slice(row * width, (row + 2) * width)
        high, low = halves(g_ref[:, where])
        hidden = dot3(headt_ref[...], high, low)
        second = second_ref[:, where]
        delta = hidden * (1.0 - second * second)
        for part in range(2):
            value = delta[:, part * width : (part + 1) * width]
            put_moved(d2_high, d2_low, row + part, value, -1)
            x = row + part - 2
            if 0 <= x < tile:
                put_own(own2_high, own2_low, x, value)
    for row in range(tile + 2):
        put_moved(act_high, act_low, row, first_ref[:, (row + 2) * width : (row + 3) * width], 1)
    limit = act_high.shape[0]
    out2 = dot3_nt(act_high[...], act_low[...], own2_high[...], own2_low[...])
    par_ref[:limit, : 3 * CH] = out2
    inside2 = jnp.concatenate([inside] * 2, axis=1)
    for row in range(0, tile + 2, 2):
        total = jnp.zeros((CH, 2 * width), F32)
        for a in range(3):
            start = row + 1 - STEPS[a]
            where = slice(start * width, (start + 2) * width)
            total = total + dot3(w2b_ref[a], d2_high[:, where], d2_low[:, where])
        first = first_ref[:, (row + 2) * width : (row + 4) * width]
        delta = total * (1.0 - first * first) * inside2
        for part in range(2):
            value = delta[:, part * width : (part + 1) * width]
            put_moved(d1_high, d1_low, row + part, value, -1)
            x = row + part - 1
            if 0 <= x < tile:
                put_own(own1_high, own1_low, x, value)
    high, low = halves(wind_stack[...])
    par_ref[limit : limit + 16, : 3 * CH] = dot3_nt(high, low, own1_high[...], own1_low[...])
    mid = slice(2 * width, (2 + tile) * width)
    own_rows = jnp.concatenate([own] * tile, axis=1)
    g_high, g_low = halves(jnp.where(own_rows, g_ref[:, mid], 0.0))
    s_high, s_low = halves(second_ref[:, mid])
    raw = dot3_nt(g_high, g_low, s_high, s_low)
    place = lax.broadcasted_iota(jnp.int32, raw.shape, 0)
    mean0 = jnp.sum(jnp.where(place < 9, raw, 0.0), axis=0, keepdims=True) / 9.0
    mean1 = jnp.sum(jnp.where((place >= 9) & (place < 18), raw, 0.0), axis=0, keepdims=True) / 9.0
    par_ref[limit + 16 : limit + 16 + CH, :CH] = CORRECTION * (raw - jnp.where(place < 9, mean0, mean1))
    for row in range(0, tile, 2):
        total = jnp.zeros((16, 2 * width), F32)
        for a in range(3):
            start = row + 1 - STEPS[a]
            where = slice(start * width, (start + 2) * width)
            total = total + dot3(w1b_ref[a], d1_high[:, where], d1_low[:, where])
        for part in range(2):
            net_ref[:, row + part, :] = total[:4, part * width : part * width + cols]
    for level in range(LEVELS):
        cx = COURANT * wind_ref[2 * level, HALO : HALO + tile, :cols]
        cy = COURANT * wind_ref[2 * level + 1, HALO : HALO + tile, :cols]
        px, py = lax_wendroff(cx), lax_wendroff(cy)
        dx, dy = (0.5 + cx, -2.0 * cx, cx - 0.5), (0.5 + cy, -2.0 * cy, cy - 0.5)
        gx_sum = jnp.zeros((tile, cols), F32)
        gy_sum = jnp.zeros((tile, cols), F32)
        for a in range(3):
            for b in range(3):
                grad = sum_ref[9 * level + 3 * a + b, :tile, :cols]
                gx_sum = gx_sum + grad * (dx[a] * py[b])
                gy_sum = gy_sum + grad * (px[a] * dy[b])
        wgrad_ref[2 * level] = COURANT * gx_sum + net_ref[2 * level]
        wgrad_ref[2 * level + 1] = COURANT * gy_sum + net_ref[2 * level + 1]


def lax_wendroff(courant):
    return (
        0.5 * courant + 0.5 * courant * courant,
        1.0 - courant * courant,
        0.5 * courant * courant - 0.5 * courant,
    )


def tracer_kernel(levels_ref, wind_ref, corr_ref, main_ref, below_ref, above_ref, out_ref, coef_ref):
    count, tile, cols = out_ref.shape
    for level in range(LEVELS):
        px = lax_wendroff(COURANT * wind_ref[2 * level])
        py = lax_wendroff(COURANT * wind_ref[2 * level + 1])
        for a in range(3):
            for b in range(3):
                coef = corr_ref[9 * level + 3 * a + b] + px[a] * py[b]
                coef = turn(turn(coef, -STEPS[b], 1), HALO - STEPS[a], 0)
                coef_ref[level, 3 * a + b] = coef[:tile, :cols]

    def step(t, carry):
        level = levels_ref[t]
        field = load_field(count + t, main_ref, below_ref, above_ref)
        total = jnp.zeros((tile, cols), F32)
        for b in range(3):
            moved = turn(field, -STEPS[b], 1)
            for a in range(3):
                total = total + coef_ref[level, 3 * a + b] * turn(moved, -STEPS[a], 0)[:tile, :cols]
        out_ref[t] = total.astype(BF16)
        return carry

    lax.fori_loop(0, count, step, 0, unroll=4)


def call(kernel, outs, scratch, smem, operands, flops):
    specs = [pl.BlockSpec(memory_space=pltpu.SMEM if i < smem else pltpu.VMEM) for i in range(len(operands))]
    whole = pl.BlockSpec(memory_space=pltpu.VMEM)
    return pl.pallas_call(
        kernel,
        out_shape=outs,
        in_specs=specs,
        out_specs=[whole] * len(outs) if isinstance(outs, (list, tuple)) else whole,
        scratch_shapes=scratch,
        compiler_params=pltpu.CompilerParams(vmem_limit_bytes=40 * 1024 * 1024),
        cost_estimate=pl.CostEstimate(flops=flops, bytes_accessed=2_000_000, transcendentals=0),
    )(*operands)


def stacked(weights):
    return jnp.concatenate(pieces(weights, 2), axis=-2).astype(BF16)


def pad_to(array, rows, cols):
    widths = [(0, 0)] * (array.ndim - 2) + [(0, rows - array.shape[-2]), (0, cols - array.shape[-1])]
    return jnp.pad(array, widths)


def ring_pairs(size, wrap):
    up = [(i, (i + 1) % size) for i in range(size if wrap else size - 1)]
    return up, [(j, i) for i, j in up]


def sum_over(value, axis):
    size = lax.axis_size(axis)
    if size & (size - 1):
        return lax.psum(value, axis)
    step = 1
    while step < size:
        value = value + lax.ppermute(value, axis, [(i, i ^ step) for i in range(size)])
        step *= 2
    return value


def body(tracers, cotangent, winds, levels, conv1, bias1, conv2, bias2, head):
    count, tile, cols = tracers.shape
    n_wind = winds.shape[0]
    width = cols + LANES
    rows = tile + 2 * HALO
    gy, gy_size = lax.axis_index("gy"), lax.axis_size("gy")
    field = jnp.concatenate([tracers, cotangent] + [p.astype(BF16) for p in pieces(winds, 3)], axis=0)
    head_cols, tail_cols = field[..., :LANES], field[..., cols - LANES :]
    lane = lax.broadcasted_iota(jnp.int32, (1, 1, LANES), 2)
    up, down = ring_pairs(gy_size, False)
    if gy_size == 2:
        got = lax.ppermute(jnp.where(gy == 0, tail_cols, head_cols), "gy", up + down)
        side = jnp.where(jnp.where(gy == 0, lane < HALO, lane >= LANES - HALO), got, 0)
    else:
        right = lax.ppermute(head_cols, "gy", down)
        left = lax.ppermute(tail_cols, "gy", up)
        side = jnp.where(lane < HALO, right, jnp.where(lane >= LANES - HALO, left, 0))
    side = side.astype(BF16)
    main = jnp.concatenate([field, side], axis=2)
    up, down = ring_pairs(lax.axis_size("gx"), True)
    above = lax.ppermute(main[:, tile - HALO :], "gx", up)
    below = lax.ppermute(main[:, :HALO], "gx", down)

    def wind_of(part):
        split = part[2 * count :].astype(F32)
        return split[:n_wind] + split[n_wind : 2 * n_wind] + split[2 * n_wind :]

    wind_ext = jnp.concatenate([wind_of(above), wind_of(main), wind_of(below)], axis=1)
    place = lax.broadcasted_iota(jnp.int32, (1, width), 1)
    has_right, has_left = gy < gy_size - 1, gy > 0
    inside = jnp.where(place < cols, True, jnp.where(place < cols + LANES // 2, has_right, has_left)).astype(F32)

    split1 = conv1.reshape(CH, n_wind, 3, 3)
    split2 = conv2.reshape(CH, CH, 3, 3)
    w1 = stacked(pad_to(split1.transpose(2, 0, 3, 1).reshape(3, CH, 3 * n_wind), CH, 16))
    w2 = stacked(split2.transpose(2, 0, 3, 1).reshape(3, CH, 3 * CH))
    w2b = stacked(split2.transpose(2, 1, 3, 0).reshape(3, CH, 3 * CH))
    w1b = stacked(pad_to(split1.transpose(2, 1, 3, 0).reshape(3, n_wind, 3 * CH), 16, 3 * CH))
    by_level = head.reshape(LEVELS, 9, CH)
    centred = (CORRECTION * (by_level - jnp.mean(by_level, axis=1, keepdims=True))).reshape(9 * LEVELS, CH)
    head_w = stacked(pad_to(centred, CH, CH))
    head_t = stacked(pad_to(centred.T, CH, CH))

    vmem = pltpu.VMEM
    mine = call(
        grad_kernel,
        jax.ShapeDtypeStruct((9 * LEVELS, rows, width), F32),
        [vmem((3, count, rows, width), F32), vmem((count, rows, width), F32)],
        1,
        (levels, main, below, above),
        2_000_000,
    )
    pairs = [(i, i ^ 1) for i in range(lax.axis_size("tracer"))]
    other = lax.ppermute(mine, "tracer", pairs)
    first, second, corr = call(
        forward_kernel,
        [
            jax.ShapeDtypeStruct((CH, (rows - 2) * width), F32),
            jax.ShapeDtypeStruct((CH, (rows - 4) * width), F32),
            jax.ShapeDtypeStruct((9 * LEVELS, rows, width), F32),
        ],
        [vmem((16, rows * width), F32)] + [vmem((3 * CH, (rows - 2) * width), BF16)] * 2,
        0,
        (wind_ext, inside, w1, bias1[:, None], w2, bias2[:, None], head_w),
        2_000_000,
    )
    ring, own = (tile + 4) * width, (tile + 2) * width
    wind_grad, params = call(
        backward_kernel,
        [jax.ShapeDtypeStruct((n_wind, tile, cols), F32), jax.ShapeDtypeStruct((160, LANES), F32)],
        [vmem((9 * LEVELS, rows, width), F32), vmem((CH, ring), F32)]
        + [vmem((3 * CH, ring), BF16)] * 2
        + [vmem((3 * CH, own), BF16)] * 2
        + [vmem((3 * CH + 16, own), BF16)] * 2
        + [vmem((3 * CH, own), BF16)] * 4
        + [vmem((16, own), F32), vmem((n_wind, tile, cols), F32)],
        0,
        (mine, other, wind_ext, inside, first, second, head_t, w2b, w1b),
        2_000_000,
    )
    params = sum_over(sum_over(params, "gy"), "gx")
    tracer_grad = call(
        tracer_kernel,
        jax.ShapeDtypeStruct((count, tile, cols), BF16),
        [vmem((LEVELS, 9, tile, cols), F32)],
        1,
        (levels, wind_ext, corr, main, below, above),
        2_000_000,
    )
    conv2_grad = params[: 3 * CH, : 3 * CH].reshape(3, CH, 3, CH).transpose(3, 1, 2, 0).reshape(CH, 9 * CH)
    bias2_grad = params[3 * CH, CH : 2 * CH]
    low = params[3 * CH + 16 : 3 * CH + 32, : 3 * CH]
    conv1_grad = low[: 3 * n_wind].reshape(3, n_wind, 3, CH).transpose(3, 1, 2, 0).reshape(CH, 9 * n_wind)
    bias1_grad = low[3 * n_wind, CH : 2 * CH]
    head_grad = params[3 * CH + 32 : 3 * CH + 32 + 9 * LEVELS, :CH]
    return (tracer_grad, wind_grad, conv1_grad, bias1_grad, conv2_grad, bias2_grad, head_grad)


def solution(mesh):
    return jax.shard_map(
        body,
        mesh=mesh,
        in_specs=(
            P(("member", "tracer"), "gx", "gy"),
            P(("member", "tracer"), "gx", "gy"),
            P("member", "gx", "gy"),
            P(("member", "tracer")),
            P(),
            P(),
            P(),
            P(),
            P(),
        ),
        out_specs=(
            P(("member", "tracer"), "gx", "gy"),
            P("member", "gx", "gy"),
            P("member", None),
            P("member"),
            P("member", None),
            P("member"),
            P("member", None),
        ),
        check_vma=False,
    )
```

time: 190 us -> 53.7 us (0.28)
  starting transfers between devices: 57.6 us -> 10.1 us
  blocking collectives: 39.4 us -> 0 us
  matrix products: 30.2 us -> 0 us
  between operations: 15.8 us -> 1.02 us
  Pallas kernels: 0 us -> 13.2 us
  local copies, waits for them, and re-layouts: 19.8 us -> 8.73 us
  other arithmetic: 5.99 us -> 0.74 us
    ppermute x24 -> x7, starting transfers between devices: 57.5 us -> 10.1 us  [the longest x1 3.65 us: body(): below = lax.ppermute(main[:, :HALO], 'gx', down)]
    psum x1 -> x0, blocking collectives: 39.4 us -> none  [body(): lax.psum((conv1_grad, bias1_grad, conv2_grad, bias2_grad, head_grad), ('g...]
    dot_general x75 -> x0, matrix products: 30.2 us -> none  [the longest x18 7.96 us: convolve_local(): jnp.einsum('oi,ixy->oxy', kernel[:, :, offset], window(padded, 1 + step_x...]
    pallas_call x0 -> x4, Pallas kernels: none -> 13.2 us  [call(): pl.pallas_call(kernel, out_shape=outs, in_specs=specs, out_specs=[whole]...]
    unnamed x147 -> x22, local copies, waits for them, and re-layouts: 15.9 us -> 6.06 us
    concatenate x10, other arithmetic: 2.79 us -> 0.47 us  [the longest x2 0.23 us: body(): main = jnp.concatenate([field, side], axis=2)]
    slice x15 -> x3, local copies, waits for them, and re-layouts: 2.82 us -> 0.61 us  [the longest x1 0.6 us: body(): head_grad = params[3 * CH + 32:3 * CH + 32 + 9 * LEVELS, :CH]]
    ppermute x24 -> x7, waiting for transfers between devices: 19.6 us -> 19.6 us  [the longest x3 9.06 us: sum_over(): lax.ppermute(value, axis, [(i, i ^ step) for i in range(size)])]
  transfers between devices with their start and end apart: 25 -> 7, of which waited for: 11 -> 5; matrix products, arithmetic and copies ran while one was open for 15% -> 3% of each run, Pallas kernels for 0% -> 11%
where the time goes in v1:
time: 53.7 us; the launch traced here: 53.4 us
  waiting for transfers between devices  19.6 us (36%)
  Pallas kernels  13.2 us (25%)
  starting transfers between devices  10.1 us (19%)
  local copies, waits for them, and re-layouts  8.73 us (16%)
  between operations  1.02 us (2%)
  other arithmetic  0.74 us (1%)
    pallas_call x4, Pallas kernels, call(): pl.pallas_call(kernel, out_shape=outs, in_specs=specs, out_specs=[whole]...  13.2 us
    ppermute x3, waiting for transfers between devices, sum_over(): lax.ppermute(value, axis, [(i, i ^ step) for i in range(size)])  9.06 us
    ppermute x1, waiting for transfers between devices, body(): below = lax.ppermute(main[:, :HALO], 'gx', down)  6.09 us
    unnamed x22, local copies, waits for them, and re-layouts  6.06 us
    ppermute x1, waiting for transfers between devices, body(): above = lax.ppermute(main[:, tile - HALO:], 'gx', up)  4.44 us
    ppermute x1, starting transfers between devices, body(): below = lax.ppermute(main[:, :HALO], 'gx', down)  3.65 us
    ppermute x3, starting transfers between devices, sum_over(): lax.ppermute(value, axis, [(i, i ^ step) for i in range(size)])  3.37 us
    ppermute x1, starting transfers between devices, body(): lax.ppermute(jnp.where(gy == 0, tail_cols, head_cols), 'gy', up + down)  3 us
  transfers between devices with their start and end apart: 7, of which 5 were waited for; matrix products, arithmetic and copies ran while one was open for 3% of the time, Pallas kernels for 11%

profile of v1, /device:TPU:0, one launch (start us, length us, event | category | flops | bytes accessed | tf_op | source)
XLA Modules:
  0.0 53.4 jit_solution(17538005713349707573)
XLA Ops:
  0.6 0.0 copy-start.2
  0.6 0.9 %constant_dynamic-update-slice_fusion.1 = bf16[76,8,256]{2,1,0:T(8,128)(2,1)S(1)} fusion(bf16[32,8,256]{2,1,0:T(8,128)(2,1)} %param.9), kind=kLoop, calls=%fused_computation.61 | loop fusion | bytes 262144
  1.6 0.0 copy-done.2
  1.6 0.0 copy-start.1
  1.6 0.7 %copy-done.1 = f32[4,8,256]{2,1,0:T(8,128)S(1)} copy-done((f32[4,8,256]{2,1,0:T(8,128)S(1)}, f32[4,8,256]{2,1,0:T(8,128)}, u32[]{:S(2)}) %copy-start.1) | copy-done | bytes 32792
  2.4 0.0 copy-start.5
  2.4 3.0 %collective-permute-start = (bf16[76,8,128]{2,1,0:T(8,128)(2,1)S(1)}, bf16[76,8,128]{2,1,0:T(8,128)(2,1)S(1)}, u32[]{:S(2)}, u32[]{:S(2)}) collective-permute-start(bf16[76,8,128]{2,1,0:T(8,128)(2,1)S(1)} %slice_select_fusion), channel_id=1, source_target_pairs={{0,2},{2,0},{1,3},{3,1},{4,6},{6,4},{5,7},{7,5},{8,10},{10,8},{9,1... | collective-permute-start | bytes 466952 | tf_op jit(solution)/shard_map/ppermute | solution.py:311
  5.5 0.0 copy-done.5
  5.5 0.1 copy.58
  5.6 0.0 copy-start.4
  5.6 0.8 %copy-done.4 = f32[32,288]{1,0:T(8,128)S(1)} copy-done((f32[32,288]{1,0:T(8,128)S(1)}, f32[32,288]{1,0:T(8,128)}, u32[]{:S(2)}) %copy-start.4) | copy-done | bytes 36888
  6.4 0.1 copy.60
  6.5 0.1 reshape.94
  6.5 0.1 copy.61
  6.7 0.1 reshape.95
  6.8 0.0 copy-start.3
  6.9 0.7 %copy-done.3 = f32[18,32]{1,0:T(8,128)S(1)} copy-done((f32[18,32]{1,0:T(8,128)S(1)}, f32[18,32]{1,0:T(8,128)}, u32[]{:S(2)}) %copy-start.3) | copy-done | bytes 2328
  7.6 0.1 copy.62
  7.7 0.1 reshape.103
  7.9 0.1 reshape.104
  8.0 0.1 pad_maximum_fusion.6
  8.1 0.1 pad_maximum_fusion.7
  8.2 0.1 copy.63.w1_ref
  8.3 0.0 copy-start.6
  8.3 0.6 %copy-done.6 = f32[32]{0:T(128)S(1)} copy-done((f32[32]{0:T(128)S(1)}, f32[32]{0:T(128)}, u32[]{:S(2)}) %copy-start.6) | copy-done | bytes 152
  9.0 0.1 copy.64.b1_ref
  9.1 0.0 copy-start.7
  9.1 0.7 %copy-done.7 = f32[32]{0:T(128)S(1)} copy-done((f32[32]{0:T(128)S(1)}, f32[32]{0:T(128)}, u32[]{:S(2)}) %copy-start.7) | copy-done | bytes 152
  9.7 0.1 copy.65.b2_ref
  9.8 0.1 copy.66.head_ref
  9.9 0.0 collective-permute-done
  10.0 0.2 fusion
  10.2 3.7 %collective-permute-start.2 = (bf16[76,4,384]{2,1,0:T(4,128)(2,1)S(1)}, bf16[76,4,384]{2,1,0:T(4,128)(2,1)S(1)}, u32[]{:S(2)}, u32[]{:S(2)}) collective-permute-start(bf16[76,4,384]{2,1,0:T(4,128)(2,1)S(1)} %get-tuple-element.39), channel_id=1, source_target_pairs={{4,0},{8,4},{12,8},{0,12},{5,1},{9,5},{13,9},{1,13},{6,2},{10,6},{... | collective-permute-start | bytes 700424 | tf_op jit(solution)/shard_map/ppermute | solution.py:321
  13.9 0.0 collective-permute-start.1
  13.9 0.0 copy-start
  13.9 6.1 %collective-permute-done.2.below_ref = bf16[76,4,384]{2,1,0:T(4,128)(2,1)S(1)} collective-permute-done((bf16[76,4,384]{2,1,0:T(4,128)(2,1)S(1)}, bf16[76,4,384]{2,1,0:T(4,128)(2,1)S(1)}, u32[]{:S(2)}, u32[]{:S(2)}) %collective-permute-start.2) | collective-permute-done | bytes 233504 | tf_op jit(solution)/shard_map/ppermute | solution.py:321
  20.0 4.4 %collective-permute-done.1.above_ref = bf16[76,4,384]{2,1,0:T(4,128)(2,1)S(1)} collective-permute-done((bf16[76,4,384]{2,1,0:T(4,128)(2,1)S(1)}, bf16[76,4,384]{2,1,0:T(4,128)(2,1)S(1)}, u32[]{:S(2)}, u32[]{:S(2)}) %collective-permute-start.1) | collective-permute-done | bytes 233504 | tf_op jit(solution)/shard_map/ppermute | solution.py:320
  24.4 0.0 copy-done
  24.4 3.0 %shard_map.146.mine_ref = f32[18,16,384]{2,1,0:T(8,128)S(1)} custom-call(s32[32]{0:T(128)S(1)} %copy-done, bf16[76,8,384]{2,1,0:T(8,128)(2,1)S(1)} %pad_maximum_fusion.main_ref, bf16[76,4,384]{2,1,0:T(4,128)(2,1)S(1)} %collective-permute-done.2.below_ref, bf16[76,4,384]{2,1,0:T(4,128)(2,1)S(1)} %collective-permute-done.1.above_ref), custom_call_target="tpu_custom_call" | custom-call | flops 2000000 | bytes 2000000 | tf_op jit(solution)/shard_map/pallas_call | solution.py:264
  27.5 0.1 collective-permute-start.3
  27.7 3.8 %shard_map.144 = (f32[32,5376]{1,0:T(8,128)S(1)}, f32[32,4608]{1,0:T(8,128)S(1)}, f32[18,16,384]{2,1,0:T(8,128)S(1)}) custom-call(f32[4,16,384]{2,1,0:T(8,128)S(1)} %pad_maximum_fusion.1.wind_ref, f32[1,384]{1,0:T(1,128)S(1)} %select_convert_fusion.inside_ref, bf16[3,64,16]{2,1,0:T(8,128)(2,1)S(1)} %copy.63.w1_ref, f32[32,1]{1,0:T(8,128)S(1)} %copy.64.b1_ref, ...), custom_call_target="tpu_custom_call" | custom-call | flops 2000000 | bytes 2000000 | tf_op jit(solution)/shard_map/pallas_call | solution.py:264
  31.4 0.0 collective-permute-done.3.other_ref
  31.5 4.1 %shard_map.147 = (f32[4,8,256]{2,1,0:T(8,128)}, f32[160,128]{1,0:T(8,128)S(1)}) custom-call(f32[18,16,384]{2,1,0:T(8,128)S(1)} %shard_map.146.mine_ref, f32[18,16,384]{2,1,0:T(8,128)S(1)} %collective-permute-done.3.other_ref, f32[4,16,384]{2,1,0:T(8,128)S(1)} %pad_maximum_fusion.1.wind_ref, f32[1,384]{1,0:T(1,128)S(1)} %select_convert_fusion.inside_ref, ...), custom_call_target="tpu_custom_call" | custom-call | flops 2000000 | bytes 2000000 | tf_op jit(solution)/shard_map/pallas_call | solution.py:264
  35.6 0.9 %collective-permute-start.4 = (f32[160,128]{1,0:T(8,128)S(1)}, f32[160,128]{1,0:T(8,128)S(1)}, u32[]{:S(2)}, u32[]{:S(2)}) collective-permute-start(f32[160,128]{1,0:T(8,128)S(1)} %get-tuple-element.16), channel_id=1, source_target_pairs={{0,2},{2,0},{1,3},{3,1},{4,6},{6,4},{5,7},{7,5},{8,10},{10,8},{9,1... | collective-permute-start | bytes 245768 | tf_op jit(solution)/shard_map/ppermute | solution.py:295
  36.5 3.9 %collective-permute-done.4 = f32[160,128]{1,0:T(8,128)S(1)} collective-permute-done((f32[160,128]{1,0:T(8,128)S(1)}, f32[160,128]{1,0:T(8,128)S(1)}, u32[]{:S(2)}, u32[]{:S(2)}) %collective-permute-start.4) | collective-permute-done | bytes 81952 | tf_op jit(solution)/shard_map/ppermute | solution.py:295
  40.4 1.7 %collective-permute-start.5 = (f32[160,128]{1,0:T(8,128)S(1)}, f32[160,128]{1,0:T(8,128)S(1)}, u32[]{:S(2)}, u32[]{:S(2)}) collective-permute-start(f32[160,128]{1,0:T(8,128)S(1)} %add.41), channel_id=1, source_target_pairs={{0,4},{4,0},{8,12},{12,8},{1,5},{5,1},{9,13},{13,9},{2,6},{6,2},{1... | collective-permute-start | bytes 245768 | tf_op jit(solution)/shard_map/ppermute | solution.py:295
  42.1 2.8 %collective-permute-done.5 = f32[160,128]{1,0:T(8,128)S(1)} collective-permute-done((f32[160,128]{1,0:T(8,128)S(1)}, f32[160,128]{1,0:T(8,128)S(1)}, u32[]{:S(2)}, u32[]{:S(2)}) %collective-permute-start.5) | collective-permute-done | bytes 81952 | tf_op jit(solution)/shard_map/ppermute | solution.py:295
  44.9 0.8 %collective-permute-start.6 = (f32[160,128]{1,0:T(8,128)S(1)}, f32[160,128]{1,0:T(8,128)S(1)}, u32[]{:S(2)}, u32[]{:S(2)}) collective-permute-start(f32[160,128]{1,0:T(8,128)S(1)} %add.42), channel_id=1, source_target_pairs={{0,8},{4,12},{8,0},{12,4},{1,9},{5,13},{9,1},{13,5},{2,10},{6,14},... | collective-permute-start | bytes 245768 | tf_op jit(solution)/shard_map/ppermute | solution.py:295
  45.7 2.3 %shard_map.145 = bf16[32,8,256]{2,1,0:T(8,128)(2,1)} custom-call(s32[32]{0:T(128)S(1)} %copy-done, f32[4,16,384]{2,1,0:T(8,128)S(1)} %pad_maximum_fusion.1.wind_ref, f32[18,16,384]{2,1,0:T(8,128)S(1)} %get-tuple-element.12.corr_ref, bf16[76,8,384]{2,1,0:T(8,128)(2,1)S(1)} %pad_maximum_fusion.main_ref, ...), custom_call_target="tpu_custom_call" | custom-call | flops 2000000 | bytes 2000000 | tf_op jit(solution)/shard_map/pallas_call | solution.py:264
  48.0 2.3 %collective-permute-done.6 = f32[160,128]{1,0:T(8,128)S(1)} collective-permute-done((f32[160,128]{1,0:T(8,128)S(1)}, f32[160,128]{1,0:T(8,128)S(1)}, u32[]{:S(2)}, u32[]{:S(2)}) %collective-permute-start.6) | collective-permute-done | bytes 81952 | tf_op jit(solution)/shard_map/ppermute | solution.py:295
  50.4 0.6 %slice_bitcast_fusion = (f32[32]{0:T(128)}, f32[32]{0:T(128)}) fusion(f32[160,128]{1,0:T(8,128)S(1)} %add.43), kind=kLoop, calls=%fused_computation.66 | loop fusion | bytes 512 | tf_op jit(solution)/shard_map/squeeze | solution.py:390
  51.0 0.6 %slice.110 = f32[18,32]{1,0:T(8,128)} slice(f32[160,128]{1,0:T(8,128)S(1)} %add.43), slice={[128:146], [0:32]} | slice | bytes 4608 | tf_op jit(solution)/shard_map/slice | solution.py:394
  51.6 0.1 reshape.99
  51.7 0.7 %copy.71 = f32[32,36]{1,0:T(8,128)} copy(f32[32,36]{0,1:T(8,128)S(1)} %reshape.100) | data formatting | bytes 9216
  52.4 0.1 reshape.101
  52.5 0.1 copy.70
  52.6 0.1 reshape.102
  52.7 0.7 %copy.72 = f32[32,288]{1,0:T(8,128)} copy(f32[32,288]{0,1:T(8,128)S(1)} %reshape.102) | data formatting | bytes 73728
  (44 shorter events, 0.5 us)
Async XLA Ops:
  0.6 1.0 %copy-start.2 = (bf16[32,8,256]{2,1,0:T(8,128)(2,1)S(1)}, bf16[32,8,256]{2,1,0:T(8,128)(2,1)}, u32[]{:S(2)}) copy-start(bf16[32,8,256]{2,1,0:T(8,128)(2,1)} %param.10) | copy-start | bytes 393220
  1.6 0.8 %copy-start.1 = (f32[4,8,256]{2,1,0:T(8,128)S(1)}, f32[4,8,256]{2,1,0:T(8,128)}, u32[]{:S(2)}) copy-start(f32[4,8,256]{2,1,0:T(8,128)} %param.11) | copy-start | bytes 98308
  2.4 3.0 %copy-start.5 = (f32[32,36]{1,0:T(8,128)S(1)}, f32[32,36]{1,0:T(8,128)}, u32[]{:S(2)}) copy-start(f32[32,36]{1,0:T(8,128)} %param.13) | copy-start | bytes 13828
  2.4 7.5 %collective-permute-start = (bf16[76,8,128]{2,1,0:T(8,128)(2,1)S(1)}, bf16[76,8,128]{2,1,0:T(8,128)(2,1)S(1)}, u32[]{:S(2)}, u32[]{:S(2)}) collective-permute-start(bf16[76,8,128]{2,1,0:T(8,128)(2,1)S(1)} %slice_select_fusion), channel_id=1, source_target_pairs={{0,2},{2,0},{1,3},{3,1},{4,6},{6,4},{5,7},{7,5},{8,10},{10,8},{9,1... | collective-permute-start | bytes 466952 | tf_op jit(solution)/shard_map/ppermute | solution.py:311
  5.6 0.8 %copy-start.4 = (f32[32,288]{1,0:T(8,128)S(1)}, f32[32,288]{1,0:T(8,128)}, u32[]{:S(2)}) copy-start(f32[32,288]{1,0:T(8,128)} %param.15) | copy-start | bytes 110596
  6.8 0.7 %copy-start.3 = (f32[18,32]{1,0:T(8,128)S(1)}, f32[18,32]{1,0:T(8,128)}, u32[]{:S(2)}) copy-start(f32[18,32]{1,0:T(8,128)} %param.17) | copy-start | bytes 6916
  8.3 0.7 %copy-start.6 = (f32[32]{0:T(128)S(1)}, f32[32]{0:T(128)}, u32[]{:S(2)}) copy-start(f32[32]{0:T(128)} %param.14) | copy-start | bytes 388
  9.1 0.7 %copy-start.7 = (f32[32]{0:T(128)S(1)}, f32[32]{0:T(128)}, u32[]{:S(2)}) copy-start(f32[32]{0:T(128)} %param.16) | copy-start | bytes 388
  10.2 9.8 %collective-permute-start.2 = (bf16[76,4,384]{2,1,0:T(4,128)(2,1)S(1)}, bf16[76,4,384]{2,1,0:T(4,128)(2,1)S(1)}, u32[]{:S(2)}, u32[]{:S(2)}) collective-permute-start(bf16[76,4,384]{2,1,0:T(4,128)(2,1)S(1)} %get-tuple-element.39), channel_id=1, source_target_pairs={{4,0},{8,4},{12,8},{0,12},{5,1},{9,5},{13,9},{1,13},{6,2},{10,6},{... | collective-permute-start | bytes 700424 | tf_op jit(solution)/shard_map/ppermute | solution.py:321
  13.9 10.6 %collective-permute-start.1 = (bf16[76,4,384]{2,1,0:T(4,128)(2,1)S(1)}, bf16[76,4,384]{2,1,0:T(4,128)(2,1)S(1)}, u32[]{:S(2)}, u32[]{:S(2)}) collective-permute-start(bf16[76,4,384]{2,1,0:T(4,128)(2,1)S(1)} %get-tuple-element.38), channel_id=1, source_target_pairs={{0,4},{4,8},{8,12},{12,0},{1,5},{5,9},{9,13},{13,1},{2,6},{6,10},{... | collective-permute-start | bytes 700424 | tf_op jit(solution)/shard_map/ppermute | solution.py:320
  13.9 10.6 %copy-start = (s32[32]{0:T(128)S(1)}, s32[32]{0:T(128)}, u32[]{:S(2)}) copy-start(s32[32]{0:T(128)} %levels_ref.3) | copy-start | bytes 388
  27.5 4.0 %collective-permute-start.3 = (f32[18,16,384]{2,1,0:T(8,128)S(1)}, f32[18,16,384]{2,1,0:T(8,128)S(1)}, u32[]{:S(2)}, u32[]{:S(2)}) collective-permute-start(f32[18,16,384]{2,1,0:T(8,128)S(1)} %shard_map.146.mine_ref), channel_id=1, source_target_pairs={{0,1},{1,0},{2,3},{3,2},{4,5},{5,4},{6,7},{7,6},{8,9},{9,8},{10,11... | collective-permute-start | bytes 1327112 | tf_op jit(solution)/shard_map/ppermute | solution.py:353
  35.6 4.8 %collective-permute-start.4 = (f32[160,128]{1,0:T(8,128)S(1)}, f32[160,128]{1,0:T(8,128)S(1)}, u32[]{:S(2)}, u32[]{:S(2)}) collective-permute-start(f32[160,128]{1,0:T(8,128)S(1)} %get-tuple-element.16), channel_id=1, source_target_pairs={{0,2},{2,0},{1,3},{3,1},{4,6},{6,4},{5,7},{7,5},{8,10},{10,8},{9,1... | collective-permute-start | bytes 245768 | tf_op jit(solution)/shard_map/ppermute | solution.py:295
  40.4 4.5 %collective-permute-start.5 = (f32[160,128]{1,0:T(8,128)S(1)}, f32[160,128]{1,0:T(8,128)S(1)}, u32[]{:S(2)}, u32[]{:S(2)}) collective-permute-start(f32[160,128]{1,0:T(8,128)S(1)} %add.41), channel_id=1, source_target_pairs={{0,4},{4,0},{8,12},{12,8},{1,5},{5,1},{9,13},{13,9},{2,6},{6,2},{1... | collective-permute-start | bytes 245768 | tf_op jit(solution)/shard_map/ppermute | solution.py:295
  44.9 5.4 %collective-permute-start.6 = (f32[160,128]{1,0:T(8,128)S(1)}, f32[160,128]{1,0:T(8,128)S(1)}, u32[]{:S(2)}, u32[]{:S(2)}) collective-permute-start(f32[160,128]{1,0:T(8,128)S(1)} %add.42), channel_id=1, source_target_pairs={{0,8},{4,12},{8,0},{12,4},{1,9},{5,13},{9,1},{13,5},{2,10},{6,14},... | collective-permute-start | bytes 245768 | tf_op jit(solution)/shard_map/ppermute | solution.py:295

commit v2 on v1

--- a/solution.py
+++ b/solution.py
@@ -14,6 +14,7 @@
 STEPS = (-1, 0, 1)
 HALO = 4
 LANES = 128
+GROUP = LANES // (2 * HALO)
 F32 = jnp.float32
 BF16 = jnp.bfloat16
 NT = (((1,), (1,)), ((), ()))
@@ -51,27 +52,84 @@
     return pltpu.roll(value, shift, axis) if shift else value
 
 
-def load_field(index, main_ref, below_ref, above_ref):
-    strip = jnp.concatenate([below_ref[index].astype(F32), above_ref[index].astype(F32)], axis=0)
-    return jnp.concatenate([main_ref[index].astype(F32), strip], axis=0)
-
-
-def grad_kernel(levels_ref, main_ref, below_ref, above_ref, out_ref, moved_ref, cot_ref):
+def side_mask():
+    lane = lax.broadcasted_iota(jnp.int32, (1, LANES), 1)
+    return (lane < HALO) | (lane >= LANES - HALO)
+
+
+def rows_of(below, above):
+    return jnp.concatenate([below.astype(F32), above.astype(F32)], axis=0)
+
+
+def sides_of(group, side_ref, below_ref, above_ref, channels):
+    index = channels + group % 3
+    where = slice(group // 3 * LANES, (group // 3 + 1) * LANES)
+    return side_ref[group].astype(F32), rows_of(below_ref[index, :, where], above_ref[index, :, where])
+
+
+def placed(side, j):
+    return jnp.where(side_mask(), pltpu.roll(side, LANES - HALO - 2 * HALO * j, 1), 0.0)
+
+
+def load_field(index, main, below_ref, above_ref, sides, j):
+    top = jnp.concatenate([main.astype(F32), placed(sides[0], j)], axis=1)
+    strip = jnp.concatenate([rows_of(below_ref[index], above_ref[index]), placed(sides[1], j)], axis=1)
+    return jnp.concatenate([top, strip], axis=0)
+
+
+def pack_kernel(tracer_ref, cot_ref, wind_ref, out_ref):
+    count = tracer_ref.shape[0]
+    cols = tracer_ref.shape[2]
+    lane = lax.broadcasted_iota(jnp.int32, (1, LANES), 1)
+    mask = side_mask()
+
+    def lifted(head, tail, j):
+        both = jnp.where(lane < HALO, head, tail)
+        return pltpu.roll(jnp.where(mask, both, 0.0), HALO + 2 * HALO * j, 1)
+
+    group = 0
+    for ref in (tracer_ref, cot_ref):
+        for start in range(0, count, GROUP):
+            total = jnp.zeros(out_ref.shape[1:], F32)
+            for j in range(GROUP):
+                head = ref[start + j, :, :LANES].astype(F32)
+                tail = ref[start + j, :, cols - LANES :].astype(F32)
+                total = total + lifted(head, tail, j)
+            out_ref[group] = total.astype(BF16)
+            group += 1
+    total = jnp.zeros(out_ref.shape[1:], F32)
+    for i in range(wind_ref.shape[0]):
+        head, tail = wind_ref[i, :, :LANES], wind_ref[i, :, cols - LANES :]
+        for part in range(3):
+            high_head, high_tail = head.astype(BF16).astype(F32), tail.astype(BF16).astype(F32)
+            total = total + lifted(high_head, high_tail, part * wind_ref.shape[0] + i)
+            head, tail = head - high_head, tail - high_tail
+    out_ref[group] = total.astype(BF16)
+    out_ref[group + 1] = jnp.zeros(out_ref.shape[1:], BF16)
+
+
+def grad_kernel(levels_ref, tracer_ref, cot_ref, side_ref, below_ref, above_ref, out_ref, moved_ref, held_ref):
     count = levels_ref.shape[0]
-
-    def fill(t, carry):
-        field = load_field(t, main_ref, below_ref, above_ref)
-        for b in range(3):
-            moved_ref[b, t] = turn(field, STEPS[b], 1)
-        cot_ref[t] = load_field(count + t, main_ref, below_ref, above_ref)
-        return carry
-
-    lax.fori_loop(0, count, fill, 0, unroll=4)
+    channels = below_ref.shape[0] - 3
+    groups = count // GROUP
+    for group in range(groups):
+        near = sides_of(group, side_ref, below_ref, above_ref, channels)
+        far = sides_of(groups + group, side_ref, below_ref, above_ref, channels)
+
+        def fill(j, carry):
+            t = group * GROUP + j
+            field = load_field(t, tracer_ref[t], below_ref, above_ref, near, j)
+            for b in range(3):
+                moved_ref[b, t] = turn(field, STEPS[b], 1)
+            held_ref[t] = load_field(count + t, cot_ref[t], below_ref, above_ref, far, j)
+            return carry
+
+        lax.fori_loop(0, GROUP, fill, 0, unroll=4)
     for a in range(3):
         for b in range(3):
 
             def step(t, sums):
-                product = cot_ref[t] * turn(moved_ref[b, t], STEPS[a], 0)
+                product = held_ref[t] * turn(moved_ref[b, t], STEPS[a], 0)
                 upper = levels_ref[t].astype(F32)
                 return sums[0] + product, sums[1] + upper * product
 
@@ -98,8 +156,29 @@
             stack_ref[b * count : (b + 1) * count, row * width : (row + 1) * width] = turn(value, STEPS[b], 1)
 
 
-def forward_kernel(wind_ref, inside_ref, w1_ref, b1_ref, w2_ref, b2_ref, head_ref, first_ref, second_ref, corr_ref, stack_ref, high_ref, low_ref):
-    rows, width = wind_ref.shape[1:]
+def forward_kernel(
+    own_ref, side_ref, below_ref, above_ref, inside_ref, w1_ref, b1_ref, w2_ref, b2_ref, head_ref,
+    first_ref, second_ref, corr_ref, wind_ref,
+    stack_ref, high_ref, low_ref,
+):
+    count, rows, width = wind_ref.shape
+    tile, cols = own_ref.shape[1:]
+    channels = below_ref.shape[0] - 3
+    side, side_rows = sides_of((channels - 3 * count) // GROUP, side_ref, below_ref, above_ref, channels)
+    for i in range(count):
+        wind_ref[i, HALO : HALO + tile, :cols] = own_ref[i]
+        wide = [jnp.zeros((tile, LANES), F32), jnp.zeros((tile, LANES), F32)]
+        strip = jnp.zeros((2 * HALO, cols), F32)
+        for part in range(3):
+            j = part * count + i
+            wide[0] = wide[0] + placed(side, j)
+            wide[1] = wide[1] + placed(side_rows, j)
+            index = channels - 3 * count + j
+            strip = strip + rows_of(below_ref[index], above_ref[index])
+        wind_ref[i, HALO : HALO + tile, cols:] = wide[0]
+        for value, where in ((strip, slice(0, cols)), (wide[1], slice(cols, width))):
+            wind_ref[i, HALO + tile :, where] = value[:HALO]
+            wind_ref[i, :HALO, where] = value[HALO:]
     stack_ref[...] = jnp.zeros(stack_ref.shape, F32)
     put_winds(wind_ref, stack_ref, 0, rows)
     bias1, bias2 = b1_ref[...], b2_ref[...]
@@ -127,13 +206,13 @@
 
 
 def backward_kernel(
-    mine_ref, other_ref, wind_ref, inside_ref, first_ref, second_ref, headt_ref, w2b_ref, w1b_ref,
-    wgrad_ref, par_ref,
-    sum_ref, g_ref, d2_high, d2_low, own2_high, own2_low, act_high, act_low, d1_high, d1_low, own1_high, own1_low, wind_stack, net_ref,
+    mine_ref, other_ref, wind_ref, inside_ref, first_ref, second_ref, headt_ref, w2b_ref,
+    par_ref, d1_ref,
+    sum_ref, g_ref, d2_high, d2_low, own2_high, own2_low, act_high, act_low, own1_high, own1_low, wind_stack,
 ):
     cells = g_ref.shape[1]
     width = wind_ref.shape[2]
-    cols = wgrad_ref.shape[2]
+    cols = width - LANES
     ring = cells // width
     tile = ring - 4
     sum_ref[...] = mine_ref[...] + other_ref[...]
@@ -149,8 +228,7 @@
     wind_stack[...] = jnp.zeros(wind_stack.shape, F32)
     put_winds(wind_ref, wind_stack, 3, tile + 2)
     wind_stack[12:13, :] = jnp.ones((1, wind_stack.shape[1]), F32)
-    act_high[3 * CH :, :] = jnp.ones((act_high.shape[0] - 3 * CH, act_high.shape[1]), BF16)
-    act_low[3 * CH :, :] = jnp.zeros((act_high.shape[0] - 3 * CH, act_high.shape[1]), BF16)
+    bias2 = jnp.zeros((CH, width), F32)
 
     def put_own(high_ref, low_ref, x, value):
         high, low = halves(jnp.where(own, value, 0.0))
@@ -170,11 +248,12 @@
             x = row + part - 2
             if 0 <= x < tile:
                 put_own(own2_high, own2_low, x, value)
+                bias2 = bias2 + jnp.where(own, value, 0.0)
     for row in range(tile + 2):
         put_moved(act_high, act_low, row, first_ref[:, (row + 2) * width : (row + 3) * width], 1)
-    limit = act_high.shape[0]
-    out2 = dot3_nt(act_high[...], act_low[...], own2_high[...], own2_low[...])
-    par_ref[:limit, : 3 * CH] = out2
+    par_ref[...] = jnp.zeros(par_ref.shape, F32)
+    par_ref[:, : 3 * CH] = dot3_nt(act_high[...], act_low[...], own2_high[...], own2_low[...])
+    par_ref[:CH, 3 * CH + 16 : 3 * CH + 17] = jnp.sum(bias2, axis=1, keepdims=True)
     inside2 = jnp.concatenate([inside] * 2, axis=1)
     for row in range(0, tile + 2, 2):
         total = jnp.zeros((CH, 2 * width), F32)
@@ -184,23 +263,29 @@
             total = total + dot3(w2b_ref[a], d2_high[:, where], d2_low[:, where])
         first = first_ref[:, (row + 2) * width : (row + 4) * width]
         delta = total * (1.0 - first * first) * inside2
+        d1_ref[:, row * width : (row + 2) * width] = delta
         for part in range(2):
             value = delta[:, part * width : (part + 1) * width]
-            put_moved(d1_high, d1_low, row + part, value, -1)
             x = row + part - 1
             if 0 <= x < tile:
                 put_own(own1_high, own1_low, x, value)
     high, low = halves(wind_stack[...])
-    par_ref[limit : limit + 16, : 3 * CH] = dot3_nt(high, low, own1_high[...], own1_low[...])
+    par_ref[:, 3 * CH : 3 * CH + 16] = dot3_nt(own1_high[...], own1_low[...], high, low)
     mid = slice(2 * width, (2 + tile) * width)
     own_rows = jnp.concatenate([own] * tile, axis=1)
     g_high, g_low = halves(jnp.where(own_rows, g_ref[:, mid], 0.0))
     s_high, s_low = halves(second_ref[:, mid])
-    raw = dot3_nt(g_high, g_low, s_high, s_low)
-    place = lax.broadcasted_iota(jnp.int32, raw.shape, 0)
-    mean0 = jnp.sum(jnp.where(place < 9, raw, 0.0), axis=0, keepdims=True) / 9.0
-    mean1 = jnp.sum(jnp.where((place >= 9) & (place < 18), raw, 0.0), axis=0, keepdims=True) / 9.0
-    par_ref[limit + 16 : limit + 16 + CH, :CH] = CORRECTION * (raw - jnp.where(place < 9, mean0, mean1))
+    raw = dot3_nt(s_high, s_low, g_high, g_low)
+    for level in range(LEVELS):
+        rows = slice((level + 1) * CH, (level + 2) * CH)
+        par_ref[rows, 3 * CH + 16 : 3 * CH + 25] = raw[:, 9 * level : 9 * level + 9]
+
+
+def wind_kernel(mine_ref, other_ref, wind_ref, d1_ref, w1b_ref, wgrad_ref, d1_high, d1_low, net_ref):
+    tile, cols = wgrad_ref.shape[1:]
+    width = wind_ref.shape[2]
+    for row in range(tile + 2):
+        put_moved(d1_high, d1_low, row, d1_ref[:, row * width : (row + 1) * width], -1)
     for row in range(0, tile, 2):
         total = jnp.zeros((16, 2 * width), F32)
         for a in range(3):
@@ -218,11 +303,56 @@
         gy_sum = jnp.zeros((tile, cols), F32)
         for a in range(3):
             for b in range(3):
-                grad = sum_ref[9 * level + 3 * a + b, :tile, :cols]
+                k = 9 * level + 3 * a + b
+                grad = mine_ref[k, :tile, :cols] + other_ref[k, :tile, :cols]
                 gx_sum = gx_sum + grad * (dx[a] * py[b])
                 gy_sum = gy_sum + grad * (px[a] * dy[b])
         wgrad_ref[2 * level] = COURANT * gx_sum + net_ref[2 * level]
         wgrad_ref[2 * level + 1] = COURANT * gy_sum + net_ref[2 * level + 1]
+
+
+def final_kernel(mine_ref, other_ref, c1_ref, b1_ref, c2_ref, b2_ref, head_ref):
+    total = mine_ref[...] + other_ref[...]
+    across = jnp.concatenate([total, jnp.zeros((LANES - total.shape[0], LANES), F32)], axis=0).T
+    size2, size1 = c2_ref.shape[1], c1_ref.shape[1]
+    n_wind = size1 // 9
+    split, rest = [], total
+    turned, rest_t = [], across[: 3 * CH, : 3 * CH]
+    for _ in range(3):
+        high = rest.astype(BF16)
+        split.append(high)
+        rest = rest - high.astype(F32)
+        high = rest_t.astype(BF16)
+        turned.append(high)
+        rest_t = rest_t - high.astype(F32)
+    source = lax.broadcasted_iota(jnp.int32, (3 * CH, size2), 0)
+    target = lax.broadcasted_iota(jnp.int32, (3 * CH, size2), 1)
+    source1 = lax.broadcasted_iota(jnp.int32, (LANES, size1), 0) - 3 * CH
+    target1 = lax.broadcasted_iota(jnp.int32, (LANES, size1), 1)
+    out2 = jnp.zeros((CH, size2), F32)
+    out1 = jnp.zeros((CH, size1), F32)
+    for a in range(3):
+        rows = slice(a * CH, (a + 1) * CH)
+        pick2 = jnp.zeros((3 * CH, size2), F32)
+        pick1 = jnp.zeros((LANES, size1), F32)
+        for b in range(3):
+            shift = 3 * a + b
+            lies = (source >= b * CH) & (source < (b + 1) * CH)
+            pick2 = jnp.where(lies & (target == 9 * (source - b * CH) + shift), 1.0, pick2)
+            lies = (source1 >= b * n_wind) & (source1 < (b + 1) * n_wind)
+            pick1 = jnp.where(lies & (target1 == 9 * (source1 - b * n_wind) + shift), 1.0, pick1)
+        pick2, pick1 = pick2.astype(BF16), pick1.astype(BF16)
+        for part in range(3):
+            out2 = out2 + jnp.dot(turned[part][rows], pick2, preferred_element_type=F32)
+            out1 = out1 + jnp.dot(split[part][rows], pick1, preferred_element_type=F32)
+    c2_ref[...] = out2
+    c1_ref[...] = out1
+    b1_ref[...] = across[3 * CH + 3 * n_wind : 3 * CH + 3 * n_wind + 1, CH : 2 * CH]
+    b2_ref[...] = across[3 * CH + 16 : 3 * CH + 17, :CH]
+    for level in range(LEVELS):
+        raw = across[3 * CH + 16 : 3 * CH + 25, (level + 1) * CH : (level + 2) * CH]
+        mean = jnp.sum(raw, axis=0, keepdims=True) / 9.0
+        head_ref[9 * level : 9 * level + 9, :] = CORRECTION * (raw - mean)
 
 
 def lax_wendroff(courant):
@@ -233,7 +363,7 @@
     )
 
 
-def tracer_kernel(levels_ref, wind_ref, corr_ref, main_ref, below_ref, above_ref, out_ref, coef_ref):
+def tracer_kernel(levels_ref, wind_ref, corr_ref, held_ref, side_ref, below_ref, above_ref, out_ref, coef_ref):
     count, tile, cols = out_ref.shape
     for level in range(LEVELS):
         px = lax_wendroff(COURANT * wind_ref[2 * level])
@@ -244,18 +374,24 @@
                 coef = turn(turn(coef, -STEPS[b], 1), HALO - STEPS[a], 0)
                 coef_ref[level, 3 * a + b] = coef[:tile, :cols]
 
-    def step(t, carry):
-        level = levels_ref[t]
-        field = load_field(count + t, main_ref, below_ref, above_ref)
-        total = jnp.zeros((tile, cols), F32)
-        for b in range(3):
-            moved = turn(field, -STEPS[b], 1)
-            for a in range(3):
-                total = total + coef_ref[level, 3 * a + b] * turn(moved, -STEPS[a], 0)[:tile, :cols]
-        out_ref[t] = total.astype(BF16)
-        return carry
-
-    lax.fori_loop(0, count, step, 0, unroll=4)
+    channels = below_ref.shape[0] - 3
+    groups = count // GROUP
+    for group in range(groups):
+        sides = sides_of(groups + group, side_ref, below_ref, above_ref, channels)
+
+        def step(j, carry):
+            t = group * GROUP + j
+            level = levels_ref[t]
+            field = load_field(count + t, held_ref[t], below_ref, above_ref, sides, j)
+            total = jnp.zeros((tile, cols), F32)
+            for b in range(3):
+                moved = turn(field, -STEPS[b], 1)
+                for a in range(3):
+                    total = total + coef_ref[level, 3 * a + b] * turn(moved, -STEPS[a], 0)[:tile, :cols]
+            out_ref[t] = total.astype(BF16)
+            return carry
+
+        lax.fori_loop(0, GROUP, step, 0, unroll=4)
 
 
 def call(kernel, outs, scratch, smem, operands, flops):
@@ -286,15 +422,19 @@
     return up, [(j, i) for i, j in up]
 
 
-def sum_over(value, axis):
-    size = lax.axis_size(axis)
-    if size & (size - 1):
-        return lax.psum(value, axis)
-    step = 1
-    while step < size:
-        value = value + lax.ppermute(value, axis, [(i, i ^ step) for i in range(size)])
-        step *= 2
-    return value
+def sum_rounds(value, axes):
+    other = jnp.zeros_like(value)
+    for axis in axes:
+        size = lax.axis_size(axis)
+        if size & (size - 1):
+            value, other = lax.psum(value + other, axis), jnp.zeros_like(value)
+            continue
+        step = 1
+        while step < size:
+            value = value + other
+            other = lax.ppermute(value, axis, [(i, i ^ step) for i in range(size)])
+            step *= 2
+    return value, other
 
 
 def body(tracers, cotangent, winds, levels, conv1, bias1, conv2, bias2, head):
@@ -304,27 +444,29 @@
     rows = tile + 2 * HALO
     gy, gy_size = lax.axis_index("gy"), lax.axis_size("gy")
     field = jnp.concatenate([tracers, cotangent] + [p.astype(BF16) for p in pieces(winds, 3)], axis=0)
-    head_cols, tail_cols = field[..., :LANES], field[..., cols - LANES :]
-    lane = lax.broadcasted_iota(jnp.int32, (1, 1, LANES), 2)
+    groups = -(-field.shape[0] // GROUP)
+    packed = call(
+        pack_kernel,
+        jax.ShapeDtypeStruct((groups + 1, tile, LANES), BF16),
+        [],
+        0,
+        (tracers, cotangent, winds),
+        200_000,
+    )
     up, down = ring_pairs(gy_size, False)
+    lane = lax.broadcasted_iota(jnp.int32, (1, 1, LANES), 2) % (2 * HALO)
     if gy_size == 2:
-        got = lax.ppermute(jnp.where(gy == 0, tail_cols, head_cols), "gy", up + down)
-        side = jnp.where(jnp.where(gy == 0, lane < HALO, lane >= LANES - HALO), got, 0)
+        got = lax.ppermute(packed, "gy", up + down)
+        side = jnp.where(jnp.where(gy == 0, lane >= HALO, lane < HALO), got, 0)
     else:
-        right = lax.ppermute(head_cols, "gy", down)
-        left = lax.ppermute(tail_cols, "gy", up)
-        side = jnp.where(lane < HALO, right, jnp.where(lane >= LANES - HALO, left, 0))
+        right = lax.ppermute(packed, "gy", down)
+        left = lax.ppermute(packed, "gy", up)
+        side = jnp.where(lane >= HALO, right, left)
     side = side.astype(BF16)
-    main = jnp.concatenate([field, side], axis=2)
+    wide = jnp.concatenate([side[:3], side[3:]], axis=2)
     up, down = ring_pairs(lax.axis_size("gx"), True)
-    above = lax.ppermute(main[:, tile - HALO :], "gx", up)
-    below = lax.ppermute(main[:, :HALO], "gx", down)
-
-    def wind_of(part):
-        split = part[2 * count :].astype(F32)
-        return split[:n_wind] + split[n_wind : 2 * n_wind] + split[2 * n_wind :]
-
-    wind_ext = jnp.concatenate([wind_of(above), wind_of(main), wind_of(below)], axis=1)
+    above = lax.ppermute(jnp.concatenate([field[:, tile - HALO :], wide[:, tile - HALO :]], axis=0), "gx", up)
+    below = lax.ppermute(jnp.concatenate([field[:, :HALO], wide[:, :HALO]], axis=0), "gx", down)
     place = lax.broadcasted_iota(jnp.int32, (1, width), 1)
     has_right, has_left = gy < gy_size - 1, gy > 0
     inside = jnp.where(place < cols, True, jnp.where(place < cols + LANES // 2, has_right, has_left)).astype(F32)
@@ -346,53 +488,68 @@
         jax.ShapeDtypeStruct((9 * LEVELS, rows, width), F32),
         [vmem((3, count, rows, width), F32), vmem((count, rows, width), F32)],
         1,
-        (levels, main, below, above),
+        (levels, tracers, cotangent, side, below, above),
         2_000_000,
     )
     pairs = [(i, i ^ 1) for i in range(lax.axis_size("tracer"))]
     other = lax.ppermute(mine, "tracer", pairs)
-    first, second, corr = call(
+    first, second, corr, wind_ext = call(
         forward_kernel,
         [
             jax.ShapeDtypeStruct((CH, (rows - 2) * width), F32),
             jax.ShapeDtypeStruct((CH, (rows - 4) * width), F32),
             jax.ShapeDtypeStruct((9 * LEVELS, rows, width), F32),
+            jax.ShapeDtypeStruct((n_wind, rows, width), F32),
         ],
         [vmem((16, rows * width), F32)] + [vmem((3 * CH, (rows - 2) * width), BF16)] * 2,
         0,
-        (wind_ext, inside, w1, bias1[:, None], w2, bias2[:, None], head_w),
+        (winds, side, below, above, inside, w1, bias1[:, None], w2, bias2[:, None], head_w),
         2_000_000,
     )
     ring, own = (tile + 4) * width, (tile + 2) * width
-    wind_grad, params = call(
+    params, delta = call(
         backward_kernel,
-        [jax.ShapeDtypeStruct((n_wind, tile, cols), F32), jax.ShapeDtypeStruct((160, LANES), F32)],
+        [jax.ShapeDtypeStruct((3 * CH, LANES), F32), jax.ShapeDtypeStruct((CH, own), F32)],
         [vmem((9 * LEVELS, rows, width), F32), vmem((CH, ring), F32)]
         + [vmem((3 * CH, ring), BF16)] * 2
-        + [vmem((3 * CH, own), BF16)] * 2
-        + [vmem((3 * CH + 16, own), BF16)] * 2
-        + [vmem((3 * CH, own), BF16)] * 4
-        + [vmem((16, own), F32), vmem((n_wind, tile, cols), F32)],
+        + [vmem((3 * CH, own), BF16)] * 6
+        + [vmem((16, own), F32)],
         0,
-        (mine, other, wind_ext, inside, first, second, head_t, w2b, w1b),
+        (mine, other, wind_ext, inside, first, second, head_t, w2b),
         2_000_000,
     )
-    params = sum_over(sum_over(params, "gy"), "gx")
+    params = sum_rounds(params, ("gy", "gx"))
     tracer_grad = call(
         tracer_kernel,
         jax.ShapeDtypeStruct((count, tile, cols), BF16),
         [vmem((LEVELS, 9, tile, cols), F32)],
         1,
-        (levels, wind_ext, corr, main, below, above),
+        (levels, wind_ext, corr, cotangent, side, below, above),
         2_000_000,
     )
-    conv2_grad = params[: 3 * CH, : 3 * CH].reshape(3, CH, 3, CH).transpose(3, 1, 2, 0).reshape(CH, 9 * CH)
-    bias2_grad = params[3 * CH, CH : 2 * CH]
-    low = params[3 * CH + 16 : 3 * CH + 32, : 3 * CH]
-    conv1_grad = low[: 3 * n_wind].reshape(3, n_wind, 3, CH).transpose(3, 1, 2, 0).reshape(CH, 9 * n_wind)
-    bias1_grad = low[3 * n_wind, CH : 2 * CH]
-    head_grad = params[3 * CH + 32 : 3 * CH + 32 + 9 * LEVELS, :CH]
-    return (tracer_grad, wind_grad, conv1_grad, bias1_grad, conv2_grad, bias2_grad, head_grad)
+    wind_grad = call(
+        wind_kernel,
+        jax.ShapeDtypeStruct((n_wind, tile, cols), F32),
+        [vmem((3 * CH, own), BF16)] * 2 + [vmem((n_wind, tile, cols), F32)],
+        0,
+        (mine, other, wind_ext, delta, w1b),
+        2_000_000,
+    )
+    conv1_grad, bias1_grad, conv2_grad, bias2_grad, head_grad = call(
+        final_kernel,
+        [
+            jax.ShapeDtypeStruct(conv1.shape, F32),
+            jax.ShapeDtypeStruct((1, CH), F32),
+            jax.ShapeDtypeStruct(conv2.shape, F32),
+            jax.ShapeDtypeStruct((1, CH), F32),
+            jax.ShapeDtypeStruct(head.shape, F32),
+        ],
+        [],
+        0,
+        params,
+        200_000,
+    )
+    return (tracer_grad, wind_grad, conv1_grad, bias1_grad[0], conv2_grad, bias2_grad[0], head_grad)
 
 
 def solution(mesh):

time: 53.7 us -> 48.4 us (0.901)
  waiting for transfers between devices: 19.6 us -> 11.4 us
  Pallas kernels: 13.2 us -> 16.2 us
    ppermute x6, waiting for transfers between devices: 19.6 us -> 11.4 us  [the longest x3 5.97 us: sum_rounds(): other = lax.ppermute(value, axis, [(i, i ^ step) for i in range(size)])]
    pallas_call x4 -> x7, Pallas kernels: 13.2 us -> 16.2 us  [call(): pl.pallas_call(kernel, out_shape=outs, in_specs=specs, out_specs=[whole]...]
    unnamed x22 -> x28, local copies, waits for them, and re-layouts: 6.06 us -> 7.75 us
    squeeze x1 -> x0, local copies, waits for them, and re-layouts: 0.59 us -> none  [body(): bias2_grad = params[3 * CH, CH:2 * CH]]
  transfers between devices with their start and end apart: 7 -> 7, of which waited for: 5 -> 4; matrix products, arithmetic and copies ran while one was open for 3% -> 4% of each run, Pallas kernels for 11% -> 17%
where the time goes in v2:
time: 48.4 us; the launch traced here: 48 us
  Pallas kernels  16.2 us (33%)
  waiting for transfers between devices  11.4 us (24%)
  starting transfers between devices  9.98 us (21%)
  local copies, waits for them, and re-layouts  8.93 us (18%)
  between operations  0.95 us (2%)
  other arithmetic  0.55 us (1%)
    pallas_call x7, Pallas kernels, call(): pl.pallas_call(kernel, out_shape=outs, in_specs=specs, out_specs=[whole]...  16.2 us
    unnamed x28, local copies, waits for them, and re-layouts  7.75 us
    ppermute x3, waiting for transfers between devices, sum_rounds(): other = lax.ppermute(value, axis, [(i, i ^ step) for i in range(size)])  5.97 us
    ppermute x1, starting transfers between devices, body(): lax.ppermute(jnp.concatenate([field[:, :HALO], wide[:, :HALO]], axis=0),...  3.65 us
    ppermute x3, starting transfers between devices, sum_rounds(): other = lax.ppermute(value, axis, [(i, i ^ step) for i in range(size)])  3.19 us
    ppermute x1, starting transfers between devices, body(): got = lax.ppermute(packed, 'gy', up + down)  3 us
    ppermute x1, waiting for transfers between devices, body(): lax.ppermute(jnp.concatenate([field[:, tile - HALO:], wide[:, tile - HALO...  2.9 us
    ppermute x1, waiting for transfers between devices, body(): lax.ppermute(jnp.concatenate([field[:, :HALO], wide[:, :HALO]], axis=0),...  2.5 us
  transfers between devices with their start and end apart: 7, of which 4 were waited for; matrix products, arithmetic and copies ran while one was open for 4% of the time, Pallas kernels for 17%

profile of v2, /device:TPU:0, one launch (start us, length us, event | category | flops | bytes accessed | tf_op | source)
XLA Modules:
  0.0 48.0 jit_solution(6439134314348470734)
XLA Ops:
  0.6 0.0 copy-start
  0.6 0.9 %copy-done = bf16[32,8,256]{2,1,0:T(8,128)(2,1)S(1)} copy-done((bf16[32,8,256]{2,1,0:T(8,128)(2,1)S(1)}, bf16[32,8,256]{2,1,0:T(8,128)(2,1)}, u32[]{:S(2)}) %copy-start) | copy-done | bytes 131096
  1.5 0.0 copy-start.2
  1.5 0.9 %copy-done.2 = bf16[32,8,256]{2,1,0:T(8,128)(2,1)S(1)} copy-done((bf16[32,8,256]{2,1,0:T(8,128)(2,1)S(1)}, bf16[32,8,256]{2,1,0:T(8,128)(2,1)}, u32[]{:S(2)}) %copy-start.2) | copy-done | bytes 131096
  2.4 0.0 copy-start.4
  2.4 0.8 %copy-done.4 = f32[4,8,256]{2,1,0:T(8,128)S(1)} copy-done((f32[4,8,256]{2,1,0:T(8,128)S(1)}, f32[4,8,256]{2,1,0:T(8,128)}, u32[]{:S(2)}) %copy-start.4) | copy-done | bytes 32792
  3.2 0.1 shard_map.144
  3.3 3.0 %collective-permute-start = (bf16[6,8,128]{2,1,0:T(8,128)(2,1)S(1)}, bf16[6,8,128]{2,1,0:T(8,128)(2,1)S(1)}, u32[]{:S(2)}, u32[]{:S(2)}) collective-permute-start(bf16[6,8,128]{2,1,0:T(8,128)(2,1)S(1)} %shard_map.144), channel_id=1, source_target_pairs={{0,2},{2,0},{1,3},{3,1},{4,6},{6,4},{5,7},{7,5},{8,10},{10,8},{9,1... | collective-permute-start | bytes 36872 | tf_op jit(solution)/shard_map/ppermute | solution.py:459
  6.3 0.0 copy-start.1
  6.4 0.9 %copy-done.1 = bf16[32,8,256]{2,1,0:T(8,128)(2,1)S(1)} copy-done((bf16[32,8,256]{2,1,0:T(8,128)(2,1)S(1)}, bf16[32,8,256]{2,1,0:T(8,128)(2,1)}, u32[]{:S(2)}) %copy-start.1) | copy-done | bytes 131096
  7.2 0.0 copy-start.5
  7.3 0.7 %copy-done.5 = f32[4,8,256]{2,1,0:T(8,128)S(1)} copy-done((f32[4,8,256]{2,1,0:T(8,128)S(1)}, f32[4,8,256]{2,1,0:T(8,128)}, u32[]{:S(2)}) %copy-start.5) | copy-done | bytes 32792
  8.0 0.0 copy-start.9
  8.0 0.1 fusion.20
  8.2 0.6 %copy-done.9 = f32[32,36]{1,0:T(8,128)S(1)} copy-done((f32[32,36]{1,0:T(8,128)S(1)}, f32[32,36]{1,0:T(8,128)}, u32[]{:S(2)}) %copy-start.9) | copy-done | bytes 4632
  8.7 0.1 copy.48
  8.9 0.0 copy-start.8
  8.9 0.8 %copy-done.8 = f32[32,288]{1,0:T(8,128)S(1)} copy-done((f32[32,288]{1,0:T(8,128)S(1)}, f32[32,288]{1,0:T(8,128)}, u32[]{:S(2)}) %copy-start.8) | copy-done | bytes 36888
  9.7 0.1 copy.50
  9.8 0.1 reshape.92
  9.8 0.1 copy.51
  10.0 0.1 reshape.93
  10.1 0.0 copy-start.7
  10.1 0.7 %copy-done.7 = f32[18,32]{1,0:T(8,128)S(1)} copy-done((f32[18,32]{1,0:T(8,128)S(1)}, f32[18,32]{1,0:T(8,128)}, u32[]{:S(2)}) %copy-start.7) | copy-done | bytes 2328
  10.9 0.1 copy.52
  11.0 0.1 pad_maximum_fusion.6
  11.1 0.0 collective-permute-done
  11.2 0.1 pad_maximum_fusion.1
  11.3 3.7 %collective-permute-start.1 = (bf16[79,4,256]{2,1,0:T(4,128)(2,1)S(1)}, bf16[79,4,256]{2,1,0:T(4,128)(2,1)S(1)}, u32[]{:S(2)}, u32[]{:S(2)}) collective-permute-start(bf16[79,4,256]{2,1,0:T(4,128)(2,1)S(1)} %pad_maximum_fusion.1), channel_id=1, source_target_pairs={{4,0},{8,4},{12,8},{0,12},{5,1},{9,5},{13,9},{1,13},{6,2},{10,6},{... | collective-permute-start | bytes 485384 | tf_op jit(solution)/shard_map/ppermute | solution.py:469
  14.9 0.1 fusion
  15.0 0.1 collective-permute-start.2
  15.1 0.1 pad_maximum_fusion.7
  15.2 0.1 copy.53.w1_ref
  15.3 0.0 copy-start.10
  15.3 0.6 %copy-done.10 = f32[32]{0:T(128)S(1)} copy-done((f32[32]{0:T(128)S(1)}, f32[32]{0:T(128)}, u32[]{:S(2)}) %copy-start.10) | copy-done | bytes 152
  15.9 0.1 copy.54.b1_ref
  16.0 0.0 copy-start.11
  16.0 0.7 %copy-done.11 = f32[32]{0:T(128)S(1)} copy-done((f32[32]{0:T(128)S(1)}, f32[32]{0:T(128)}, u32[]{:S(2)}) %copy-start.11) | copy-done | bytes 152
  16.7 0.1 copy.55.b2_ref
  16.8 0.1 copy.56.head_ref
  16.9 0.0 copy-start.3
  16.9 0.1 reshape.97
  17.0 0.0 copy-start.6
  17.0 2.5 %collective-permute-done.1.below_ref = bf16[79,4,256]{2,1,0:T(4,128)(2,1)S(1)} collective-permute-done((bf16[79,4,256]{2,1,0:T(4,128)(2,1)S(1)}, bf16[79,4,256]{2,1,0:T(4,128)(2,1)S(1)}, u32[]{:S(2)}, u32[]{:S(2)}) %collective-permute-start.1) | collective-permute-done | bytes 161824 | tf_op jit(solution)/shard_map/ppermute | solution.py:469
  19.5 2.9 %collective-permute-done.2.above_ref = bf16[79,4,256]{2,1,0:T(4,128)(2,1)S(1)} collective-permute-done((bf16[79,4,256]{2,1,0:T(4,128)(2,1)S(1)}, bf16[79,4,256]{2,1,0:T(4,128)(2,1)S(1)}, u32[]{:S(2)}, u32[]{:S(2)}) %collective-permute-start.2) | collective-permute-done | bytes 161824 | tf_op jit(solution)/shard_map/ppermute | solution.py:468
  22.4 0.0 copy-done.3
  22.4 0.0 copy-done.6
  22.4 3.4 %shard_map.147.mine_ref = f32[18,16,384]{2,1,0:T(8,128)S(1)} custom-call(s32[32]{0:T(128)S(1)} %copy-done.6, bf16[32,8,256]{2,1,0:T(8,128)(2,1)S(1)} %copy-done.3, bf16[32,8,256]{2,1,0:T(8,128)(2,1)S(1)} %copy-done.1, bf16[6,8,128]{2,1,0:T(8,128)(2,1)S(1)} %broadcast_select_fusion.side_ref, bf16[79,4,256]{2,1,0:T(4,128)(2,1)S(1)} %collective-permute-done.1.below_ref, ...), custom_call_target="tpu_custom_call" | custom-call | flops 2000000 | bytes 2000000 | tf_op jit(solution)/shard_map/pallas_call | solution.py:400
  25.8 0.1 collective-permute-start.3
  26.0 3.9 %shard_map.145 = (f32[32,5376]{1,0:T(8,128)S(1)}, f32[32,4608]{1,0:T(8,128)S(1)}, f32[18,16,384]{2,1,0:T(8,128)S(1)}, f32[4,16,384]{2,1,0:T(8,128)S(1)}) custom-call(f32[4,8,256]{2,1,0:T(8,128)S(1)} %copy-done.5, bf16[6,8,128]{2,1,0:T(8,128)(2,1)S(1)} %broadcast_select_fusion.side_ref, bf16[79,4,256]{2,1,0:T(4,128)(2,1)S(1)} %collective-permute-done.1.below_ref, ...), custom_call_target="tpu_custom_call" | custom-call | flops 2000000 | bytes 2000000 | tf_op jit(solution)/shard_map/pallas_call | solution.py:400
  29.9 0.0 collective-permute-done.3.other_ref
  29.9 3.7 %shard_map.148 = (f32[96,128]{1,0:T(8,128)S(1)}, f32[32,3840]{1,0:T(8,128)S(1)}) custom-call(f32[18,16,384]{2,1,0:T(8,128)S(1)} %shard_map.147.mine_ref, f32[18,16,384]{2,1,0:T(8,128)S(1)} %collective-permute-done.3.other_ref, f32[4,16,384]{2,1,0:T(8,128)S(1)} %get-tuple-element.18.wind_ref, f32[1,384]{1,0:T(1,128)S(1)} %select_convert_fusion.inside_ref, ...), custom_call_target="tpu_custom_call" | custom-call | flops 2000000 | bytes 2000000 | tf_op jit(solution)/shard_map/pallas_call | solution.py:400
  33.5 0.6 %collective-permute-start.4 = (f32[96,128]{1,0:T(8,128)S(1)}, f32[96,128]{1,0:T(8,128)S(1)}, u32[]{:S(2)}, u32[]{:S(2)}) collective-permute-start(f32[96,128]{1,0:T(8,128)S(1)} %get-tuple-element.23), channel_id=1, source_target_pairs={{0,2},{2,0},{1,3},{3,1},{4,6},{6,4},{5,7},{7,5},{8,10},{10,8},{9,1... | collective-permute-start | bytes 147464 | tf_op jit(solution)/shard_map/ppermute | solution.py:435
  34.1 0.1 reshape.98
  34.2 3.5 %collective-permute-done.4 = f32[96,128]{1,0:T(8,128)S(1)} collective-permute-done((f32[96,128]{1,0:T(8,128)S(1)}, f32[96,128]{1,0:T(8,128)S(1)}, u32[]{:S(2)}, u32[]{:S(2)}) %collective-permute-start.4) | collective-permute-done | bytes 49184 | tf_op jit(solution)/shard_map/ppermute | solution.py:435
  37.7 1.7 %collective-permute-start.5 = (f32[96,128]{1,0:T(8,128)S(1)}, f32[96,128]{1,0:T(8,128)S(1)}, u32[]{:S(2)}, u32[]{:S(2)}) collective-permute-start(f32[96,128]{1,0:T(8,128)S(1)} %add.28), channel_id=1, source_target_pairs={{0,4},{4,0},{8,12},{12,8},{1,5},{5,1},{9,13},{13,9},{2,6},{6,2},{1... | collective-permute-start | bytes 147464 | tf_op jit(solution)/shard_map/ppermute | solution.py:435
  39.4 2.5 %collective-permute-done.5 = f32[96,128]{1,0:T(8,128)S(1)} collective-permute-done((f32[96,128]{1,0:T(8,128)S(1)}, f32[96,128]{1,0:T(8,128)S(1)}, u32[]{:S(2)}, u32[]{:S(2)}) %collective-permute-start.5) | collective-permute-done | bytes 49184 | tf_op jit(solution)/shard_map/ppermute | solution.py:435
  41.9 0.9 %collective-permute-start.6 = (f32[96,128]{1,0:T(8,128)S(1)}, f32[96,128]{1,0:T(8,128)S(1)}, u32[]{:S(2)}, u32[]{:S(2)}) collective-permute-start(f32[96,128]{1,0:T(8,128)S(1)} %add.29.mine_ref), channel_id=1, source_target_pairs={{0,8},{4,12},{8,0},{12,4},{1,9},{5,13},{9,1},{13,5},{2,10},{6,14},... | collective-permute-start | bytes 147464 | tf_op jit(solution)/shard_map/ppermute | solution.py:435
  42.8 2.7 %shard_map.146 = bf16[32,8,256]{2,1,0:T(8,128)(2,1)} custom-call(s32[32]{0:T(128)S(1)} %copy-done.6, f32[4,16,384]{2,1,0:T(8,128)S(1)} %get-tuple-element.18.wind_ref, f32[18,16,384]{2,1,0:T(8,128)S(1)} %get-tuple-element.19.corr_ref, bf16[32,8,256]{2,1,0:T(8,128)(2,1)S(1)} %copy-done.1, bf16[6,8,128]{2,1,0:T(8,128)(2,1)S(1)} %broadcast_select_fusion.side_ref, ...), custom_call_target="tpu_custom_call" | custom-call | flops 2000000 | bytes 2000000 | tf_op jit(solution)/shard_map/pallas_call | solution.py:400
  45.5 1.4 %shard_map.149 = f32[4,8,256]{2,1,0:T(8,128)} custom-call(f32[18,16,384]{2,1,0:T(8,128)S(1)} %shard_map.147.mine_ref, f32[18,16,384]{2,1,0:T(8,128)S(1)} %collective-permute-done.3.other_ref, f32[4,16,384]{2,1,0:T(8,128)S(1)} %get-tuple-element.18.wind_ref, f32[32,3840]{1,0:T(8,128)S(1)} %get-tuple-element.22.d1_ref, ...), custom_call_target="tpu_custom_call" | custom-call | flops 2000000 | bytes 2000000 | tf_op jit(solution)/shard_map/pallas_call | solution.py:400
  47.0 0.0 collective-permute-done.6.other_ref
  47.0 1.0 %shard_map.150 = (f32[32,36]{1,0:T(8,128)}, f32[1,32]{1,0:T(1,128)}, f32[32,288]{1,0:T(8,128)}, f32[1,32]{1,0:T(1,128)}, f32[18,32]{1,0:T(8,128)}) custom-call(f32[96,128]{1,0:T(8,128)S(1)} %add.29.mine_ref, f32[96,128]{1,0:T(8,128)S(1)} %collective-permute-done.6.other_ref), custom_call_target="tpu_custom_call" | custom-call | flops 200000 | bytes 2000000 | tf_op jit(solution)/shard_map/pallas_call | solution.py:400
  (33 shorter events, 0.3 us)
Async XLA Ops:
  0.6 0.9 %copy-start = (bf16[32,8,256]{2,1,0:T(8,128)(2,1)S(1)}, bf16[32,8,256]{2,1,0:T(8,128)(2,1)}, u32[]{:S(2)}) copy-start(bf16[32,8,256]{2,1,0:T(8,128)(2,1)} %cot_ref.3) | copy-start | bytes 393220
  1.5 0.9 %copy-start.2 = (bf16[32,8,256]{2,1,0:T(8,128)(2,1)S(1)}, bf16[32,8,256]{2,1,0:T(8,128)(2,1)}, u32[]{:S(2)}) copy-start(bf16[32,8,256]{2,1,0:T(8,128)(2,1)} %tracer_ref.3) | copy-start | bytes 393220
  2.4 0.8 %copy-start.4 = (f32[4,8,256]{2,1,0:T(8,128)S(1)}, f32[4,8,256]{2,1,0:T(8,128)}, u32[]{:S(2)}) copy-start(f32[4,8,256]{2,1,0:T(8,128)} %own_ref.1) | copy-start | bytes 98308
  3.3 7.8 %collective-permute-start = (bf16[6,8,128]{2,1,0:T(8,128)(2,1)S(1)}, bf16[6,8,128]{2,1,0:T(8,128)(2,1)S(1)}, u32[]{:S(2)}, u32[]{:S(2)}) collective-permute-start(bf16[6,8,128]{2,1,0:T(8,128)(2,1)S(1)} %shard_map.144), channel_id=1, source_target_pairs={{0,2},{2,0},{1,3},{3,1},{4,6},{6,4},{5,7},{7,5},{8,10},{10,8},{9,1... | collective-permute-start | bytes 36872 | tf_op jit(solution)/shard_map/ppermute | solution.py:459
  6.3 0.9 %copy-start.1 = (bf16[32,8,256]{2,1,0:T(8,128)(2,1)S(1)}, bf16[32,8,256]{2,1,0:T(8,128)(2,1)}, u32[]{:S(2)}) copy-start(bf16[32,8,256]{2,1,0:T(8,128)(2,1)} %cot_ref.3) | copy-start | bytes 393220
  7.2 0.8 %copy-start.5 = (f32[4,8,256]{2,1,0:T(8,128)S(1)}, f32[4,8,256]{2,1,0:T(8,128)}, u32[]{:S(2)}) copy-start(f32[4,8,256]{2,1,0:T(8,128)} %own_ref.1) | copy-start | bytes 98308
  8.0 0.7 %copy-start.9 = (f32[32,36]{1,0:T(8,128)S(1)}, f32[32,36]{1,0:T(8,128)}, u32[]{:S(2)}) copy-start(f32[32,36]{1,0:T(8,128)} %param.13) | copy-start | bytes 13828
  8.9 0.8 %copy-start.8 = (f32[32,288]{1,0:T(8,128)S(1)}, f32[32,288]{1,0:T(8,128)}, u32[]{:S(2)}) copy-start(f32[32,288]{1,0:T(8,128)} %param.15) | copy-start | bytes 110596
  10.1 0.7 %copy-start.7 = (f32[18,32]{1,0:T(8,128)S(1)}, f32[18,32]{1,0:T(8,128)}, u32[]{:S(2)}) copy-start(f32[18,32]{1,0:T(8,128)} %param.17) | copy-start | bytes 6916
  11.3 8.3 %collective-permute-start.1 = (bf16[79,4,256]{2,1,0:T(4,128)(2,1)S(1)}, bf16[79,4,256]{2,1,0:T(4,128)(2,1)S(1)}, u32[]{:S(2)}, u32[]{:S(2)}) collective-permute-start(bf16[79,4,256]{2,1,0:T(4,128)(2,1)S(1)} %pad_maximum_fusion.1), channel_id=1, source_target_pairs={{4,0},{8,4},{12,8},{0,12},{5,1},{9,5},{13,9},{1,13},{6,2},{10,6},{... | collective-permute-start | bytes 485384 | tf_op jit(solution)/shard_map/ppermute | solution.py:469
  15.0 7.4 %collective-permute-start.2 = (bf16[79,4,256]{2,1,0:T(4,128)(2,1)S(1)}, bf16[79,4,256]{2,1,0:T(4,128)(2,1)S(1)}, u32[]{:S(2)}, u32[]{:S(2)}) collective-permute-start(bf16[79,4,256]{2,1,0:T(4,128)(2,1)S(1)} %fusion), channel_id=1, source_target_pairs={{0,4},{4,8},{8,12},{12,0},{1,5},{5,9},{9,13},{13,1},{2,6},{6,10},{... | collective-permute-start | bytes 485384 | tf_op jit(solution)/shard_map/ppermute | solution.py:468
  15.3 0.7 %copy-start.10 = (f32[32]{0:T(128)S(1)}, f32[32]{0:T(128)}, u32[]{:S(2)}) copy-start(f32[32]{0:T(128)} %param.14) | copy-start | bytes 388
  16.0 0.7 %copy-start.11 = (f32[32]{0:T(128)S(1)}, f32[32]{0:T(128)}, u32[]{:S(2)}) copy-start(f32[32]{0:T(128)} %param.16) | copy-start | bytes 388
  16.9 5.6 %copy-start.3 = (bf16[32,8,256]{2,1,0:T(8,128)(2,1)S(1)}, bf16[32,8,256]{2,1,0:T(8,128)(2,1)}, u32[]{:S(2)}) copy-start(bf16[32,8,256]{2,1,0:T(8,128)(2,1)} %tracer_ref.3) | copy-start | bytes 393220
  17.0 5.4 %copy-start.6 = (s32[32]{0:T(128)S(1)}, s32[32]{0:T(128)}, u32[]{:S(2)}) copy-start(s32[32]{0:T(128)} %levels_ref.3) | copy-start | bytes 388
  25.8 4.0 %collective-permute-start.3 = (f32[18,16,384]{2,1,0:T(8,128)S(1)}, f32[18,16,384]{2,1,0:T(8,128)S(1)}, u32[]{:S(2)}, u32[]{:S(2)}) collective-permute-start(f32[18,16,384]{2,1,0:T(8,128)S(1)} %shard_map.147.mine_ref), channel_id=1, source_target_pairs={{0,1},{1,0},{2,3},{3,2},{4,5},{5,4},{6,7},{7,6},{8,9},{9,8},{10,11... | collective-permute-start | bytes 1327112 | tf_op jit(solution)/shard_map/ppermute | solution.py:495
  33.5 4.2 %collective-permute-start.4 = (f32[96,128]{1,0:T(8,128)S(1)}, f32[96,128]{1,0:T(8,128)S(1)}, u32[]{:S(2)}, u32[]{:S(2)}) collective-permute-start(f32[96,128]{1,0:T(8,128)S(1)} %get-tuple-element.23), channel_id=1, source_target_pairs={{0,2},{2,0},{1,3},{3,1},{4,6},{6,4},{5,7},{7,5},{8,10},{10,8},{9,1... | collective-permute-start | bytes 147464 | tf_op jit(solution)/shard_map/ppermute | solution.py:435
  37.7 4.2 %collective-permute-start.5 = (f32[96,128]{1,0:T(8,128)S(1)}, f32[96,128]{1,0:T(8,128)S(1)}, u32[]{:S(2)}, u32[]{:S(2)}) collective-permute-start(f32[96,128]{1,0:T(8,128)S(1)} %add.28), channel_id=1, source_target_pairs={{0,4},{4,0},{8,12},{12,8},{1,5},{5,1},{9,13},{13,9},{2,6},{6,2},{1... | collective-permute-start | bytes 147464 | tf_op jit(solution)/shard_map/ppermute | solution.py:435
  41.9 5.0 %collective-permute-start.6 = (f32[96,128]{1,0:T(8,128)S(1)}, f32[96,128]{1,0:T(8,128)S(1)}, u32[]{:S(2)}, u32[]{:S(2)}) collective-permute-start(f32[96,128]{1,0:T(8,128)S(1)} %add.29.mine_ref), channel_id=1, source_target_pairs={{0,8},{4,12},{8,0},{12,4},{1,9},{5,13},{9,1},{13,5},{2,10},{6,14},... | collective-permute-start | bytes 147464 | tf_op jit(solution)/shard_map/ppermute | solution.py:435

commit v3 on v2

--- a/solution.py
+++ b/solution.py
@@ -62,8 +62,9 @@
 
 
 def sides_of(group, side_ref, below_ref, above_ref, channels):
-    index = channels + group % 3
-    where = slice(group // 3 * LANES, (group // 3 + 1) * LANES)
+    half = side_ref.shape[0] // 2
+    index = channels + group % half
+    where = slice(group // half * LANES, (group // half + 1) * LANES)
     return side_ref[group].astype(F32), rows_of(below_ref[index, :, where], above_ref[index, :, where])
 
 
@@ -77,9 +78,23 @@
     return jnp.concatenate([top, strip], axis=0)
 
 
-def pack_kernel(tracer_ref, cot_ref, wind_ref, out_ref):
-    count = tracer_ref.shape[0]
-    cols = tracer_ref.shape[2]
+def run_copies(sources, targets, sems):
+    copies = [pltpu.make_async_copy(a, b, sems.at[i]) for i, (a, b) in enumerate(zip(sources, targets))]
+    for copy in copies:
+        copy.start()
+    for copy in copies:
+        copy.wait()
+
+
+def pack_kernel(tracer_hbm, cot_hbm, wind_hbm, out_ref, tracer_ref, cot_ref, wind_ref, sems):
+    cols = tracer_hbm.shape[2]
+    hbm = (tracer_hbm, cot_hbm, wind_hbm)
+    refs = (tracer_ref, cot_ref, wind_ref)
+    run_copies(
+        [ref.at[:, :, where] for ref in hbm for where in (slice(0, LANES), slice(cols - LANES, cols))],
+        [ref.at[part] for ref in refs for part in range(2)],
+        sems,
+    )
     lane = lax.broadcasted_iota(jnp.int32, (1, LANES), 1)
     mask = side_mask()
 
@@ -87,64 +102,141 @@
         both = jnp.where(lane < HALO, head, tail)
         return pltpu.roll(jnp.where(mask, both, 0.0), HALO + 2 * HALO * j, 1)
 
-    group = 0
-    for ref in (tracer_ref, cot_ref):
-        for start in range(0, count, GROUP):
+    groups = tracer_ref.shape[1] // GROUP
+    for group, ref in ((0, tracer_ref), (groups + 1, cot_ref)):
+        for start in range(0, ref.shape[1], GROUP):
             total = jnp.zeros(out_ref.shape[1:], F32)
             for j in range(GROUP):
-                head = ref[start + j, :, :LANES].astype(F32)
-                tail = ref[start + j, :, cols - LANES :].astype(F32)
-                total = total + lifted(head, tail, j)
+                total = total + lifted(ref[0, start + j].astype(F32), ref[1, start + j].astype(F32), j)
             out_ref[group] = total.astype(BF16)
             group += 1
     total = jnp.zeros(out_ref.shape[1:], F32)
-    for i in range(wind_ref.shape[0]):
-        head, tail = wind_ref[i, :, :LANES], wind_ref[i, :, cols - LANES :]
+    count = wind_ref.shape[1]
+    for i in range(count):
+        head, tail = wind_ref[0, i], wind_ref[1, i]
         for part in range(3):
             high_head, high_tail = head.astype(BF16).astype(F32), tail.astype(BF16).astype(F32)
-            total = total + lifted(high_head, high_tail, part * wind_ref.shape[0] + i)
+            total = total + lifted(high_head, high_tail, part * count + i)
             head, tail = head - high_head, tail - high_tail
-    out_ref[group] = total.astype(BF16)
-    out_ref[group + 1] = jnp.zeros(out_ref.shape[1:], BF16)
-
-
-def grad_kernel(levels_ref, tracer_ref, cot_ref, side_ref, below_ref, above_ref, out_ref, moved_ref, held_ref):
+    out_ref[groups] = total.astype(BF16)
+    out_ref[2 * groups + 1] = jnp.zeros(out_ref.shape[1:], BF16)
+
+
+def picker(shape, source_axis, wanted):
+    source = lax.broadcasted_iota(jnp.int32, shape, source_axis)
+    target = lax.broadcasted_iota(jnp.int32, shape, 1 - source_axis)
+    return jnp.where(source == wanted(target), 1.0, 0.0).astype(BF16)
+
+
+def prep_kernel(
+    c1_hbm, b1_hbm, c2_hbm, b2_hbm, head_hbm,
+    w1_ref, w2_ref, w2b_ref, w1b_ref, hw_ref, ht_ref, b1_ref, b2_ref,
+    c1, b1, c2, b2, head, wide_ref, slim_ref, tall_ref, sems,
+):
+    run_copies((c1_hbm, b1_hbm, c2_hbm, b2_hbm, head_hbm), (c1, b1, c2, b2, head), sems)
+    n_wind = c1.shape[1] // 9
+
+    def wanted2(target):
+        return 9 * (target & (CH - 1)) + (target >> 5)
+
+    def wanted1(target):
+        a, r = target >> 4, target & 15
+        b = (r >= n_wind).astype(jnp.int32) + (r >= 2 * n_wind).astype(jnp.int32)
+        return jnp.where(r < 3 * n_wind, 9 * (r - n_wind * b) + 3 * a + b, -1)
+
+    both2 = jnp.concatenate(halves(c2[...]), axis=0)
+    size = both2.shape[1]
+    w2_ref[...] = jnp.dot(both2, picker((size, size), 0, wanted2), preferred_element_type=F32).astype(BF16)
+    turned = lax.dot_general(picker((size, size), 1, wanted2), both2, NT, preferred_element_type=F32)
+    both1 = jnp.concatenate(halves(c1[...]), axis=0)
+    size = both1.shape[1]
+    w1_ref[...] = jnp.dot(both1, picker((size, 48), 0, wanted1), preferred_element_type=F32).astype(BF16)
+    turned1 = lax.dot_general(picker((48, size), 1, wanted1), both1, NT, preferred_element_type=F32)
+    slim_ref[...] = jnp.zeros(slim_ref.shape, F32)
+    for q in range(9):
+        where = slice(q * CH, (q + 1) * CH)
+        start = q // 3 * 16 + q % 3 * n_wind
+        for part in range(2):
+            lanes = slice(part * CH, (part + 1) * CH)
+            wide_ref[lanes, where] = turned[where, lanes]
+            slim_ref[16 * part : 16 * part + n_wind, where] = turned1[start : start + n_wind, lanes]
+    w2b_ref[...] = wide_ref[...].astype(BF16)
+    w1b_ref[...] = slim_ref[...].astype(BF16)
+    tall_ref[...] = jnp.zeros(tall_ref.shape, F32)
+    for level in range(LEVELS):
+        rows = slice(9 * level, 9 * level + 9)
+        part = head[rows, :]
+        part = CORRECTION * (part - jnp.sum(part, axis=0, keepdims=True) / 9.0)
+        high = part.astype(BF16).astype(F32)
+        tall_ref[rows, :] = high
+        tall_ref[CH + 9 * level : CH + 9 * level + 9, :] = part - high
+    tall = tall_ref[...].astype(BF16)
+    hw_ref[...] = tall
+    unit = picker((CH, CH), 0, lambda target: target)
+    across = lax.dot_general(unit, tall, NT, preferred_element_type=F32)
+    ht_ref[:CH, :] = across[:, :CH].astype(BF16)
+    ht_ref[CH:, :] = across[:, CH:].astype(BF16)
+    for source, target in ((b1, b1_ref), (b2, b2_ref)):
+        target[...] = jnp.sum(unit.astype(F32) * source[...], axis=1, keepdims=True)
+
+
+def grad_kernel(levels_ref, field_ref, side_ref, below_ref, above_ref, out_ref, moved_ref, held_ref):
     count = levels_ref.shape[0]
+    slots, rows, width = moved_ref.shape[1:]
     channels = below_ref.shape[0] - 3
     groups = count // GROUP
+    lower = jnp.int32(0)
     for group in range(groups):
         near = sides_of(group, side_ref, below_ref, above_ref, channels)
-        far = sides_of(groups + group, side_ref, below_ref, above_ref, channels)
-
-        def fill(j, carry):
+        far = sides_of(groups + 1 + group, side_ref, below_ref, above_ref, channels)
+
+        def fill(j, lower):
             t = group * GROUP + j
-            field = load_field(t, tracer_ref[t], below_ref, above_ref, near, j)
-            for b in range(3):
-                moved_ref[b, t] = turn(field, STEPS[b], 1)
-            held_ref[t] = load_field(count + t, cot_ref[t], below_ref, above_ref, far, j)
-            return carry
-
-        lax.fori_loop(0, GROUP, fill, 0, unroll=4)
-    for a in range(3):
-        for b in range(3):
-
-            def step(t, sums):
-                product = held_ref[t] * turn(moved_ref[b, t], STEPS[a], 0)
-                upper = levels_ref[t].astype(F32)
-                return sums[0] + product, sums[1] + upper * product
-
-            zero = jnp.zeros(out_ref.shape[1:], F32)
-            total, second = lax.fori_loop(0, count, step, (zero, zero), unroll=4)
-            out_ref[3 * a + b] = total - second
-            out_ref[9 + 3 * a + b] = second
+            low = levels_ref[t] == 0
+            slot = jnp.where(low, lower, slots - 1 - t + lower)
+            field = load_field(t, field_ref[t], below_ref, above_ref, near, j)
+            cot = load_field(count + t, field_ref[count + t], below_ref, above_ref, far, j)
+            for step in range(3):
+                moved_ref[step, slot] = turn(field, STEPS[step], 1)
+                held_ref[step, slot] = turn(cot, -STEPS[step], 0)
+            return jnp.where(low, lower + 1, lower)
+
+        lower = lax.fori_loop(0, GROUP, fill, lower, unroll=4)
+    for gap in (0, 1, 2, 5, 6, 7):
+        for step in range(3):
+            moved_ref[step, lower + gap] = jnp.zeros((rows, width), F32)
+            held_ref[step, lower + gap] = jnp.zeros((rows, width), F32)
+    for level in range(LEVELS):
+        trips = lax.shift_right_logical((lower if level == 0 else count - lower) + 3, 2)
+        for start in range(0, width, LANES):
+            lanes = slice(start, start + LANES)
+
+            def step(trip, sums):
+                for part in range(4):
+                    slot = 4 * trip + part
+                    slot = slot if level == 0 else slots - 1 - slot
+                    near = [moved_ref[b, slot, :, lanes] for b in range(3)]
+                    far = [held_ref[a, slot, :, lanes] for a in range(3)]
+                    sums = tuple(sums[k] + far[k // 3] * near[k % 3] for k in range(9))
+                return sums
+
+            sums = lax.fori_loop(0, trips, step, (jnp.zeros((rows, LANES), F32),) * 9)
+            for k in range(9):
+                out_ref[9 * level + k, :, lanes] = turn(sums[k], STEPS[k // 3], 0)
 
 
 def put_moved(high_ref, low_ref, row, value, sign):
     width = value.shape[1]
-    for b in range(3):
-        high, low = halves(turn(value, sign * STEPS[b], 1))
-        high_ref[b * CH : (b + 1) * CH, row * width : (row + 1) * width] = high
-        low_ref[b * CH : (b + 1) * CH, row * width : (row + 1) * width] = low
+    for ref, part in zip((high_ref, low_ref), halves(value)):
+        for b in range(3):
+            ref[b * CH : (b + 1) * CH, row * width : (row + 1) * width] = turn(part, sign * STEPS[b], 1)
+
+
+def convolved(weights, high_ref, low_ref, starts, width):
+    def rows(ref):
+        return jnp.concatenate([ref[:, start * width : (start + 2) * width] for start in starts], axis=0)
+
+    return dot3(weights, rows(high_ref), rows(low_ref))
 
 
 def put_winds(wind_ref, stack_ref, first_row, rows):
@@ -159,12 +251,12 @@
 def forward_kernel(
     own_ref, side_ref, below_ref, above_ref, inside_ref, w1_ref, b1_ref, w2_ref, b2_ref, head_ref,
     first_ref, second_ref, corr_ref, wind_ref,
-    stack_ref, high_ref, low_ref,
+    stack_ref, wind_high, wind_low, high_ref, low_ref,
 ):
     count, rows, width = wind_ref.shape
     tile, cols = own_ref.shape[1:]
     channels = below_ref.shape[0] - 3
-    side, side_rows = sides_of((channels - 3 * count) // GROUP, side_ref, below_ref, above_ref, channels)
+    side, side_rows = sides_of((channels - 3 * count) // (2 * GROUP), side_ref, below_ref, above_ref, channels)
     for i in range(count):
         wind_ref[i, HALO : HALO + tile, :cols] = own_ref[i]
         wide = [jnp.zeros((tile, LANES), F32), jnp.zeros((tile, LANES), F32)]
@@ -181,23 +273,18 @@
             wind_ref[i, :HALO, where] = value[HALO:]
     stack_ref[...] = jnp.zeros(stack_ref.shape, F32)
     put_winds(wind_ref, stack_ref, 0, rows)
+    wind_high[...], wind_low[...] = halves(stack_ref[...])
     bias1, bias2 = b1_ref[...], b2_ref[...]
     inside = jnp.concatenate([inside_ref[...]] * 2, axis=1)
     for row in range(0, rows - 2, 2):
-        total = jnp.zeros((CH, 2 * width), F32) + bias1
-        for a in range(3):
-            high, low = halves(stack_ref[:, (row + a) * width : (row + a + 2) * width])
-            total = total + dot3(w1_ref[a], high, low)
-        value = jnp.tanh(total) * inside
+        starts = (row, row + 1, row + 2)
+        value = jnp.tanh(convolved(w1_ref[...], wind_high, wind_low, starts, width) + bias1) * inside
         first_ref[:, row * width : (row + 2) * width] = value
         for part in range(2):
             put_moved(high_ref, low_ref, row + part, value[:, part * width : (part + 1) * width], 1)
     for row in range(0, rows - 4, 2):
-        total = jnp.zeros((CH, 2 * width), F32) + bias2
-        for a in range(3):
-            where = slice((row + a) * width, (row + a + 2) * width)
-            total = total + dot3(w2_ref[a], high_ref[:, where], low_ref[:, where])
-        value = jnp.tanh(total)
+        starts = (row, row + 1, row + 2)
+        value = jnp.tanh(convolved(w2_ref[...], high_ref, low_ref, starts, width) + bias2)
         second_ref[:, row * width : (row + 2) * width] = value
         high, low = halves(value)
         corr = dot3(head_ref[...], high, low)
@@ -256,11 +343,7 @@
     par_ref[:CH, 3 * CH + 16 : 3 * CH + 17] = jnp.sum(bias2, axis=1, keepdims=True)
     inside2 = jnp.concatenate([inside] * 2, axis=1)
     for row in range(0, tile + 2, 2):
-        total = jnp.zeros((CH, 2 * width), F32)
-        for a in range(3):
-            start = row + 1 - STEPS[a]
-            where = slice(start * width, (start + 2) * width)
-            total = total + dot3(w2b_ref[a], d2_high[:, where], d2_low[:, where])
+        total = convolved(w2b_ref[...], d2_high, d2_low, (row + 2, row + 1, row), width)
         first = first_ref[:, (row + 2) * width : (row + 4) * width]
         delta = total * (1.0 - first * first) * inside2
         d1_ref[:, row * width : (row + 2) * width] = delta
@@ -287,11 +370,7 @@
     for row in range(tile + 2):
         put_moved(d1_high, d1_low, row, d1_ref[:, row * width : (row + 1) * width], -1)
     for row in range(0, tile, 2):
-        total = jnp.zeros((16, 2 * width), F32)
-        for a in range(3):
-            start = row + 1 - STEPS[a]
-            where = slice(start * width, (start + 2) * width)
-            total = total + dot3(w1b_ref[a], d1_high[:, where], d1_low[:, where])
+        total = convolved(w1b_ref[...], d1_high, d1_low, (row + 2, row + 1, row), width)
         for part in range(2):
             net_ref[:, row + part, :] = total[:4, part * width : part * width + cols]
     for level in range(LEVELS):
@@ -363,7 +442,7 @@
     )
 
 
-def tracer_kernel(levels_ref, wind_ref, corr_ref, held_ref, side_ref, below_ref, above_ref, out_ref, coef_ref):
+def tracer_kernel(levels_ref, wind_ref, corr_ref, field_ref, side_ref, below_ref, above_ref, out_ref, coef_ref):
     count, tile, cols = out_ref.shape
     for level in range(LEVELS):
         px = lax_wendroff(COURANT * wind_ref[2 * level])
@@ -377,12 +456,12 @@
     channels = below_ref.shape[0] - 3
     groups = count // GROUP
     for group in range(groups):
-        sides = sides_of(groups + group, side_ref, below_ref, above_ref, channels)
+        sides = sides_of(groups + 1 + group, side_ref, below_ref, above_ref, channels)
 
         def step(j, carry):
             t = group * GROUP + j
             level = levels_ref[t]
-            field = load_field(count + t, held_ref[t], below_ref, above_ref, sides, j)
+            field = load_field(count + t, field_ref[count + t], below_ref, above_ref, sides, j)
             total = jnp.zeros((tile, cols), F32)
             for b in range(3):
                 moved = turn(field, -STEPS[b], 1)
@@ -394,8 +473,8 @@
         lax.fori_loop(0, GROUP, step, 0, unroll=4)
 
 
-def call(kernel, outs, scratch, smem, operands, flops):
-    specs = [pl.BlockSpec(memory_space=pltpu.SMEM if i < smem else pltpu.VMEM) for i in range(len(operands))]
+def call(kernel, outs, scratch, operands, spaces=None, flops=2_000_000, vmem=40):
+    specs = [pl.BlockSpec(memory_space=(spaces or {}).get(i, pltpu.VMEM)) for i in range(len(operands))]
     whole = pl.BlockSpec(memory_space=pltpu.VMEM)
     return pl.pallas_call(
         kernel,
@@ -403,18 +482,9 @@
         in_specs=specs,
         out_specs=[whole] * len(outs) if isinstance(outs, (list, tuple)) else whole,
         scratch_shapes=scratch,
-        compiler_params=pltpu.CompilerParams(vmem_limit_bytes=40 * 1024 * 1024),
+        compiler_params=pltpu.CompilerParams(vmem_limit_bytes=vmem * 1024 * 1024),
         cost_estimate=pl.CostEstimate(flops=flops, bytes_accessed=2_000_000, transcendentals=0),
     )(*operands)
-
-
-def stacked(weights):
-    return jnp.concatenate(pieces(weights, 2), axis=-2).astype(BF16)
-
-
-def pad_to(array, rows, cols):
-    widths = [(0, 0)] * (array.ndim - 2) + [(0, rows - array.shape[-2]), (0, cols - array.shape[-1])]
-    return jnp.pad(array, widths)
 
 
 def ring_pairs(size, wrap):
@@ -422,8 +492,8 @@
     return up, [(j, i) for i, j in up]
 
 
-def sum_rounds(value, axes):
-    other = jnp.zeros_like(value)
+def sum_rounds(value, axes, beside):
+    other, done = jnp.zeros_like(value), []
     for axis in axes:
         size = lax.axis_size(axis)
         if size & (size - 1):
@@ -432,9 +502,13 @@
         step = 1
         while step < size:
             value = value + other
+            if step > 1 or axis != axes[0]:
+                if len(done) < len(beside):
+                    value, made = lax.optimization_barrier((value, beside[len(done)]))
+                    done.append(made)
             other = lax.ppermute(value, axis, [(i, i ^ step) for i in range(size)])
             step *= 2
-    return value, other
+    return value, other, tuple(done) + tuple(beside[len(done) :])
 
 
 def body(tracers, cotangent, winds, levels, conv1, bias1, conv2, bias2, head):
@@ -442,17 +516,45 @@
     n_wind = winds.shape[0]
     width = cols + LANES
     rows = tile + 2 * HALO
+    vmem, spec = pltpu.VMEM, jax.ShapeDtypeStruct
     gy, gy_size = lax.axis_index("gy"), lax.axis_size("gy")
-    field = jnp.concatenate([tracers, cotangent] + [p.astype(BF16) for p in pieces(winds, 3)], axis=0)
-    groups = -(-field.shape[0] // GROUP)
     packed = call(
         pack_kernel,
-        jax.ShapeDtypeStruct((groups + 1, tile, LANES), BF16),
-        [],
-        0,
+        spec((2 * (count // GROUP) + 2, tile, LANES), BF16),
+        [vmem((2, count, tile, LANES), BF16)] * 2
+        + [vmem((2, n_wind, tile, LANES), F32), pltpu.SemaphoreType.DMA((6,))],
         (tracers, cotangent, winds),
+        {i: pltpu.HBM for i in range(3)},
         200_000,
-    )
+        63,
+    )
+    w1, w2, w2b, w1b, head_w, head_t, bias1_col, bias2_col = call(
+        prep_kernel,
+        [
+            spec((2 * CH, 48), BF16),
+            spec((2 * CH, 9 * CH), BF16),
+            spec((2 * CH, 9 * CH), BF16),
+            spec((32, 9 * CH), BF16),
+            spec((2 * CH, CH), BF16),
+            spec((2 * CH, CH), BF16),
+            spec((CH, 1), F32),
+            spec((CH, 1), F32),
+        ],
+        [
+            vmem(conv1.shape, F32),
+            vmem((1, CH), F32),
+            vmem(conv2.shape, F32),
+            vmem((1, CH), F32),
+            vmem(head.shape, F32),
+            vmem((2 * CH, 9 * CH), F32),
+            vmem((32, 9 * CH), F32),
+            vmem((2 * CH, CH), F32),
+            pltpu.SemaphoreType.DMA((5,)),
+        ],
+        (conv1, bias1[None], conv2, bias2[None], head),
+        {i: pltpu.HBM for i in range(5)},
+    )
+    field = jnp.concatenate([tracers, cotangent] + [p.astype(BF16) for p in pieces(winds, 3)], axis=0)
     up, down = ring_pairs(gy_size, False)
     lane = lax.broadcasted_iota(jnp.int32, (1, 1, LANES), 2) % (2 * HALO)
     if gy_size == 2:
@@ -463,7 +565,8 @@
         left = lax.ppermute(packed, "gy", up)
         side = jnp.where(lane >= HALO, right, left)
     side = side.astype(BF16)
-    wide = jnp.concatenate([side[:3], side[3:]], axis=2)
+    half = side.shape[0] // 2
+    wide = jnp.concatenate([side[:half], side[half:]], axis=2)
     up, down = ring_pairs(lax.axis_size("gx"), True)
     above = lax.ppermute(jnp.concatenate([field[:, tile - HALO :], wide[:, tile - HALO :]], axis=0), "gx", up)
     below = lax.ppermute(jnp.concatenate([field[:, :HALO], wide[:, :HALO]], axis=0), "gx", down)
@@ -471,83 +574,58 @@
     has_right, has_left = gy < gy_size - 1, gy > 0
     inside = jnp.where(place < cols, True, jnp.where(place < cols + LANES // 2, has_right, has_left)).astype(F32)
 
-    split1 = conv1.reshape(CH, n_wind, 3, 3)
-    split2 = conv2.reshape(CH, CH, 3, 3)
-    w1 = stacked(pad_to(split1.transpose(2, 0, 3, 1).reshape(3, CH, 3 * n_wind), CH, 16))
-    w2 = stacked(split2.transpose(2, 0, 3, 1).reshape(3, CH, 3 * CH))
-    w2b = stacked(split2.transpose(2, 1, 3, 0).reshape(3, CH, 3 * CH))
-    w1b = stacked(pad_to(split1.transpose(2, 1, 3, 0).reshape(3, n_wind, 3 * CH), 16, 3 * CH))
-    by_level = head.reshape(LEVELS, 9, CH)
-    centred = (CORRECTION * (by_level - jnp.mean(by_level, axis=1, keepdims=True))).reshape(9 * LEVELS, CH)
-    head_w = stacked(pad_to(centred, CH, CH))
-    head_t = stacked(pad_to(centred.T, CH, CH))
-
-    vmem = pltpu.VMEM
+    above, below, w1, w2 = lax.optimization_barrier((above, below, w1, w2))
     mine = call(
         grad_kernel,
-        jax.ShapeDtypeStruct((9 * LEVELS, rows, width), F32),
-        [vmem((3, count, rows, width), F32), vmem((count, rows, width), F32)],
-        1,
-        (levels, tracers, cotangent, side, below, above),
-        2_000_000,
-    )
-    pairs = [(i, i ^ 1) for i in range(lax.axis_size("tracer"))]
-    other = lax.ppermute(mine, "tracer", pairs)
+        spec((9 * LEVELS, rows, width), F32),
+        [vmem((3, count + 8, rows, width), F32)] * 2,
+        (levels, field, side, below, above),
+        {0: pltpu.SMEM},
+    )
+    other = lax.ppermute(mine, "tracer", [(i, i ^ 1) for i in range(lax.axis_size("tracer"))])
     first, second, corr, wind_ext = call(
         forward_kernel,
         [
-            jax.ShapeDtypeStruct((CH, (rows - 2) * width), F32),
-            jax.ShapeDtypeStruct((CH, (rows - 4) * width), F32),
-            jax.ShapeDtypeStruct((9 * LEVELS, rows, width), F32),
-            jax.ShapeDtypeStruct((n_wind, rows, width), F32),
+            spec((CH, (rows - 2) * width), F32),
+            spec((CH, (rows - 4) * width), F32),
+            spec((9 * LEVELS, rows, width), F32),
+            spec((n_wind, rows, width), F32),
         ],
-        [vmem((16, rows * width), F32)] + [vmem((3 * CH, (rows - 2) * width), BF16)] * 2,
-        0,
-        (winds, side, below, above, inside, w1, bias1[:, None], w2, bias2[:, None], head_w),
-        2_000_000,
+        [vmem((16, rows * width), F32)]
+        + [vmem((16, rows * width), BF16)] * 2
+        + [vmem((3 * CH, (rows - 2) * width), BF16)] * 2,
+        (winds, side, below, above, inside, w1, bias1_col, w2, bias2_col, head_w),
     )
     ring, own = (tile + 4) * width, (tile + 2) * width
     params, delta = call(
         backward_kernel,
-        [jax.ShapeDtypeStruct((3 * CH, LANES), F32), jax.ShapeDtypeStruct((CH, own), F32)],
+        [spec((3 * CH, LANES), F32), spec((CH, own), F32)],
         [vmem((9 * LEVELS, rows, width), F32), vmem((CH, ring), F32)]
         + [vmem((3 * CH, ring), BF16)] * 2
         + [vmem((3 * CH, own), BF16)] * 6
         + [vmem((16, own), F32)],
-        0,
         (mine, other, wind_ext, inside, first, second, head_t, w2b),
-        2_000_000,
-    )
-    params = sum_rounds(params, ("gy", "gx"))
+    )
     tracer_grad = call(
         tracer_kernel,
-        jax.ShapeDtypeStruct((count, tile, cols), BF16),
+        spec((count, tile, cols), BF16),
         [vmem((LEVELS, 9, tile, cols), F32)],
-        1,
-        (levels, wind_ext, corr, cotangent, side, below, above),
-        2_000_000,
+        (levels, wind_ext, corr, field, side, below, above),
+        {0: pltpu.SMEM},
     )
     wind_grad = call(
         wind_kernel,
-        jax.ShapeDtypeStruct((n_wind, tile, cols), F32),
+        spec((n_wind, tile, cols), F32),
         [vmem((3 * CH, own), BF16)] * 2 + [vmem((n_wind, tile, cols), F32)],
-        0,
         (mine, other, wind_ext, delta, w1b),
-        2_000_000,
-    )
+    )
+    mine, other, (tracer_grad, wind_grad) = sum_rounds(params, ("gy", "gx"), (tracer_grad, wind_grad))
     conv1_grad, bias1_grad, conv2_grad, bias2_grad, head_grad = call(
         final_kernel,
-        [
-            jax.ShapeDtypeStruct(conv1.shape, F32),
-            jax.ShapeDtypeStruct((1, CH), F32),
-            jax.ShapeDtypeStruct(conv2.shape, F32),
-            jax.ShapeDtypeStruct((1, CH), F32),
-            jax.ShapeDtypeStruct(head.shape, F32),
-        ],
+        [spec(conv1.shape, F32), spec((1, CH), F32), spec(conv2.shape, F32), spec((1, CH), F32), spec(head.shape, F32)],
         [],
-        0,
-        params,
-        200_000,
+        (mine, other),
+        flops=200_000,
     )
     return (tracer_grad, wind_grad, conv1_grad, bias1_grad[0], conv2_grad, bias2_grad[0], head_grad)
 

time: 48.4 us -> 42.5 us (0.88)
  local copies, waits for them, and re-layouts: 8.93 us -> 3.09 us
  starting transfers between devices: 9.98 us -> 11.3 us
  waiting for transfers between devices: 11.4 us -> 10.2 us
    unnamed x28 -> x20, local copies, waits for them, and re-layouts: 7.75 us -> 2.98 us
    ppermute x1, starting transfers between devices: 0.06 us -> 2.16 us  [body(): lax.ppermute(jnp.concatenate([field[:, tile - HALO:], wide[:, tile - HALO...]
    ppermute x1, starting transfers between devices: 3.65 us -> 2.09 us  [body(): lax.ppermute(jnp.concatenate([field[:, :HALO], wide[:, :HALO]], axis=0),...]
    ppermute x1, waiting for transfers between devices: 2.5 us -> 1.17 us  [body(): lax.ppermute(jnp.concatenate([field[:, :HALO], wide[:, :HALO]], axis=0),...]
    ppermute x1, waiting for transfers between devices: 2.9 us -> 3.8 us  [body(): lax.ppermute(jnp.concatenate([field[:, tile - HALO:], wide[:, tile - HALO...]
    ppermute x3, starting transfers between devices: 3.19 us -> 4.02 us  [sum_rounds(): other = lax.ppermute(value, axis, [(i, i ^ step) for i in range(size)])]
    ppermute x3, waiting for transfers between devices: 5.97 us -> 5.16 us  [sum_rounds(): other = lax.ppermute(value, axis, [(i, i ^ step) for i in range(size)])]
    pallas_call x7 -> x8, Pallas kernels: 16.2 us -> 16.6 us  [call(): pl.pallas_call(kernel, out_shape=outs, in_specs=specs, out_specs=[whole]...]
  transfers between devices with their start and end apart: 7 -> 7, of which waited for: 4 -> 6; matrix products, arithmetic and copies ran while one was open for 4% -> 0% of each run, Pallas kernels for 17% -> 18%
where the time goes in v3:
time: 42.5 us; the launch traced here: 42.3 us
  Pallas kernels  16.6 us (39%)
  starting transfers between devices  11.3 us (27%)
  waiting for transfers between devices  10.2 us (24%)
  local copies, waits for them, and re-layouts  3.09 us (7%)
  between operations  0.82 us (2%)
    pallas_call x8, Pallas kernels, call(): pl.pallas_call(kernel, out_shape=outs, in_specs=specs, out_specs=[whole]...  16.6 us
    ppermute x3, waiting for transfers between devices, sum_rounds(): other = lax.ppermute(value, axis, [(i, i ^ step) for i in range(size)])  5.16 us
    ppermute x3, starting transfers between devices, sum_rounds(): other = lax.ppermute(value, axis, [(i, i ^ step) for i in range(size)])  4.02 us
    ppermute x1, waiting for transfers between devices, body(): lax.ppermute(jnp.concatenate([field[:, tile - HALO:], wide[:, tile - HALO...  3.8 us
    ppermute x1, starting transfers between devices, body(): got = lax.ppermute(packed, 'gy', up + down)  3 us
    unnamed x20, local copies, waits for them, and re-layouts  2.98 us
    ppermute x1, starting transfers between devices, body(): lax.ppermute(jnp.concatenate([field[:, tile - HALO:], wide[:, tile - HALO...  2.16 us
    ppermute x1, starting transfers between devices, body(): lax.ppermute(jnp.concatenate([field[:, :HALO], wide[:, :HALO]], axis=0),...  2.09 us
  transfers between devices with their start and end apart: 7, of which 6 were waited for; matrix products, arithmetic and copies ran while one was open for 0% of the time, Pallas kernels for 18%

profile of v3, /device:TPU:0, one launch (start us, length us, event | category | flops | bytes accessed | tf_op | source)
XLA Modules:
  0.0 42.3 jit_solution(8518448616843132794)
XLA Ops:
  0.6 0.0 copy-start.7
  0.6 1.7 %shard_map.144 = bf16[6,8,128]{2,1,0:T(8,128)(2,1)} custom-call(bf16[32,8,256]{2,1,0:T(8,128)(2,1)} %tracer_hbm.1, bf16[32,8,256]{2,1,0:T(8,128)(2,1)} %cot_hbm.1, f32[4,8,256]{2,1,0:T(8,128)} %own_ref.1), custom_call_target="tpu_custom_call" | custom-call | flops 200000 | bytes 2000000 | tf_op jit(solution)/shard_map/pallas_call | solution.py:479
  2.4 3.0 %collective-permute-start = (bf16[6,8,128]{2,1,0:T(8,128)(2,1)}, bf16[6,8,128]{2,1,0:T(8,128)(2,1)S(1)}, u32[]{:S(2)}, u32[]{:S(2)}) collective-permute-start(bf16[6,8,128]{2,1,0:T(8,128)(2,1)} %shard_map.144), channel_id=1, source_target_pairs={{0,2},{2,0},{1,3},{3,1},{4,6},{6,4},{5,7},{7,5},{8,10},{10,8},{9,1... | collective-permute-start | bytes 36872 | tf_op jit(solution)/shard_map/ppermute | solution.py:561
  5.4 0.0 copy-done.7
  5.4 0.0 copy-start.8
  5.4 0.9 %copy-done.8 = bf16[32,8,256]{2,1,0:T(8,128)(2,1)S(1)} copy-done((bf16[32,8,256]{2,1,0:T(8,128)(2,1)S(1)}, bf16[32,8,256]{2,1,0:T(8,128)(2,1)}, u32[]{:S(2)}) %copy-start.8) | copy-done | bytes 131096
  6.3 0.0 copy-start
  6.3 0.7 %copy-done = f32[4,8,256]{2,1,0:T(8,128)S(1)} copy-done((f32[4,8,256]{2,1,0:T(8,128)S(1)}, f32[4,8,256]{2,1,0:T(8,128)}, u32[]{:S(2)}) %copy-start) | copy-done | bytes 32792
  7.1 0.1 fusion.7
  7.2 0.1 collective-permute-done
  7.3 0.1 fusion
  7.4 0.0 copy-start.1
  7.4 0.0 copy-start.2
  7.4 0.0 copy-start.3
  7.4 0.1 pad_maximum_fusion.1
  7.5 2.2 %collective-permute-start.1 = (bf16[79,4,256]{2,1,0:T(4,128)(2,1)S(1)}, bf16[79,4,256]{2,1,0:T(4,128)(2,1)S(1)}, u32[]{:S(2)}, u32[]{:S(2)}) collective-permute-start(bf16[79,4,256]{2,1,0:T(4,128)(2,1)S(1)} %pad_maximum_fusion.1), channel_id=1, source_target_pairs={{0,4},{4,8},{8,12},{12,0},{1,5},{5,9},{9,13},{13,1},{2,6},{6,10},{... | collective-permute-start | bytes 485384 | tf_op jit(solution)/shard_map/ppermute | solution.py:571
  9.7 2.1 %collective-permute-start.2 = (bf16[79,4,256]{2,1,0:T(4,128)(2,1)S(1)}, bf16[79,4,256]{2,1,0:T(4,128)(2,1)S(1)}, u32[]{:S(2)}, u32[]{:S(2)}) collective-permute-start(bf16[79,4,256]{2,1,0:T(4,128)(2,1)S(1)} %fusion), channel_id=1, source_target_pairs={{4,0},{8,4},{12,8},{0,12},{5,1},{9,5},{13,9},{1,13},{6,2},{10,6},{... | collective-permute-start | bytes 485384 | tf_op jit(solution)/shard_map/ppermute | solution.py:572
  11.8 0.0 copy-start.5
  11.8 0.0 copy-start.6
  11.8 0.0 copy-done.1
  11.8 0.0 copy-done.2
  11.8 0.0 copy-done.3
  11.8 0.6 %copy-done.5 = f32[32]{0:T(128)S(1)} copy-done((f32[32]{0:T(128)S(1)}, f32[32]{0:T(128)}, u32[]{:S(2)}) %copy-start.5) | copy-done | bytes 152
  12.5 0.0 copy-done.6
  12.5 0.5 %shard_map.145 = (bf16[64,48]{1,0:T(8,128)(2,1)S(1)}, bf16[64,288]{1,0:T(8,128)(2,1)S(1)}, bf16[64,288]{1,0:T(8,128)(2,1)S(1)}, bf16[32,288]{1,0:T(8,128)(2,1)S(...) custom-call(f32[32,36]{1,0:T(8,128)S(1)} %copy-done.2, ...), custom_call_target="tpu_custom_call" | custom-call | flops 2000000 | bytes 2000000 | tf_op jit(solution)/shard_map/pallas_call | solution.py:479
  13.0 3.8 %collective-permute-done.1.above_ref = bf16[79,4,256]{2,1,0:T(4,128)(2,1)S(1)} collective-permute-done((bf16[79,4,256]{2,1,0:T(4,128)(2,1)S(1)}, bf16[79,4,256]{2,1,0:T(4,128)(2,1)S(1)}, u32[]{:S(2)}, u32[]{:S(2)}) %collective-permute-start.1) | collective-permute-done | bytes 161824 | tf_op jit(solution)/shard_map/ppermute | solution.py:571
  16.8 1.2 %collective-permute-done.2.below_ref = bf16[79,4,256]{2,1,0:T(4,128)(2,1)S(1)} collective-permute-done((bf16[79,4,256]{2,1,0:T(4,128)(2,1)S(1)}, bf16[79,4,256]{2,1,0:T(4,128)(2,1)S(1)}, u32[]{:S(2)}, u32[]{:S(2)}) %collective-permute-start.2) | collective-permute-done | bytes 161824 | tf_op jit(solution)/shard_map/ppermute | solution.py:572
  18.0 0.0 copy-start.4
  18.0 0.7 %copy-done.4 = s32[32]{0:T(128)S(1)} copy-done((s32[32]{0:T(128)S(1)}, s32[32]{0:T(128)}, u32[]{:S(2)}) %copy-start.4) | copy-done | bytes 152
  18.6 2.6 %shard_map.146.mine_ref = f32[18,16,384]{2,1,0:T(8,128)S(1)} custom-call(s32[32]{0:T(128)S(1)} %copy-done.4, bf16[76,8,256]{2,1,0:T(8,128)(2,1)S(1)} %fusion.3.field_ref, bf16[6,8,128]{2,1,0:T(8,128)(2,1)S(1)} %broadcast_select_fusion.side_ref, bf16[79,4,256]{2,1,0:T(4,128)(2,1)S(1)} %collective-permute-done.2.below_ref, ...), custom_call_target="tpu_custom_call" | custom-call | flops 2000000 | bytes 2000000 | tf_op jit(solution)/shard_map/pallas_call | solution.py:479
  21.2 0.1 collective-permute-start.3
  21.3 2.9 %shard_map.147 = (f32[32,5376]{1,0:T(8,128)S(1)}, f32[32,4608]{1,0:T(8,128)S(1)}, f32[18,16,384]{2,1,0:T(8,128)S(1)}, f32[4,16,384]{2,1,0:T(8,128)S(1)}) custom-call(f32[4,8,256]{2,1,0:T(8,128)S(1)} %copy-done, bf16[6,8,128]{2,1,0:T(8,128)(2,1)S(1)} %broadcast_select_fusion.side_ref, bf16[79,4,256]{2,1,0:T(4,128)(2,1)S(1)} %collective-permute-done.2.below_ref, ...), custom_call_target="tpu_custom_call" | custom-call | flops 2000000 | bytes 2000000 | tf_op jit(solution)/shard_map/pallas_call | solution.py:479
  24.2 0.0 collective-permute-done.3.other_ref
  24.2 3.7 %shard_map.148 = (f32[96,128]{1,0:T(8,128)S(1)}, f32[32,3840]{1,0:T(8,128)S(1)}) custom-call(f32[18,16,384]{2,1,0:T(8,128)S(1)} %shard_map.146.mine_ref, f32[18,16,384]{2,1,0:T(8,128)S(1)} %collective-permute-done.3.other_ref, f32[4,16,384]{2,1,0:T(8,128)S(1)} %get-tuple-element.43.wind_ref, f32[1,384]{1,0:T(1,128)S(1)} %select_convert_fusion.inside_ref, ...), custom_call_target="tpu_custom_call" | custom-call | flops 2000000 | bytes 2000000 | tf_op jit(solution)/shard_map/pallas_call | solution.py:479
  27.9 1.2 %collective-permute-start.4 = (f32[96,128]{1,0:T(8,128)S(1)}, f32[96,128]{1,0:T(8,128)S(1)}, u32[]{:S(2)}, u32[]{:S(2)}) collective-permute-start(f32[96,128]{1,0:T(8,128)S(1)} %get-tuple-element.48), channel_id=1, source_target_pairs={{0,2},{2,0},{1,3},{3,1},{4,6},{6,4},{5,7},{7,5},{8,10},{10,8},{9,1... | collective-permute-start | bytes 147464 | tf_op jit(solution)/shard_map/ppermute | solution.py:509
  29.1 2.7 %shard_map.149 = bf16[32,8,256]{2,1,0:T(8,128)(2,1)} custom-call(s32[32]{0:T(128)S(1)} %copy-done.4, f32[4,16,384]{2,1,0:T(8,128)S(1)} %get-tuple-element.43.wind_ref, f32[18,16,384]{2,1,0:T(8,128)S(1)} %get-tuple-element.49.corr_ref, bf16[76,8,256]{2,1,0:T(8,128)(2,1)S(1)} %fusion.3.field_ref, bf16[6,8,128]{2,1,0:T(8,128)(2,1)S(1)} %broadcast_select_fusion.side_ref, ...), custom_call_target="tpu_custom_call" | custom-call | flops 2000000 | bytes 2000000 | tf_op jit(solution)/shard_map/pallas_call | solution.py:479
  31.9 0.2 collective-permute-done.4
  32.1 1.2 %collective-permute-start.5 = (f32[96,128]{1,0:T(8,128)S(1)}, f32[96,128]{1,0:T(8,128)S(1)}, u32[]{:S(2)}, u32[]{:S(2)}) collective-permute-start(f32[96,128]{1,0:T(8,128)S(1)} %add.20), channel_id=1, source_target_pairs={{0,4},{4,0},{8,12},{12,8},{1,5},{5,1},{9,13},{13,9},{2,6},{6,2},{1... | collective-permute-start | bytes 147464 | tf_op jit(solution)/shard_map/ppermute | solution.py:509
  33.3 1.5 %shard_map.150 = f32[4,8,256]{2,1,0:T(8,128)} custom-call(f32[18,16,384]{2,1,0:T(8,128)S(1)} %shard_map.146.mine_ref, f32[18,16,384]{2,1,0:T(8,128)S(1)} %collective-permute-done.3.other_ref, f32[4,16,384]{2,1,0:T(8,128)S(1)} %get-tuple-element.43.wind_ref, f32[32,3840]{1,0:T(8,128)S(1)} %get-tuple-element.52.d1_ref, ...), custom_call_target="tpu_custom_call" | custom-call | flops 2000000 | bytes 2000000 | tf_op jit(solution)/shard_map/pallas_call | solution.py:479
  34.8 1.5 %collective-permute-done.5 = f32[96,128]{1,0:T(8,128)S(1)} collective-permute-done((f32[96,128]{1,0:T(8,128)S(1)}, f32[96,128]{1,0:T(8,128)S(1)}, u32[]{:S(2)}, u32[]{:S(2)}) %collective-permute-start.5) | collective-permute-done | bytes 49184 | tf_op jit(solution)/shard_map/ppermute | solution.py:509
  36.3 1.6 %collective-permute-start.6 = (f32[96,128]{1,0:T(8,128)S(1)}, f32[96,128]{1,0:T(8,128)S(1)}, u32[]{:S(2)}, u32[]{:S(2)}) collective-permute-start(f32[96,128]{1,0:T(8,128)S(1)} %add.21.mine_ref), channel_id=1, source_target_pairs={{0,8},{4,12},{8,0},{12,4},{1,9},{5,13},{9,1},{13,5},{2,10},{6,14},... | collective-permute-start | bytes 147464 | tf_op jit(solution)/shard_map/ppermute | solution.py:509
  37.9 3.5 %collective-permute-done.6.other_ref = f32[96,128]{1,0:T(8,128)S(1)} collective-permute-done((f32[96,128]{1,0:T(8,128)S(1)}, f32[96,128]{1,0:T(8,128)S(1)}, u32[]{:S(2)}, u32[]{:S(2)}) %collective-permute-start.6) | collective-permute-done | bytes 49184 | tf_op jit(solution)/shard_map/ppermute | solution.py:509
  41.3 1.0 %shard_map.151 = (f32[32,36]{1,0:T(8,128)}, f32[1,32]{1,0:T(1,128)}, f32[32,288]{1,0:T(8,128)}, f32[1,32]{1,0:T(1,128)}, f32[18,32]{1,0:T(8,128)}) custom-call(f32[96,128]{1,0:T(8,128)S(1)} %add.21.mine_ref, f32[96,128]{1,0:T(8,128)S(1)} %collective-permute-done.6.other_ref), custom_call_target="tpu_custom_call" | custom-call | flops 200000 | bytes 2000000 | tf_op jit(solution)/shard_map/pallas_call | solution.py:479
  (12 shorter events, 0.1 us)
Async XLA Ops:
  0.6 4.8 %copy-start.7 = (bf16[32,8,256]{2,1,0:T(8,128)(2,1)S(1)}, bf16[32,8,256]{2,1,0:T(8,128)(2,1)}, u32[]{:S(2)}) copy-start(bf16[32,8,256]{2,1,0:T(8,128)(2,1)} %tracer_hbm.1) | copy-start | bytes 393220
  2.4 4.9 %collective-permute-start = (bf16[6,8,128]{2,1,0:T(8,128)(2,1)}, bf16[6,8,128]{2,1,0:T(8,128)(2,1)S(1)}, u32[]{:S(2)}, u32[]{:S(2)}) collective-permute-start(bf16[6,8,128]{2,1,0:T(8,128)(2,1)} %shard_map.144), channel_id=1, source_target_pairs={{0,2},{2,0},{1,3},{3,1},{4,6},{6,4},{5,7},{7,5},{8,10},{10,8},{9,1... | collective-permute-start | bytes 36872 | tf_op jit(solution)/shard_map/ppermute | solution.py:561
  5.4 0.9 %copy-start.8 = (bf16[32,8,256]{2,1,0:T(8,128)(2,1)S(1)}, bf16[32,8,256]{2,1,0:T(8,128)(2,1)}, u32[]{:S(2)}) copy-start(bf16[32,8,256]{2,1,0:T(8,128)(2,1)} %cot_hbm.1) | copy-start | bytes 393220
  6.3 0.8 %copy-start = (f32[4,8,256]{2,1,0:T(8,128)S(1)}, f32[4,8,256]{2,1,0:T(8,128)}, u32[]{:S(2)}) copy-start(f32[4,8,256]{2,1,0:T(8,128)} %own_ref.1) | copy-start | bytes 98308
  7.4 4.4 %copy-start.1 = (f32[32,288]{1,0:T(8,128)S(1)}, f32[32,288]{1,0:T(8,128)}, u32[]{:S(2)}) copy-start(f32[32,288]{1,0:T(8,128)} %c2_hbm.1) | copy-start | bytes 110596
  7.4 4.4 %copy-start.2 = (f32[32,36]{1,0:T(8,128)S(1)}, f32[32,36]{1,0:T(8,128)}, u32[]{:S(2)}) copy-start(f32[32,36]{1,0:T(8,128)} %c1_hbm.1) | copy-start | bytes 13828
  7.4 4.4 %copy-start.3 = (f32[18,32]{1,0:T(8,128)S(1)}, f32[18,32]{1,0:T(8,128)}, u32[]{:S(2)}) copy-start(f32[18,32]{1,0:T(8,128)} %head_hbm.1) | copy-start | bytes 6916
  7.5 9.2 %collective-permute-start.1 = (bf16[79,4,256]{2,1,0:T(4,128)(2,1)S(1)}, bf16[79,4,256]{2,1,0:T(4,128)(2,1)S(1)}, u32[]{:S(2)}, u32[]{:S(2)}) collective-permute-start(bf16[79,4,256]{2,1,0:T(4,128)(2,1)S(1)} %pad_maximum_fusion.1), channel_id=1, source_target_pairs={{0,4},{4,8},{8,12},{12,0},{1,5},{5,9},{9,13},{13,1},{2,6},{6,10},{... | collective-permute-start | bytes 485384 | tf_op jit(solution)/shard_map/ppermute | solution.py:571
  9.7 8.2 %collective-permute-start.2 = (bf16[79,4,256]{2,1,0:T(4,128)(2,1)S(1)}, bf16[79,4,256]{2,1,0:T(4,128)(2,1)S(1)}, u32[]{:S(2)}, u32[]{:S(2)}) collective-permute-start(bf16[79,4,256]{2,1,0:T(4,128)(2,1)S(1)} %fusion), channel_id=1, source_target_pairs={{4,0},{8,4},{12,8},{0,12},{5,1},{9,5},{13,9},{1,13},{6,2},{10,6},{... | collective-permute-start | bytes 485384 | tf_op jit(solution)/shard_map/ppermute | solution.py:572
  11.8 0.7 %copy-start.5 = (f32[32]{0:T(128)S(1)}, f32[32]{0:T(128)}, u32[]{:S(2)}) copy-start(f32[32]{0:T(128)} %param.14) | copy-start | bytes 388
  11.8 0.7 %copy-start.6 = (f32[32]{0:T(128)S(1)}, f32[32]{0:T(128)}, u32[]{:S(2)}) copy-start(f32[32]{0:T(128)} %param.16) | copy-start | bytes 388
  18.0 0.7 %copy-start.4 = (s32[32]{0:T(128)S(1)}, s32[32]{0:T(128)}, u32[]{:S(2)}) copy-start(s32[32]{0:T(128)} %levels_ref.3) | copy-start | bytes 388
  21.2 3.0 %collective-permute-start.3 = (f32[18,16,384]{2,1,0:T(8,128)S(1)}, f32[18,16,384]{2,1,0:T(8,128)S(1)}, u32[]{:S(2)}, u32[]{:S(2)}) collective-permute-start(f32[18,16,384]{2,1,0:T(8,128)S(1)} %shard_map.146.mine_ref), channel_id=1, source_target_pairs={{0,1},{1,0},{2,3},{3,2},{4,5},{5,4},{6,7},{7,6},{8,9},{9,8},{10,11... | collective-permute-start | bytes 1327112 | tf_op jit(solution)/shard_map/ppermute | solution.py:585
  27.9 4.2 %collective-permute-start.4 = (f32[96,128]{1,0:T(8,128)S(1)}, f32[96,128]{1,0:T(8,128)S(1)}, u32[]{:S(2)}, u32[]{:S(2)}) collective-permute-start(f32[96,128]{1,0:T(8,128)S(1)} %get-tuple-element.48), channel_id=1, source_target_pairs={{0,2},{2,0},{1,3},{3,1},{4,6},{6,4},{5,7},{7,5},{8,10},{10,8},{9,1... | collective-permute-start | bytes 147464 | tf_op jit(solution)/shard_map/ppermute | solution.py:509
  32.1 4.1 %collective-permute-start.5 = (f32[96,128]{1,0:T(8,128)S(1)}, f32[96,128]{1,0:T(8,128)S(1)}, u32[]{:S(2)}, u32[]{:S(2)}) collective-permute-start(f32[96,128]{1,0:T(8,128)S(1)} %add.20), channel_id=1, source_target_pairs={{0,4},{4,0},{8,12},{12,8},{1,5},{5,1},{9,13},{13,9},{2,6},{6,2},{1... | collective-permute-start | bytes 147464 | tf_op jit(solution)/shard_map/ppermute | solution.py:509
  36.3 5.0 %collective-permute-start.6 = (f32[96,128]{1,0:T(8,128)S(1)}, f32[96,128]{1,0:T(8,128)S(1)}, u32[]{:S(2)}, u32[]{:S(2)}) collective-permute-start(f32[96,128]{1,0:T(8,128)S(1)} %add.21.mine_ref), channel_id=1, source_target_pairs={{0,8},{4,12},{8,0},{12,4},{1,9},{5,13},{9,1},{13,5},{2,10},{6,14},... | collective-permute-start | bytes 147464 | tf_op jit(solution)/shard_map/ppermute | solution.py:509

commit v4 on v3

--- a/solution.py
+++ b/solution.py
@@ -20,15 +20,6 @@
 NT = (((1,), (1,)), ((), ()))
 
 
-def pieces(array, count):
-    parts = []
-    for _ in range(count):
-        part = lax.reduce_precision(array, 8, 7)
-        parts.append(part)
-        array = array - part
-    return parts
-
-
 def halves(value):
     high = value.astype(BF16)
     return high, (value - high.astype(F32)).astype(BF16)
@@ -72,10 +63,16 @@
     return jnp.where(side_mask(), pltpu.roll(side, LANES - HALO - 2 * HALO * j, 1), 0.0)
 
 
-def load_field(index, main, below_ref, above_ref, sides, j):
-    top = jnp.concatenate([main.astype(F32), placed(sides[0], j)], axis=1)
-    strip = jnp.concatenate([rows_of(below_ref[index], above_ref[index]), placed(sides[1], j)], axis=1)
-    return jnp.concatenate([top, strip], axis=0)
+def joined(main, side, strip, strip_side, j):
+    top = jnp.concatenate([main.astype(F32), placed(side, j)], axis=1)
+    return jnp.concatenate([top, jnp.concatenate([strip, placed(strip_side, j)], axis=1)], axis=0)
+
+
+def cot_strip(strip, spare, part):
+    slot = lax.broadcasted_iota(jnp.int32, strip.shape, 0)
+    value = jnp.where(slot == 0, turn(strip, 3, 0), jnp.where(slot == 6, turn(strip, -2, 0), 0.0))
+    value = jnp.where(slot == 1, spare[part : part + 1], value)
+    return jnp.where(slot == 7, spare[HALO + part : HALO + part + 1], value)
 
 
 def run_copies(sources, targets, sems):
@@ -86,38 +83,51 @@
         copy.wait()
 
 
-def pack_kernel(tracer_hbm, cot_hbm, wind_hbm, out_ref, tracer_ref, cot_ref, wind_ref, sems):
-    cols = tracer_hbm.shape[2]
-    hbm = (tracer_hbm, cot_hbm, wind_hbm)
-    refs = (tracer_ref, cot_ref, wind_ref)
-    run_copies(
-        [ref.at[:, :, where] for ref in hbm for where in (slice(0, LANES), slice(cols - LANES, cols))],
-        [ref.at[part] for ref in refs for part in range(2)],
-        sems,
-    )
+def pack_kernel(odd_ref, tracer_hbm, cot_hbm, wind_hbm, out_ref, one_ref, two_ref, tracer_ref, cot_ref, wind_ref, sems):
+    run_copies((tracer_hbm, cot_hbm, wind_hbm), (tracer_ref, cot_ref, wind_ref), sems)
+    count, tile, cols = tracer_ref.shape
+    n_wind = wind_ref.shape[0]
     lane = lax.broadcasted_iota(jnp.int32, (1, LANES), 1)
     mask = side_mask()
-
-    def lifted(head, tail, j):
-        both = jnp.where(lane < HALO, head, tail)
+    odd = jnp.full((HALO, cols), odd_ref[0], jnp.int32) == 1
+
+    def lifted(value, j):
+        both = jnp.where(lane < HALO, value[:, :LANES], value[:, cols - LANES :])
         return pltpu.roll(jnp.where(mask, both, 0.0), HALO + 2 * HALO * j, 1)
 
-    groups = tracer_ref.shape[1] // GROUP
-    for group, ref in ((0, tracer_ref), (groups + 1, cot_ref)):
-        for start in range(0, ref.shape[1], GROUP):
-            total = jnp.zeros(out_ref.shape[1:], F32)
-            for j in range(GROUP):
-                total = total + lifted(ref[0, start + j].astype(F32), ref[1, start + j].astype(F32), j)
-            out_ref[group] = total.astype(BF16)
-            group += 1
+    def put(entry, first, last):
+        one_ref[entry] = jnp.where(odd, first, last).astype(BF16)
+        two_ref[entry] = jnp.where(odd, last, first).astype(BF16)
+
+    groups = count // GROUP
+    for group in range(groups):
+        totals = [jnp.zeros(out_ref.shape[1:], F32)] * 2
+        for start in range(0, GROUP, 4):
+            first, last = [], []
+            for part in range(4):
+                j = start + part
+                t = group * GROUP + j
+                tracer, cot = tracer_ref[t].astype(F32), cot_ref[t].astype(F32)
+                totals = [totals[0] + lifted(tracer, j), totals[1] + lifted(cot, j)]
+                put(
+                    t,
+                    jnp.concatenate([tracer[:3], cot[:1]], axis=0),
+                    jnp.concatenate([cot[tile - 2 : tile - 1], tracer[tile - 3 :]], axis=0),
+                )
+                first.append(cot[1:2])
+                last.append(cot[tile - 1 :])
+            put(count + t // 4, jnp.concatenate(first, axis=0), jnp.concatenate(last, axis=0))
+        out_ref[group] = totals[0].astype(BF16)
+        out_ref[groups + 1 + group] = totals[1].astype(BF16)
+    base = count + count // 4
     total = jnp.zeros(out_ref.shape[1:], F32)
-    count = wind_ref.shape[1]
-    for i in range(count):
-        head, tail = wind_ref[0, i], wind_ref[1, i]
+    for i in range(n_wind):
+        value = wind_ref[i]
         for part in range(3):
-            high_head, high_tail = head.astype(BF16).astype(F32), tail.astype(BF16).astype(F32)
-            total = total + lifted(high_head, high_tail, part * count + i)
-            head, tail = head - high_head, tail - high_tail
+            high = value.astype(BF16).astype(F32)
+            total = total + lifted(high, part * n_wind + i)
+            put(base + part * n_wind + i, high[:HALO], high[tile - HALO :])
+            value = value - high
     out_ref[groups] = total.astype(BF16)
     out_ref[2 * groups + 1] = jnp.zeros(out_ref.shape[1:], BF16)
 
@@ -180,7 +190,7 @@
         target[...] = jnp.sum(unit.astype(F32) * source[...], axis=1, keepdims=True)
 
 
-def grad_kernel(levels_ref, field_ref, side_ref, below_ref, above_ref, out_ref, moved_ref, held_ref):
+def grad_kernel(levels_ref, tracer_ref, cot_ref, side_ref, below_ref, above_ref, out_ref, moved_ref, held_ref):
     count = levels_ref.shape[0]
     slots, rows, width = moved_ref.shape[1:]
     channels = below_ref.shape[0] - 3
@@ -190,18 +200,24 @@
         near = sides_of(group, side_ref, below_ref, above_ref, channels)
         far = sides_of(groups + 1 + group, side_ref, below_ref, above_ref, channels)
 
-        def fill(j, lower):
-            t = group * GROUP + j
-            low = levels_ref[t] == 0
-            slot = jnp.where(low, lower, slots - 1 - t + lower)
-            field = load_field(t, field_ref[t], below_ref, above_ref, near, j)
-            cot = load_field(count + t, field_ref[count + t], below_ref, above_ref, far, j)
-            for step in range(3):
-                moved_ref[step, slot] = turn(field, STEPS[step], 1)
-                held_ref[step, slot] = turn(cot, -STEPS[step], 0)
-            return jnp.where(low, lower + 1, lower)
-
-        lower = lax.fori_loop(0, GROUP, fill, lower, unroll=4)
+        def fill(entry, lower):
+            spare = count + group * (GROUP // 4) + entry
+            spare = rows_of(below_ref[spare], above_ref[spare])
+            for part in range(4):
+                j = 4 * entry + part
+                t = group * GROUP + j
+                low = levels_ref[t] == 0
+                slot = jnp.where(low, lower, slots - 1 - t + lower)
+                strip = rows_of(below_ref[t], above_ref[t])
+                field = joined(tracer_ref[t], near[0], strip, near[1], j)
+                cot = joined(cot_ref[t], far[0], cot_strip(strip, spare, part), far[1], j)
+                for step in range(3):
+                    moved_ref[step, slot] = turn(field, STEPS[step], 1)
+                    held_ref[step, slot] = turn(cot, -STEPS[step], 0)
+                lower = jnp.where(low, lower + 1, lower)
+            return lower
+
+        lower = lax.fori_loop(0, GROUP // 4, fill, lower)
     for gap in (0, 1, 2, 5, 6, 7):
         for step in range(3):
             moved_ref[step, lower + gap] = jnp.zeros((rows, width), F32)
@@ -256,7 +272,7 @@
     count, rows, width = wind_ref.shape
     tile, cols = own_ref.shape[1:]
     channels = below_ref.shape[0] - 3
-    side, side_rows = sides_of((channels - 3 * count) // (2 * GROUP), side_ref, below_ref, above_ref, channels)
+    side, side_rows = sides_of(side_ref.shape[0] // 2 - 1, side_ref, below_ref, above_ref, channels)
     for i in range(count):
         wind_ref[i, HALO : HALO + tile, :cols] = own_ref[i]
         wide = [jnp.zeros((tile, LANES), F32), jnp.zeros((tile, LANES), F32)]
@@ -442,7 +458,7 @@
     )
 
 
-def tracer_kernel(levels_ref, wind_ref, corr_ref, field_ref, side_ref, below_ref, above_ref, out_ref, coef_ref):
+def tracer_kernel(levels_ref, wind_ref, corr_ref, cot_ref, side_ref, below_ref, above_ref, out_ref, coef_ref):
     count, tile, cols = out_ref.shape
     for level in range(LEVELS):
         px = lax_wendroff(COURANT * wind_ref[2 * level])
@@ -458,19 +474,24 @@
     for group in range(groups):
         sides = sides_of(groups + 1 + group, side_ref, below_ref, above_ref, channels)
 
-        def step(j, carry):
-            t = group * GROUP + j
-            level = levels_ref[t]
-            field = load_field(count + t, field_ref[count + t], below_ref, above_ref, sides, j)
-            total = jnp.zeros((tile, cols), F32)
-            for b in range(3):
-                moved = turn(field, -STEPS[b], 1)
-                for a in range(3):
-                    total = total + coef_ref[level, 3 * a + b] * turn(moved, -STEPS[a], 0)[:tile, :cols]
-            out_ref[t] = total.astype(BF16)
+        def step(entry, carry):
+            spare = count + group * (GROUP // 4) + entry
+            spare = rows_of(below_ref[spare], above_ref[spare])
+            for part in range(4):
+                j = 4 * entry + part
+                t = group * GROUP + j
+                level = levels_ref[t]
+                strip = cot_strip(rows_of(below_ref[t], above_ref[t]), spare, part)
+                field = joined(cot_ref[t], sides[0], strip, sides[1], j)
+                total = jnp.zeros((tile, cols), F32)
+                for b in range(3):
+                    moved = turn(field, -STEPS[b], 1)
+                    for a in range(3):
+                        total = total + coef_ref[level, 3 * a + b] * turn(moved, -STEPS[a], 0)[:tile, :cols]
+                out_ref[t] = total.astype(BF16)
             return carry
 
-        lax.fori_loop(0, GROUP, step, 0, unroll=4)
+        lax.fori_loop(0, GROUP // 4, step, 0)
 
 
 def call(kernel, outs, scratch, operands, spaces=None, flops=2_000_000, vmem=40):
@@ -518,16 +539,31 @@
     rows = tile + 2 * HALO
     vmem, spec = pltpu.VMEM, jax.ShapeDtypeStruct
     gy, gy_size = lax.axis_index("gy"), lax.axis_size("gy")
-    packed = call(
+    gx, gx_size = lax.axis_index("gx"), lax.axis_size("gx")
+    paired = gx_size % 2 == 0
+    odd = (gx % 2 if paired else 0 * gx).astype(jnp.int32)
+    strip = spec((count + count // 4 + 3 * n_wind, HALO, cols), BF16)
+    packed, one, two = call(
         pack_kernel,
-        spec((2 * (count // GROUP) + 2, tile, LANES), BF16),
-        [vmem((2, count, tile, LANES), BF16)] * 2
-        + [vmem((2, n_wind, tile, LANES), F32), pltpu.SemaphoreType.DMA((6,))],
-        (tracers, cotangent, winds),
-        {i: pltpu.HBM for i in range(3)},
-        200_000,
-        63,
-    )
+        [spec((2 * (count // GROUP) + 2, tile, LANES), BF16), strip, strip],
+        [vmem((count, tile, cols), BF16)] * 2
+        + [vmem((n_wind, tile, cols), F32), pltpu.SemaphoreType.DMA((3,))],
+        (odd[None], tracers, cotangent, winds),
+        {0: pltpu.SMEM} | {i: pltpu.HBM for i in range(1, 4)},
+        vmem=60,
+    )
+    spare = ((0, packed.shape[0] // 2), (0, 0), (0, 0))
+    one, two = lax.optimization_barrier((jnp.pad(one, spare), jnp.pad(two, spare)))
+    up, down = ring_pairs(gy_size, False)
+    lane = lax.broadcasted_iota(jnp.int32, (1, 1, LANES), 2) % (2 * HALO)
+    if gy_size == 2:
+        got = lax.ppermute(packed, "gy", up + down)
+        side = jnp.where(jnp.where(gy == 0, lane >= HALO, lane < HALO), got, 0)
+    else:
+        right = lax.ppermute(packed, "gy", down)
+        left = lax.ppermute(packed, "gy", up)
+        side = jnp.where(lane >= HALO, right, left)
+    side = side.astype(BF16)
     w1, w2, w2b, w1b, head_w, head_t, bias1_col, bias2_col = call(
         prep_kernel,
         [
@@ -551,35 +587,34 @@
             vmem((2 * CH, CH), F32),
             pltpu.SemaphoreType.DMA((5,)),
         ],
-        (conv1, bias1[None], conv2, bias2[None], head),
+        lax.optimization_barrier((conv1, bias1[None], conv2, bias2[None], head, side))[:5],
         {i: pltpu.HBM for i in range(5)},
     )
-    field = jnp.concatenate([tracers, cotangent] + [p.astype(BF16) for p in pieces(winds, 3)], axis=0)
-    up, down = ring_pairs(gy_size, False)
-    lane = lax.broadcasted_iota(jnp.int32, (1, 1, LANES), 2) % (2 * HALO)
-    if gy_size == 2:
-        got = lax.ppermute(packed, "gy", up + down)
-        side = jnp.where(jnp.where(gy == 0, lane >= HALO, lane < HALO), got, 0)
-    else:
-        right = lax.ppermute(packed, "gy", down)
-        left = lax.ppermute(packed, "gy", up)
-        side = jnp.where(lane >= HALO, right, left)
-    side = side.astype(BF16)
     half = side.shape[0] // 2
     wide = jnp.concatenate([side[:half], side[half:]], axis=2)
-    up, down = ring_pairs(lax.axis_size("gx"), True)
-    above = lax.ppermute(jnp.concatenate([field[:, tile - HALO :], wide[:, tile - HALO :]], axis=0), "gx", up)
-    below = lax.ppermute(jnp.concatenate([field[:, :HALO], wide[:, :HALO]], axis=0), "gx", down)
+    first_rows, last_rows = wide[:, :HALO], wide[:, tile - HALO :]
+    is_odd = odd == 1
+    one = lax.dynamic_update_slice(one, jnp.where(is_odd, first_rows, last_rows), (one.shape[0] - half, 0, 0))
+    two = lax.dynamic_update_slice(two, jnp.where(is_odd, last_rows, first_rows), (two.shape[0] - half, 0, 0))
+    if paired:
+        ahead = [(i, i ^ 1) for i in range(gx_size)]
+        behind = [(i, (i + 1) % gx_size if i % 2 else (i - 1) % gx_size) for i in range(gx_size)]
+        one, two = lax.ppermute(one, "gx", ahead), lax.ppermute(two, "gx", behind)
+        below, above = jnp.where(is_odd, two, one), jnp.where(is_odd, one, two)
+    else:
+        up, down = ring_pairs(gx_size, True)
+        above, below = lax.ppermute(one, "gx", up), lax.ppermute(two, "gx", down)
     place = lax.broadcasted_iota(jnp.int32, (1, width), 1)
     has_right, has_left = gy < gy_size - 1, gy > 0
     inside = jnp.where(place < cols, True, jnp.where(place < cols + LANES // 2, has_right, has_left)).astype(F32)
 
-    above, below, w1, w2 = lax.optimization_barrier((above, below, w1, w2))
+    levels = jnp.clip(levels, 0, LEVELS - 1)
+    above, below, w1, w2, levels = lax.optimization_barrier((above, below, w1, w2, levels))
     mine = call(
         grad_kernel,
         spec((9 * LEVELS, rows, width), F32),
         [vmem((3, count + 8, rows, width), F32)] * 2,
-        (levels, field, side, below, above),
+        (levels, tracers, cotangent, side, below, above),
         {0: pltpu.SMEM},
     )
     other = lax.ppermute(mine, "tracer", [(i, i ^ 1) for i in range(lax.axis_size("tracer"))])
@@ -610,7 +645,7 @@
         tracer_kernel,
         spec((count, tile, cols), BF16),
         [vmem((LEVELS, 9, tile, cols), F32)],
-        (levels, wind_ext, corr, field, side, below, above),
+        (levels, wind_ext, corr, cotangent, side, below, above),
         {0: pltpu.SMEM},
     )
     wind_grad = call(

time: 42.5 us -> 40.6 us (0.955)
  local copies, waits for them, and re-layouts: 3.09 us -> 1.7 us
  starting transfers between devices: 11.3 us -> 10.8 us
    unnamed x20, local copies, waits for them, and re-layouts: 2.98 us -> 0.67 us
    ppermute x2, waiting for transfers between devices: 4.96 us -> 3.54 us  [body(): one, two = (lax.ppermute(one, 'gx', ahead), lax.ppermute(two, 'gx', behind))]
    pad x0 -> x2, local copies, waits for them, and re-layouts: none -> 1.02 us  [the longest x1 0.98 us: body(): jnp.pad(one, spare)]
    ppermute x1, waiting for transfers between devices: 0.05 us -> 0.82 us  [body(): got = lax.ppermute(packed, 'gy', up + down)]
    ppermute x3, waiting for transfers between devices: 5.16 us -> 5.72 us  [sum_rounds(): other = lax.ppermute(value, axis, [(i, i ^ step) for i in range(size)])]
    ppermute x3, starting transfers between devices: 4.02 us -> 3.55 us  [sum_rounds(): other = lax.ppermute(value, axis, [(i, i ^ step) for i in range(size)])]
  transfers between devices with their start and end apart: 7 -> 7, of which waited for: 6 -> 5; matrix products, arithmetic and copies ran while one was open for 0% -> 3% of each run, Pallas kernels for 18% -> 19%
where the time goes in v4:
time: 40.6 us; the launch traced here: 40.4 us
  Pallas kernels  16.8 us (41%)
  starting transfers between devices  10.8 us (27%)
  waiting for transfers between devices  10.1 us (25%)
  local copies, waits for them, and re-layouts  1.7 us (4%)
  between operations  0.87 us (2%)
    pallas_call x8, Pallas kernels, call(): pl.pallas_call(kernel, out_shape=outs, in_specs=specs, out_specs=[whole]...  16.8 us
    ppermute x3, waiting for transfers between devices, sum_rounds(): other = lax.ppermute(value, axis, [(i, i ^ step) for i in range(size)])  5.72 us
    ppermute x2, starting transfers between devices, body(): one, two = (lax.ppermute(one, 'gx', ahead), lax.ppermute(two, 'gx', behind))  4.2 us
    ppermute x3, starting transfers between devices, sum_rounds(): other = lax.ppermute(value, axis, [(i, i ^ step) for i in range(size)])  3.55 us
    ppermute x2, waiting for transfers between devices, body(): one, two = (lax.ppermute(one, 'gx', ahead), lax.ppermute(two, 'gx', behind))  3.54 us
    ppermute x1, starting transfers between devices, body(): got = lax.ppermute(packed, 'gy', up + down)  3 us
    pad x1, local copies, waits for them, and re-layouts, body(): jnp.pad(one, spare)  0.98 us
    ppermute x1, waiting for transfers between devices, body(): got = lax.ppermute(packed, 'gy', up + down)  0.82 us
  transfers between devices with their start and end apart: 7, of which 5 were waited for; matrix products, arithmetic and copies ran while one was open for 3% of the time, Pallas kernels for 19%

profile of v4, /device:TPU:0, one launch (start us, length us, event | category | flops | bytes accessed | tf_op | source)
XLA Modules:
  0.0 40.4 jit_solution(10757729961401256793)
XLA Ops:
  0.6 1.8 %shard_map.144 = (bf16[6,8,128]{2,1,0:T(8,128)(2,1)}, bf16[52,4,256]{2,1,0:T(4,128)(2,1)}, bf16[52,4,256]{2,1,0:T(4,128)(2,1)}) custom-call(s32[1]{0:T(128)} %bitcast.odd_ref, bf16[32,8,256]{2,1,0:T(8,128)(2,1)} %tracer_ref.1, bf16[32,8,256]{2,1,0:T(8,128)(2,1)} %cot_ref.3, f32[4,8,256]{2,1,0:T(8,128)} %own_ref.1), custom_call_target="tpu_custom_call" | custom-call | flops 2000000 | bytes 2000000 | tf_op jit(solution)/shard_map/pallas_call | solution.py:500
  2.5 3.0 %collective-permute-start = (bf16[6,8,128]{2,1,0:T(8,128)(2,1)}, bf16[6,8,128]{2,1,0:T(8,128)(2,1)S(1)}, u32[]{:S(2)}, u32[]{:S(2)}) collective-permute-start(bf16[6,8,128]{2,1,0:T(8,128)(2,1)} %get-tuple-element.48), channel_id=1, source_target_pairs={{0,2},{2,0},{1,3},{3,1},{4,6},{6,4},{5,7},{7,5},{8,10},{10,8},{9,1... | collective-permute-start | bytes 36872 | tf_op jit(solution)/shard_map/ppermute | solution.py:560
  5.5 0.0 copy-start.8
  5.5 1.0 %pad.7 = bf16[55,4,256]{2,1,0:T(4,128)(2,1)S(1)} pad(bf16[52,4,256]{2,1,0:T(4,128)(2,1)} %get-tuple-element.45, bf16[]{:T(256)} %constant.42.clone.1), padding=0_3x0_0x0_0 | pad | bytes 219138 | tf_op jit(solution)/shard_map/jit(_pad)/pad | solution.py:556
  6.5 0.0 copy-done.8
  6.5 0.0 copy-start.3
  6.6 0.8 %collective-permute-done = bf16[6,8,128]{2,1,0:T(8,128)(2,1)S(1)} collective-permute-done((bf16[6,8,128]{2,1,0:T(8,128)(2,1)}, bf16[6,8,128]{2,1,0:T(8,128)(2,1)S(1)}, u32[]{:S(2)}, u32[]{:S(2)}) %collective-permute-start) | collective-permute-done | bytes 12320 | tf_op jit(solution)/shard_map/ppermute | solution.py:560
  7.4 0.0 copy-start.9
  7.4 0.0 copy-start.4
  7.4 0.0 copy-start.5
  7.4 4.2 %collective-permute-start.2 = (bf16[55,4,256]{2,1,0:T(4,128)(2,1)S(1)}, bf16[55,4,256]{2,1,0:T(4,128)(2,1)S(1)}, u32[]{:S(2)}, u32[]{:S(2)}) collective-permute-start(bf16[55,4,256]{2,1,0:T(4,128)(2,1)S(1)} %get-tuple-element.85), channel_id=1, source_target_pairs={{0,12},{4,8},{8,4},{12,0},{1,13},{5,9},{9,5},{13,1},{2,14},{6,10},... | collective-permute-start | bytes 337928 | tf_op jit(solution)/shard_map/ppermute | solution.py:602
  11.6 0.0 collective-permute-start.1
  11.6 0.0 copy-done.9
  11.6 0.0 copy-start.6
  11.7 0.0 copy-start.7
  11.7 0.0 copy-done.3
  11.7 0.0 copy-done.4
  11.7 0.0 copy-done.5
  11.7 0.6 %copy-done.6 = f32[32]{0:T(128)S(1)} copy-done((f32[32]{0:T(128)S(1)}, f32[32]{0:T(128)}, u32[]{:S(2)}) %copy-start.6) | copy-done | bytes 152
  12.3 0.0 copy-done.7
  12.3 0.5 %shard_map.145 = (bf16[64,48]{1,0:T(8,128)(2,1)S(1)}, bf16[64,288]{1,0:T(8,128)(2,1)S(1)}, bf16[64,288]{1,0:T(8,128)(2,1)S(1)}, bf16[32,288]{1,0:T(8,128)(2,1)S(...) custom-call(f32[32,36]{1,0:T(8,128)S(1)} %copy-done.4, ...), custom_call_target="tpu_custom_call" | custom-call | flops 2000000 | bytes 2000000 | tf_op jit(solution)/shard_map/pallas_call | solution.py:500
  12.8 0.0 copy-start
  12.8 0.0 copy-start.1
  12.9 2.1 %collective-permute-done.2 = bf16[55,4,256]{2,1,0:T(4,128)(2,1)S(1)} collective-permute-done((bf16[55,4,256]{2,1,0:T(4,128)(2,1)S(1)}, bf16[55,4,256]{2,1,0:T(4,128)(2,1)S(1)}, u32[]{:S(2)}, u32[]{:S(2)}) %collective-permute-start.2) | collective-permute-done | bytes 112672 | tf_op jit(solution)/shard_map/ppermute | solution.py:602
  15.0 1.4 %collective-permute-done.1 = bf16[55,4,256]{2,1,0:T(4,128)(2,1)S(1)} collective-permute-done((bf16[55,4,256]{2,1,0:T(4,128)(2,1)S(1)}, bf16[55,4,256]{2,1,0:T(4,128)(2,1)S(1)}, u32[]{:S(2)}, u32[]{:S(2)}) %collective-permute-start.1) | collective-permute-done | bytes 112672 | tf_op jit(solution)/shard_map/ppermute | solution.py:602
  16.4 0.1 broadcast_select_fusion
  16.5 0.0 copy-done
  16.5 0.0 copy-done.1
  16.5 0.0 copy-start.2
  16.5 2.6 %shard_map.146.mine_ref = f32[18,16,384]{2,1,0:T(8,128)S(1)} custom-call(s32[32]{0:T(128)S(1)} %broadcast_clamp_fusion.levels_ref, bf16[32,8,256]{2,1,0:T(8,128)(2,1)S(1)} %copy-done.1, bf16[32,8,256]{2,1,0:T(8,128)(2,1)S(1)} %copy-done, bf16[6,8,128]{2,1,0:T(8,128)(2,1)S(1)} %broadcast_select_fusion.2.side_ref, ...), custom_call_target="tpu_custom_call" | custom-call | flops 2000000 | bytes 2000000 | tf_op jit(solution)/shard_map/pallas_call | solution.py:500
  19.2 0.1 collective-permute-start.3
  19.3 0.0 copy-done.2
  19.3 2.9 %shard_map.147 = (f32[32,5376]{1,0:T(8,128)S(1)}, f32[32,4608]{1,0:T(8,128)S(1)}, f32[18,16,384]{2,1,0:T(8,128)S(1)}, f32[4,16,384]{2,1,0:T(8,128)S(1)}) custom-call(f32[4,8,256]{2,1,0:T(8,128)S(1)} %copy-done.2, bf16[6,8,128]{2,1,0:T(8,128)(2,1)S(1)} %broadcast_select_fusion.2.side_ref, bf16[55,4,256]{2,1,0:T(4,128)(2,1)S(1)} %get-tuple-element.58.below_ref, ...), custom_call_target="tpu_custom_call" | custom-call | flops 2000000 | bytes 2000000 | tf_op jit(solution)/shard_map/pallas_call | solution.py:500
  22.2 0.0 collective-permute-done.3.other_ref
  22.2 3.7 %shard_map.148 = (f32[96,128]{1,0:T(8,128)S(1)}, f32[32,3840]{1,0:T(8,128)S(1)}) custom-call(f32[18,16,384]{2,1,0:T(8,128)S(1)} %shard_map.146.mine_ref, f32[18,16,384]{2,1,0:T(8,128)S(1)} %collective-permute-done.3.other_ref, f32[4,16,384]{2,1,0:T(8,128)S(1)} %get-tuple-element.65.wind_ref, f32[1,384]{1,0:T(1,128)S(1)} %select_convert_fusion.inside_ref, ...), custom_call_target="tpu_custom_call" | custom-call | flops 2000000 | bytes 2000000 | tf_op jit(solution)/shard_map/pallas_call | solution.py:500
  25.9 1.6 %collective-permute-start.4 = (f32[96,128]{1,0:T(8,128)S(1)}, f32[96,128]{1,0:T(8,128)S(1)}, u32[]{:S(2)}, u32[]{:S(2)}) collective-permute-start(f32[96,128]{1,0:T(8,128)S(1)} %get-tuple-element.70), channel_id=1, source_target_pairs={{0,2},{2,0},{1,3},{3,1},{4,6},{6,4},{5,7},{7,5},{8,10},{10,8},{9,1... | collective-permute-start | bytes 147464 | tf_op jit(solution)/shard_map/ppermute | solution.py:530
  27.5 2.7 %shard_map.149 = bf16[32,8,256]{2,1,0:T(8,128)(2,1)} custom-call(s32[32]{0:T(128)S(1)} %broadcast_clamp_fusion.levels_ref, f32[4,16,384]{2,1,0:T(8,128)S(1)} %get-tuple-element.65.wind_ref, f32[18,16,384]{2,1,0:T(8,128)S(1)} %get-tuple-element.71.corr_ref, bf16[32,8,256]{2,1,0:T(8,128)(2,1)S(1)} %copy-done, ...), custom_call_target="tpu_custom_call" | custom-call | flops 2000000 | bytes 2000000 | tf_op jit(solution)/shard_map/pallas_call | solution.py:500
  30.2 0.0 collective-permute-done.4
  30.2 1.4 %collective-permute-start.5 = (f32[96,128]{1,0:T(8,128)S(1)}, f32[96,128]{1,0:T(8,128)S(1)}, u32[]{:S(2)}, u32[]{:S(2)}) collective-permute-start(f32[96,128]{1,0:T(8,128)S(1)} %add.29), channel_id=1, source_target_pairs={{0,4},{4,0},{8,12},{12,8},{1,5},{5,1},{9,13},{13,9},{2,6},{6,2},{1... | collective-permute-start | bytes 147464 | tf_op jit(solution)/shard_map/ppermute | solution.py:530
  31.6 1.5 %shard_map.150 = f32[4,8,256]{2,1,0:T(8,128)} custom-call(f32[18,16,384]{2,1,0:T(8,128)S(1)} %shard_map.146.mine_ref, f32[18,16,384]{2,1,0:T(8,128)S(1)} %collective-permute-done.3.other_ref, f32[4,16,384]{2,1,0:T(8,128)S(1)} %get-tuple-element.65.wind_ref, f32[32,3840]{1,0:T(8,128)S(1)} %get-tuple-element.74.d1_ref, ...), custom_call_target="tpu_custom_call" | custom-call | flops 2000000 | bytes 2000000 | tf_op jit(solution)/shard_map/pallas_call | solution.py:500
  33.1 1.3 %collective-permute-done.5 = f32[96,128]{1,0:T(8,128)S(1)} collective-permute-done((f32[96,128]{1,0:T(8,128)S(1)}, f32[96,128]{1,0:T(8,128)S(1)}, u32[]{:S(2)}, u32[]{:S(2)}) %collective-permute-start.5) | collective-permute-done | bytes 49184 | tf_op jit(solution)/shard_map/ppermute | solution.py:530
  34.4 0.6 %collective-permute-start.6 = (f32[96,128]{1,0:T(8,128)S(1)}, f32[96,128]{1,0:T(8,128)S(1)}, u32[]{:S(2)}, u32[]{:S(2)}) collective-permute-start(f32[96,128]{1,0:T(8,128)S(1)} %add.30.mine_ref), channel_id=1, source_target_pairs={{0,8},{4,12},{8,0},{12,4},{1,9},{5,13},{9,1},{13,5},{2,10},{6,14},... | collective-permute-start | bytes 147464 | tf_op jit(solution)/shard_map/ppermute | solution.py:530
  35.0 4.5 %collective-permute-done.6.other_ref = f32[96,128]{1,0:T(8,128)S(1)} collective-permute-done((f32[96,128]{1,0:T(8,128)S(1)}, f32[96,128]{1,0:T(8,128)S(1)}, u32[]{:S(2)}, u32[]{:S(2)}) %collective-permute-start.6) | collective-permute-done | bytes 49184 | tf_op jit(solution)/shard_map/ppermute | solution.py:530
  39.4 1.0 %shard_map.151 = (f32[32,36]{1,0:T(8,128)}, f32[1,32]{1,0:T(1,128)}, f32[32,288]{1,0:T(8,128)}, f32[1,32]{1,0:T(1,128)}, f32[18,32]{1,0:T(8,128)}) custom-call(f32[96,128]{1,0:T(8,128)S(1)} %add.30.mine_ref, f32[96,128]{1,0:T(8,128)S(1)} %collective-permute-done.6.other_ref), custom_call_target="tpu_custom_call" | custom-call | flops 200000 | bytes 2000000 | tf_op jit(solution)/shard_map/pallas_call | solution.py:500
  (9 shorter events, 0.1 us)
Async XLA Ops:
  2.5 4.9 %collective-permute-start = (bf16[6,8,128]{2,1,0:T(8,128)(2,1)}, bf16[6,8,128]{2,1,0:T(8,128)(2,1)S(1)}, u32[]{:S(2)}, u32[]{:S(2)}) collective-permute-start(bf16[6,8,128]{2,1,0:T(8,128)(2,1)} %get-tuple-element.48), channel_id=1, source_target_pairs={{0,2},{2,0},{1,3},{3,1},{4,6},{6,4},{5,7},{7,5},{8,10},{10,8},{9,1... | collective-permute-start | bytes 36872 | tf_op jit(solution)/shard_map/ppermute | solution.py:560
  5.5 1.0 %copy-start.8 = (bf16[52,4,256]{2,1,0:T(4,128)(2,1)S(1)}, bf16[52,4,256]{2,1,0:T(4,128)(2,1)}, u32[]{:S(2)}) copy-start(bf16[52,4,256]{2,1,0:T(4,128)(2,1)} %get-tuple-element.46) | copy-start | bytes 319492
  6.5 5.1 %copy-start.3 = (f32[32,288]{1,0:T(8,128)S(1)}, f32[32,288]{1,0:T(8,128)}, u32[]{:S(2)}) copy-start(f32[32,288]{1,0:T(8,128)} %c2_hbm) | copy-start | bytes 110596
  7.4 4.3 %copy-start.9 = (s32[32]{0:T(128)S(1)}, s32[32]{0:T(128)}, u32[]{:S(2)}) copy-start(s32[32]{0:T(128)} %param.12) | copy-start | bytes 388
  7.4 4.3 %copy-start.4 = (f32[32,36]{1,0:T(8,128)S(1)}, f32[32,36]{1,0:T(8,128)}, u32[]{:S(2)}) copy-start(f32[32,36]{1,0:T(8,128)} %c1_hbm) | copy-start | bytes 13828
  7.4 4.3 %copy-start.5 = (f32[18,32]{1,0:T(8,128)S(1)}, f32[18,32]{1,0:T(8,128)}, u32[]{:S(2)}) copy-start(f32[18,32]{1,0:T(8,128)} %head_hbm) | copy-start | bytes 6916
  7.4 7.6 %collective-permute-start.2 = (bf16[55,4,256]{2,1,0:T(4,128)(2,1)S(1)}, bf16[55,4,256]{2,1,0:T(4,128)(2,1)S(1)}, u32[]{:S(2)}, u32[]{:S(2)}) collective-permute-start(bf16[55,4,256]{2,1,0:T(4,128)(2,1)S(1)} %get-tuple-element.85), channel_id=1, source_target_pairs={{0,12},{4,8},{8,4},{12,0},{1,13},{5,9},{9,5},{13,1},{2,14},{6,10},... | collective-permute-start | bytes 337928 | tf_op jit(solution)/shard_map/ppermute | solution.py:602
  11.6 4.8 %collective-permute-start.1 = (bf16[55,4,256]{2,1,0:T(4,128)(2,1)S(1)}, bf16[55,4,256]{2,1,0:T(4,128)(2,1)S(1)}, u32[]{:S(2)}, u32[]{:S(2)}) collective-permute-start(bf16[55,4,256]{2,1,0:T(4,128)(2,1)S(1)} %get-tuple-element.86), channel_id=1, source_target_pairs={{0,4},{4,0},{8,12},{12,8},{1,5},{5,1},{9,13},{13,9},{2,6},{6,2},{1... | collective-permute-start | bytes 337928 | tf_op jit(solution)/shard_map/ppermute | solution.py:602
  11.6 0.7 %copy-start.6 = (f32[32]{0:T(128)S(1)}, f32[32]{0:T(128)}, u32[]{:S(2)}) copy-start(f32[32]{0:T(128)} %param.14) | copy-start | bytes 388
  11.7 0.7 %copy-start.7 = (f32[32]{0:T(128)S(1)}, f32[32]{0:T(128)}, u32[]{:S(2)}) copy-start(f32[32]{0:T(128)} %param.16) | copy-start | bytes 388
  12.8 3.7 %copy-start = (bf16[32,8,256]{2,1,0:T(8,128)(2,1)S(1)}, bf16[32,8,256]{2,1,0:T(8,128)(2,1)}, u32[]{:S(2)}) copy-start(bf16[32,8,256]{2,1,0:T(8,128)(2,1)} %cot_ref.3) | copy-start | bytes 393220
  12.8 3.7 %copy-start.1 = (bf16[32,8,256]{2,1,0:T(8,128)(2,1)S(1)}, bf16[32,8,256]{2,1,0:T(8,128)(2,1)}, u32[]{:S(2)}) copy-start(bf16[32,8,256]{2,1,0:T(8,128)(2,1)} %tracer_ref.1) | copy-start | bytes 393220
  16.5 2.8 %copy-start.2 = (f32[4,8,256]{2,1,0:T(8,128)S(1)}, f32[4,8,256]{2,1,0:T(8,128)}, u32[]{:S(2)}) copy-start(f32[4,8,256]{2,1,0:T(8,128)} %own_ref.1) | copy-start | bytes 98308
  19.2 3.0 %collective-permute-start.3 = (f32[18,16,384]{2,1,0:T(8,128)S(1)}, f32[18,16,384]{2,1,0:T(8,128)S(1)}, u32[]{:S(2)}, u32[]{:S(2)}) collective-permute-start(f32[18,16,384]{2,1,0:T(8,128)S(1)} %shard_map.146.mine_ref), channel_id=1, source_target_pairs={{0,1},{1,0},{2,3},{3,2},{4,5},{5,4},{6,7},{7,6},{8,9},{9,8},{10,11... | collective-permute-start | bytes 1327112 | tf_op jit(solution)/shard_map/ppermute | solution.py:620
  25.9 4.3 %collective-permute-start.4 = (f32[96,128]{1,0:T(8,128)S(1)}, f32[96,128]{1,0:T(8,128)S(1)}, u32[]{:S(2)}, u32[]{:S(2)}) collective-permute-start(f32[96,128]{1,0:T(8,128)S(1)} %get-tuple-element.70), channel_id=1, source_target_pairs={{0,2},{2,0},{1,3},{3,1},{4,6},{6,4},{5,7},{7,5},{8,10},{10,8},{9,1... | collective-permute-start | bytes 147464 | tf_op jit(solution)/shard_map/ppermute | solution.py:530
  30.2 4.2 %collective-permute-start.5 = (f32[96,128]{1,0:T(8,128)S(1)}, f32[96,128]{1,0:T(8,128)S(1)}, u32[]{:S(2)}, u32[]{:S(2)}) collective-permute-start(f32[96,128]{1,0:T(8,128)S(1)} %add.29), channel_id=1, source_target_pairs={{0,4},{4,0},{8,12},{12,8},{1,5},{5,1},{9,13},{13,9},{2,6},{6,2},{1... | collective-permute-start | bytes 147464 | tf_op jit(solution)/shard_map/ppermute | solution.py:530
  34.4 5.0 %collective-permute-start.6 = (f32[96,128]{1,0:T(8,128)S(1)}, f32[96,128]{1,0:T(8,128)S(1)}, u32[]{:S(2)}, u32[]{:S(2)}) collective-permute-start(f32[96,128]{1,0:T(8,128)S(1)} %add.30.mine_ref), channel_id=1, source_target_pairs={{0,8},{4,12},{8,0},{12,4},{1,9},{5,13},{9,1},{13,5},{2,10},{6,14},... | collective-permute-start | bytes 147464 | tf_op jit(solution)/shard_map/ppermute | solution.py:530

commit v5 on v4

--- a/solution.py
+++ b/solution.py
@@ -27,15 +27,14 @@
 
 def dot3(weights, high, low):
     rows = weights.shape[0] // 2
-    both = jnp.dot(weights, high, preferred_element_type=F32)
-    rest = jnp.dot(weights[:rows], low, preferred_element_type=F32)
-    return both[:rows] + both[rows:] + rest
-
-
-def dot3_nt(a_high, a_low, b_high, b_low):
-    out = lax.dot_general(a_high, b_high, NT, preferred_element_type=F32)
-    out = out + lax.dot_general(a_high, b_low, NT, preferred_element_type=F32)
-    return out + lax.dot_general(a_low, b_high, NT, preferred_element_type=F32)
+    both = jnp.dot(weights, jnp.concatenate([high, low], axis=0), preferred_element_type=F32)
+    return both[:rows] + both[rows:]
+
+
+def dot3_nt(left, right):
+    rows, cols = left.shape[0] // 2, right.shape[0] // 2
+    out = lax.dot_general(left, right, NT, preferred_element_type=F32)
+    return out[:rows, :cols] + out[:rows, cols:] + out[rows:, :cols]
 
 
 def turn(value, step, axis):
@@ -141,7 +140,7 @@
 def prep_kernel(
     c1_hbm, b1_hbm, c2_hbm, b2_hbm, head_hbm,
     w1_ref, w2_ref, w2b_ref, w1b_ref, hw_ref, ht_ref, b1_ref, b2_ref,
-    c1, b1, c2, b2, head, wide_ref, slim_ref, tall_ref, sems,
+    c1, b1, c2, b2, head, wide_ref, slim_ref, tall_ref, pair_ref, sems,
 ):
     run_copies((c1_hbm, b1_hbm, c2_hbm, b2_hbm, head_hbm), (c1, b1, c2, b2, head), sems)
     n_wind = c1.shape[1] // 9
@@ -154,13 +153,20 @@
         b = (r >= n_wind).astype(jnp.int32) + (r >= 2 * n_wind).astype(jnp.int32)
         return jnp.where(r < 3 * n_wind, 9 * (r - n_wind * b) + 3 * a + b, -1)
 
+    def doubled(target, value):
+        rows, depth = value.shape[0] // 2, value.shape[1]
+        pair_ref[: 2 * rows, :depth] = value
+        pair_ref[:rows, depth : 2 * depth] = value[:rows]
+        pair_ref[rows : 2 * rows, depth : 2 * depth] = jnp.zeros((rows, depth), F32)
+        target[...] = pair_ref[: 2 * rows, : 2 * depth].astype(BF16)
+
     both2 = jnp.concatenate(halves(c2[...]), axis=0)
     size = both2.shape[1]
-    w2_ref[...] = jnp.dot(both2, picker((size, size), 0, wanted2), preferred_element_type=F32).astype(BF16)
+    doubled(w2_ref, jnp.dot(both2, picker((size, size), 0, wanted2), preferred_element_type=F32))
     turned = lax.dot_general(picker((size, size), 1, wanted2), both2, NT, preferred_element_type=F32)
     both1 = jnp.concatenate(halves(c1[...]), axis=0)
     size = both1.shape[1]
-    w1_ref[...] = jnp.dot(both1, picker((size, 48), 0, wanted1), preferred_element_type=F32).astype(BF16)
+    doubled(w1_ref, jnp.dot(both1, picker((size, 48), 0, wanted1), preferred_element_type=F32))
     turned1 = lax.dot_general(picker((48, size), 1, wanted1), both1, NT, preferred_element_type=F32)
     slim_ref[...] = jnp.zeros(slim_ref.shape, F32)
     for q in range(9):
@@ -170,8 +176,8 @@
             lanes = slice(part * CH, (part + 1) * CH)
             wide_ref[lanes, where] = turned[where, lanes]
             slim_ref[16 * part : 16 * part + n_wind, where] = turned1[start : start + n_wind, lanes]
-    w2b_ref[...] = wide_ref[...].astype(BF16)
-    w1b_ref[...] = slim_ref[...].astype(BF16)
+    doubled(w2b_ref, wide_ref[...])
+    doubled(w1b_ref, slim_ref[...])
     tall_ref[...] = jnp.zeros(tall_ref.shape, F32)
     for level in range(LEVELS):
         rows = slice(9 * level, 9 * level + 9)
@@ -181,47 +187,23 @@
         tall_ref[rows, :] = high
         tall_ref[CH + 9 * level : CH + 9 * level + 9, :] = part - high
     tall = tall_ref[...].astype(BF16)
-    hw_ref[...] = tall
+    doubled(hw_ref, tall_ref[...])
     unit = picker((CH, CH), 0, lambda target: target)
     across = lax.dot_general(unit, tall, NT, preferred_element_type=F32)
-    ht_ref[:CH, :] = across[:, :CH].astype(BF16)
-    ht_ref[CH:, :] = across[:, CH:].astype(BF16)
+    doubled(ht_ref, jnp.concatenate([across[:, :CH], across[:, CH:]], axis=0))
     for source, target in ((b1, b1_ref), (b2, b2_ref)):
         target[...] = jnp.sum(unit.astype(F32) * source[...], axis=1, keepdims=True)
 
 
-def grad_kernel(levels_ref, tracer_ref, cot_ref, side_ref, below_ref, above_ref, out_ref, moved_ref, held_ref):
-    count = levels_ref.shape[0]
+def gap_zeroed(refs, lower):
+    for ref in refs:
+        for gap in (0, 1, 2, 5, 6, 7):
+            for step in range(3):
+                ref[step, lower + gap] = jnp.zeros(ref.shape[2:], F32)
+
+
+def slot_sums(moved_ref, held_ref, lower, count, store):
     slots, rows, width = moved_ref.shape[1:]
-    channels = below_ref.shape[0] - 3
-    groups = count // GROUP
-    lower = jnp.int32(0)
-    for group in range(groups):
-        near = sides_of(group, side_ref, below_ref, above_ref, channels)
-        far = sides_of(groups + 1 + group, side_ref, below_ref, above_ref, channels)
-
-        def fill(entry, lower):
-            spare = count + group * (GROUP // 4) + entry
-            spare = rows_of(below_ref[spare], above_ref[spare])
-            for part in range(4):
-                j = 4 * entry + part
-                t = group * GROUP + j
-                low = levels_ref[t] == 0
-                slot = jnp.where(low, lower, slots - 1 - t + lower)
-                strip = rows_of(below_ref[t], above_ref[t])
-                field = joined(tracer_ref[t], near[0], strip, near[1], j)
-                cot = joined(cot_ref[t], far[0], cot_strip(strip, spare, part), far[1], j)
-                for step in range(3):
-                    moved_ref[step, slot] = turn(field, STEPS[step], 1)
-                    held_ref[step, slot] = turn(cot, -STEPS[step], 0)
-                lower = jnp.where(low, lower + 1, lower)
-            return lower
-
-        lower = lax.fori_loop(0, GROUP // 4, fill, lower)
-    for gap in (0, 1, 2, 5, 6, 7):
-        for step in range(3):
-            moved_ref[step, lower + gap] = jnp.zeros((rows, width), F32)
-            held_ref[step, lower + gap] = jnp.zeros((rows, width), F32)
     for level in range(LEVELS):
         trips = lax.shift_right_logical((lower if level == 0 else count - lower) + 3, 2)
         for start in range(0, width, LANES):
@@ -238,7 +220,96 @@
 
             sums = lax.fori_loop(0, trips, step, (jnp.zeros((rows, LANES), F32),) * 9)
             for k in range(9):
-                out_ref[9 * level + k, :, lanes] = turn(sums[k], STEPS[k // 3], 0)
+                store(level, k, lanes, sums[k])
+
+
+def slot_of(level, t, lower, slots):
+    low = level == 0
+    return jnp.where(low, lower, slots - 1 - t + lower), jnp.where(low, lower + 1, lower)
+
+
+def inner_kernel(levels_ref, tracer_ref, cot_ref, side_ref, out_ref, edge_ref, moved_ref, held_ref):
+    count, tile, cols = tracer_ref.shape
+    slots, _, width = moved_ref.shape[1:]
+    half = side_ref.shape[0] // 2
+    row = lax.broadcasted_iota(jnp.int32, (tile, width), 0)
+    lower = jnp.int32(0)
+    for group in range(count // GROUP):
+        near, far = side_ref[group].astype(F32), side_ref[half + group].astype(F32)
+
+        def fill(entry, lower):
+            for part in range(4):
+                j = 4 * entry + part
+                t = group * GROUP + j
+                slot, lower = slot_of(levels_ref[t], t, lower, slots)
+                field = jnp.concatenate([tracer_ref[t].astype(F32), placed(near, j)], axis=1)
+                cot = jnp.concatenate([cot_ref[t].astype(F32), placed(far, j)], axis=1)
+                for b in range(3):
+                    moved_ref[b, slot] = turn(field, STEPS[b], 1)
+                later, sooner = turn(cot, 1, 0), turn(cot, -1, 0)
+                held_ref[0, slot] = jnp.where(row == tile - 1, 0.0, later)
+                held_ref[1, slot] = cot
+                held_ref[2, slot] = jnp.where(row == 0, 0.0, sooner)
+                edge_ref[0, t] = turn(field, HALO, 0)
+                edge_ref[1, t] = jnp.where(row == 0, sooner, later)
+            return lower
+
+        lower = lax.fori_loop(0, GROUP // 4, fill, lower)
+    gap_zeroed((moved_ref, held_ref), lower)
+
+    def store(level, k, lanes, total):
+        out_ref[9 * level + k, :, lanes] = turn(total, STEPS[k // 3], 0)
+
+    slot_sums(moved_ref, held_ref, lower, count, store)
+
+
+def border_kernel(levels_ref, inner_ref, edge_ref, side_ref, below_ref, above_ref, out_ref, moved_ref, held_ref):
+    count = levels_ref.shape[0]
+    slots, rows, width = moved_ref.shape[1:]
+    tile = inner_ref.shape[1]
+    channels = below_ref.shape[0] - side_ref.shape[0] // 2
+    groups = count // GROUP
+    row = lax.broadcasted_iota(jnp.int32, (rows, width), 0)
+    lower = jnp.int32(0)
+    for group in range(groups):
+        near = sides_of(group, side_ref, below_ref, above_ref, channels)[1]
+        far = sides_of(groups + 1 + group, side_ref, below_ref, above_ref, channels)[1]
+
+        def fill(entry, lower):
+            spare = count + group * (GROUP // 4) + entry
+            spare = rows_of(below_ref[spare], above_ref[spare])
+            for part in range(4):
+                j = 4 * entry + part
+                t = group * GROUP + j
+                slot, lower = slot_of(levels_ref[t], t, lower, slots)
+                strip = rows_of(below_ref[t], above_ref[t])
+                field = jnp.concatenate([strip, placed(near, j)], axis=1)
+                field = jnp.where((row == 3) | (row == 4), edge_ref[0, t], field)
+                cot = jnp.concatenate([cot_strip(strip, spare, part), placed(far, j)], axis=1)
+                edge = edge_ref[1, t]
+                for b in range(3):
+                    moved_ref[b, slot] = turn(field, STEPS[b], 1)
+                held_ref[0, slot] = jnp.where(row == 7, edge, jnp.where(row == 3, turn(cot, -3, 0), turn(cot, 1, 0)))
+                held_ref[1, slot] = cot
+                held_ref[2, slot] = jnp.where(row == 0, edge, jnp.where(row == 4, turn(cot, 3, 0), turn(cot, -1, 0)))
+            return lower
+
+        lower = lax.fori_loop(0, GROUP // 4, fill, lower)
+    gap_zeroed((moved_ref, held_ref), lower)
+    place = row[:, :LANES]
+
+    def store(level, k, lanes, total):
+        index, step = 9 * level + k, STEPS[k // 3]
+        inner = inner_ref[index, :, lanes]
+        if step:
+            last = 7 if step == 1 else 0
+            shifted = turn(total, step, 0)
+            inner = inner + jnp.where(place == last, shifted, 0.0)
+            total = jnp.where(place == last, turn(total, 5 if step == 1 else 3, 0), shifted)
+        out_ref[index, :tile, lanes] = inner
+        out_ref[index, tile:, lanes] = total
+
+    slot_sums(moved_ref, held_ref, lower, count, store)
 
 
 def put_moved(high_ref, low_ref, row, value, sign):
@@ -311,7 +382,7 @@
 def backward_kernel(
     mine_ref, other_ref, wind_ref, inside_ref, first_ref, second_ref, headt_ref, w2b_ref,
     par_ref, d1_ref,
-    sum_ref, g_ref, d2_high, d2_low, own2_high, own2_low, act_high, act_low, own1_high, own1_low, wind_stack,
+    sum_ref, g_ref, d2_high, d2_low, own2_ref, act_ref, own1_ref, wind_stack,
 ):
     cells = g_ref.shape[1]
     width = wind_ref.shape[2]
@@ -326,18 +397,18 @@
         g_ref[:nine, row * width : (row + 1) * width] = sum_ref[:, (row - 2) % wrap, :]
     own = lax.broadcasted_iota(jnp.int32, (1, width), 1) < cols
     inside = inside_ref[...]
-    for ref in (own2_high, own2_low, own1_high, own1_low):
+    for ref in (own2_ref, own1_ref):
         ref[...] = jnp.zeros(ref.shape, BF16)
     wind_stack[...] = jnp.zeros(wind_stack.shape, F32)
     put_winds(wind_ref, wind_stack, 3, tile + 2)
     wind_stack[12:13, :] = jnp.ones((1, wind_stack.shape[1]), F32)
     bias2 = jnp.zeros((CH, width), F32)
 
-    def put_own(high_ref, low_ref, x, value):
-        high, low = halves(jnp.where(own, value, 0.0))
-        for a in range(3):
-            high_ref[a * CH : (a + 1) * CH, (x + a) * width : (x + a + 1) * width] = high
-            low_ref[a * CH : (a + 1) * CH, (x + a) * width : (x + a + 1) * width] = low
+    def put_own(ref, x, value):
+        for half, part in enumerate(halves(jnp.where(own, value, 0.0))):
+            for a in range(3):
+                start = (3 * half + a) * CH
+                ref[start : start + CH, (x + a) * width : (x + a + 1) * width] = part
 
     for row in range(0, ring, 2):
         where = slice(row * width, (row + 2) * width)
@@ -350,12 +421,12 @@
             put_moved(d2_high, d2_low, row + part, value, -1)
             x = row + part - 2
             if 0 <= x < tile:
-                put_own(own2_high, own2_low, x, value)
+                put_own(own2_ref, x, value)
                 bias2 = bias2 + jnp.where(own, value, 0.0)
     for row in range(tile + 2):
-        put_moved(act_high, act_low, row, first_ref[:, (row + 2) * width : (row + 3) * width], 1)
+        put_moved(act_ref.at[: 3 * CH], act_ref.at[3 * CH :], row, first_ref[:, (row + 2) * width : (row + 3) * width], 1)
     par_ref[...] = jnp.zeros(par_ref.shape, F32)
-    par_ref[:, : 3 * CH] = dot3_nt(act_high[...], act_low[...], own2_high[...], own2_low[...])
+    par_ref[:, : 3 * CH] = dot3_nt(act_ref[...], own2_ref[...])
     par_ref[:CH, 3 * CH + 16 : 3 * CH + 17] = jnp.sum(bias2, axis=1, keepdims=True)
     inside2 = jnp.concatenate([inside] * 2, axis=1)
     for row in range(0, tile + 2, 2):
@@ -367,14 +438,12 @@
             value = delta[:, part * width : (part + 1) * width]
             x = row + part - 1
             if 0 <= x < tile:
-                put_own(own1_high, own1_low, x, value)
-    high, low = halves(wind_stack[...])
-    par_ref[:, 3 * CH : 3 * CH + 16] = dot3_nt(own1_high[...], own1_low[...], high, low)
+                put_own(own1_ref, x, value)
+    par_ref[:, 3 * CH : 3 * CH + 16] = dot3_nt(own1_ref[...], jnp.concatenate(halves(wind_stack[...]), axis=0))
     mid = slice(2 * width, (2 + tile) * width)
     own_rows = jnp.concatenate([own] * tile, axis=1)
-    g_high, g_low = halves(jnp.where(own_rows, g_ref[:, mid], 0.0))
-    s_high, s_low = halves(second_ref[:, mid])
-    raw = dot3_nt(s_high, s_low, g_high, g_low)
+    grads = jnp.concatenate(halves(jnp.where(own_rows, g_ref[:, mid], 0.0)), axis=0)
+    raw = dot3_nt(jnp.concatenate(halves(second_ref[:, mid]), axis=0), grads)
     for level in range(LEVELS):
         rows = slice((level + 1) * CH, (level + 2) * CH)
         par_ref[rows, 3 * CH + 16 : 3 * CH + 25] = raw[:, 9 * level : 9 * level + 9]
@@ -513,23 +582,20 @@
     return up, [(j, i) for i, j in up]
 
 
-def sum_rounds(value, axes, beside):
-    other, done = jnp.zeros_like(value), []
-    for axis in axes:
-        size = lax.axis_size(axis)
-        if size & (size - 1):
-            value, other = lax.psum(value + other, axis), jnp.zeros_like(value)
-            continue
-        step = 1
-        while step < size:
-            value = value + other
-            if step > 1 or axis != axes[0]:
-                if len(done) < len(beside):
-                    value, made = lax.optimization_barrier((value, beside[len(done)]))
-                    done.append(made)
-            other = lax.ppermute(value, axis, [(i, i ^ step) for i in range(size)])
-            step *= 2
-    return value, other, tuple(done) + tuple(beside[len(done) :])
+def sum_rounds(value, axes, early, late):
+    sizes = [lax.axis_size(axis) for axis in axes]
+    other = jnp.zeros_like(value)
+    if any(size & (size - 1) for size in sizes):
+        return lax.psum(value, axes), other, early, late
+    rounds = [(axis, 1 << bit) for axis, size in zip(axes, sizes) for bit in range(size.bit_length() - 1)]
+    for index, (axis, step) in enumerate(rounds):
+        value = value + other
+        if index == 1:
+            value, early = lax.optimization_barrier((value, early))
+        if index == len(rounds) - 1:
+            value, late = lax.optimization_barrier((value, late))
+        other = lax.ppermute(value, axis, [(i, i ^ step) for i in range(lax.axis_size(axis))])
+    return value, other, early, late
 
 
 def body(tracers, cotangent, winds, levels, conv1, bias1, conv2, bias2, head):
@@ -567,12 +633,12 @@
     w1, w2, w2b, w1b, head_w, head_t, bias1_col, bias2_col = call(
         prep_kernel,
         [
-            spec((2 * CH, 48), BF16),
-            spec((2 * CH, 9 * CH), BF16),
-            spec((2 * CH, 9 * CH), BF16),
-            spec((32, 9 * CH), BF16),
-            spec((2 * CH, CH), BF16),
-            spec((2 * CH, CH), BF16),
+            spec((2 * CH, 96), BF16),
+            spec((2 * CH, 18 * CH), BF16),
+            spec((2 * CH, 18 * CH), BF16),
+            spec((32, 18 * CH), BF16),
+            spec((2 * CH, 2 * CH), BF16),
+            spec((2 * CH, 2 * CH), BF16),
             spec((CH, 1), F32),
             spec((CH, 1), F32),
         ],
@@ -585,6 +651,7 @@
             vmem((2 * CH, 9 * CH), F32),
             vmem((32, 9 * CH), F32),
             vmem((2 * CH, CH), F32),
+            vmem((2 * CH, 18 * CH), F32),
             pltpu.SemaphoreType.DMA((5,)),
         ],
         lax.optimization_barrier((conv1, bias1[None], conv2, bias2[None], head, side))[:5],
@@ -609,12 +676,19 @@
     inside = jnp.where(place < cols, True, jnp.where(place < cols + LANES // 2, has_right, has_left)).astype(F32)
 
     levels = jnp.clip(levels, 0, LEVELS - 1)
-    above, below, w1, w2, levels = lax.optimization_barrier((above, below, w1, w2, levels))
+    inner, edge = call(
+        inner_kernel,
+        [spec((9 * LEVELS, tile, width), F32), spec((2, count, tile, width), F32)],
+        [vmem((3, count + 8, tile, width), F32)] * 2,
+        (levels, tracers, cotangent, side),
+        {0: pltpu.SMEM},
+    )
+    above, below, w1, w2, inner = lax.optimization_barrier((above, below, w1, w2, inner))
     mine = call(
-        grad_kernel,
+        border_kernel,
         spec((9 * LEVELS, rows, width), F32),
-        [vmem((3, count + 8, rows, width), F32)] * 2,
-        (levels, tracers, cotangent, side, below, above),
+        [vmem((3, count + 8, 2 * HALO, width), F32)] * 2,
+        (levels, inner, edge, side, below, above),
         {0: pltpu.SMEM},
     )
     other = lax.ppermute(mine, "tracer", [(i, i ^ 1) for i in range(lax.axis_size("tracer"))])
@@ -637,10 +711,17 @@
         [spec((3 * CH, LANES), F32), spec((CH, own), F32)],
         [vmem((9 * LEVELS, rows, width), F32), vmem((CH, ring), F32)]
         + [vmem((3 * CH, ring), BF16)] * 2
-        + [vmem((3 * CH, own), BF16)] * 6
+        + [vmem((6 * CH, own), BF16)] * 3
         + [vmem((16, own), F32)],
         (mine, other, wind_ext, inside, first, second, head_t, w2b),
     )
+    wind_grad = call(
+        wind_kernel,
+        spec((n_wind, tile, cols), F32),
+        [vmem((3 * CH, own), BF16)] * 2 + [vmem((n_wind, tile, cols), F32)],
+        (mine, other, wind_ext, delta, w1b),
+    )
+    mine, other, wind_grad, corr = sum_rounds(params, ("gy", "gx"), wind_grad, corr)
     tracer_grad = call(
         tracer_kernel,
         spec((count, tile, cols), BF16),
@@ -648,13 +729,6 @@
         (levels, wind_ext, corr, cotangent, side, below, above),
         {0: pltpu.SMEM},
     )
-    wind_grad = call(
-        wind_kernel,
-        spec((n_wind, tile, cols), F32),
-        [vmem((3 * CH, own), BF16)] * 2 + [vmem((n_wind, tile, cols), F32)],
-        (mine, other, wind_ext, delta, w1b),
-    )
-    mine, other, (tracer_grad, wind_grad) = sum_rounds(params, ("gy", "gx"), (tracer_grad, wind_grad))
     conv1_grad, bias1_grad, conv2_grad, bias2_grad, head_grad = call(
         final_kernel,
         [spec(conv1.shape, F32), spec((1, CH), F32), spec(conv2.shape, F32), spec((1, CH), F32), spec(head.shape, F32)],

time: 40.6 us -> 38.6 us (0.951)
  waiting for transfers between devices: 10.1 us -> 8.28 us
  local copies, waits for them, and re-layouts: 1.7 us -> 1.09 us
  Pallas kernels: 16.8 us -> 17.3 us
    ppermute x2, waiting for transfers between devices: 3.54 us -> 1.75 us  [body(): one, two = (lax.ppermute(one, 'gx', ahead), lax.ppermute(two, 'gx', behind))]
    unnamed x20, local copies, waits for them, and re-layouts: 0.67 us -> 0.06 us
    pallas_call x8 -> x9, Pallas kernels: 16.8 us -> 17.3 us  [call(): pl.pallas_call(kernel, out_shape=outs, in_specs=specs, out_specs=[whole]...]
  transfers between devices with their start and end apart: 7 -> 7, of which waited for: 5 -> 6; matrix products, arithmetic and copies ran while one was open for 3% -> 3% of each run, Pallas kernels for 19% -> 25%
where the time goes in v5:
time: 38.6 us; the launch traced here: 38.5 us
  Pallas kernels  17.3 us (45%)
  starting transfers between devices  10.8 us (28%)
  waiting for transfers between devices  8.28 us (21%)
  local copies, waits for them, and re-layouts  1.09 us (3%)
  between operations  0.89 us (2%)
    pallas_call x9, Pallas kernels, call(): pl.pallas_call(kernel, out_shape=outs, in_specs=specs, out_specs=[whole]...  17.3 us
    ppermute x3, waiting for transfers between devices, sum_rounds(): lax.ppermute(value, axis, [(i, i ^ step) for i in range(lax.axis_size(axi...  5.72 us
    ppermute x2, starting transfers between devices, body(): one, two = (lax.ppermute(one, 'gx', ahead), lax.ppermute(two, 'gx', behind))  4.2 us
    ppermute x3, starting transfers between devices, sum_rounds(): lax.ppermute(value, axis, [(i, i ^ step) for i in range(lax.axis_size(axi...  3.5 us
    ppermute x1, starting transfers between devices, body(): got = lax.ppermute(packed, 'gy', up + down)  3 us
    ppermute x2, waiting for transfers between devices, body(): one, two = (lax.ppermute(one, 'gx', ahead), lax.ppermute(two, 'gx', behind))  1.75 us
    pad x1, local copies, waits for them, and re-layouts, body(): jnp.pad(one, spare)  0.98 us
    ppermute x1, waiting for transfers between devices, body(): got = lax.ppermute(packed, 'gy', up + down)  0.81 us
  transfers between devices with their start and end apart: 7, of which 6 were waited for; matrix products, arithmetic and copies ran while one was open for 3% of the time, Pallas kernels for 25%

profile of v5, /device:TPU:0, one launch (start us, length us, event | category | flops | bytes accessed | tf_op | source)
XLA Modules:
  0.0 38.5 jit_solution(17995639690753260936)
XLA Ops:
  0.6 1.8 %shard_map.144 = (bf16[6,8,128]{2,1,0:T(8,128)(2,1)}, bf16[52,4,256]{2,1,0:T(4,128)(2,1)}, bf16[52,4,256]{2,1,0:T(4,128)(2,1)}) custom-call(s32[1]{0:T(128)} %bitcast.odd_ref, bf16[32,8,256]{2,1,0:T(8,128)(2,1)} %tracer_ref.1, bf16[32,8,256]{2,1,0:T(8,128)(2,1)} %cot_ref.3, f32[4,8,256]{2,1,0:T(8,128)} %own_ref.1), custom_call_target="tpu_custom_call" | custom-call | flops 2000000 | bytes 2000000 | tf_op jit(solution)/shard_map/pallas_call | solution.py:569
  2.5 3.0 %collective-permute-start = (bf16[6,8,128]{2,1,0:T(8,128)(2,1)}, bf16[6,8,128]{2,1,0:T(8,128)(2,1)S(1)}, u32[]{:S(2)}, u32[]{:S(2)}) collective-permute-start(bf16[6,8,128]{2,1,0:T(8,128)(2,1)} %get-tuple-element.47), channel_id=1, source_target_pairs={{0,2},{2,0},{1,3},{3,1},{4,6},{6,4},{5,7},{7,5},{8,10},{10,8},{9,1... | collective-permute-start | bytes 36872 | tf_op jit(solution)/shard_map/ppermute | solution.py:626
  5.5 0.0 copy-start.8
  5.5 1.0 %pad.7 = bf16[55,4,256]{2,1,0:T(4,128)(2,1)S(1)} pad(bf16[52,4,256]{2,1,0:T(4,128)(2,1)} %get-tuple-element.48, bf16[]{:T(256)} %constant.46.clone.1), padding=0_3x0_0x0_0 | pad | bytes 219138 | tf_op jit(solution)/shard_map/jit(_pad)/pad | solution.py:622
  6.5 0.0 copy-done.8
  6.5 0.0 copy-start
  6.5 0.0 copy-start.1
  6.6 0.8 %collective-permute-done = bf16[6,8,128]{2,1,0:T(8,128)(2,1)S(1)} collective-permute-done((bf16[6,8,128]{2,1,0:T(8,128)(2,1)}, bf16[6,8,128]{2,1,0:T(8,128)(2,1)S(1)}, u32[]{:S(2)}, u32[]{:S(2)}) %collective-permute-start) | collective-permute-done | bytes 12320 | tf_op jit(solution)/shard_map/ppermute | solution.py:626
  7.4 0.0 copy-start.9
  7.4 4.2 %collective-permute-start.2 = (bf16[55,4,256]{2,1,0:T(4,128)(2,1)S(1)}, bf16[55,4,256]{2,1,0:T(4,128)(2,1)S(1)}, u32[]{:S(2)}, u32[]{:S(2)}) collective-permute-start(bf16[55,4,256]{2,1,0:T(4,128)(2,1)S(1)} %get-tuple-element.89), channel_id=1, source_target_pairs={{0,12},{4,8},{8,4},{12,0},{1,13},{5,9},{9,5},{13,1},{2,14},{6,10},... | collective-permute-start | bytes 337928 | tf_op jit(solution)/shard_map/ppermute | solution.py:669
  11.6 0.0 collective-permute-start.1
  11.6 0.0 copy-done.9
  11.6 0.0 copy-done
  11.6 0.0 copy-done.1
  11.6 0.0 copy-start.3
  11.7 0.0 copy-start.4
  11.7 0.0 copy-start.5
  11.7 0.0 copy-start.6
  11.7 0.0 copy-start.7
  11.7 2.2 %shard_map.146 = (f32[18,8,384]{2,1,0:T(8,128)S(1)}, f32[2,32,8,384]{3,2,1,0:T(8,128)S(1)}) custom-call(s32[32]{0:T(128)S(1)} %broadcast_clamp_fusion.levels_ref, bf16[32,8,256]{2,1,0:T(8,128)(2,1)S(1)} %copy-done.1, bf16[32,8,256]{2,1,0:T(8,128)(2,1)S(1)} %copy-done, bf16[6,8,128]{2,1,0:T(8,128)(2,1)S(1)} %broadcast_select_fusion.2.side_ref), custom_call_target="tpu_custom_call" | custom-call | flops 2000000 | bytes 2000000 | tf_op jit(solution)/shard_map/pallas_call | solution.py:569
  13.9 0.0 copy-done.3
  13.9 0.0 copy-done.4
  14.0 0.0 copy-done.5
  14.0 0.0 copy-done.6
  14.0 0.0 copy-done.7
  14.0 0.6 %shard_map.145 = (bf16[64,96]{1,0:T(8,128)(2,1)S(1)}, bf16[64,576]{1,0:T(8,128)(2,1)S(1)}, bf16[64,576]{1,0:T(8,128)(2,1)S(1)}, bf16[32,576]{1,0:T(8,128)(2,1)S(...) custom-call(f32[32,36]{1,0:T(8,128)S(1)} %copy-done.4, ...), custom_call_target="tpu_custom_call" | custom-call | flops 2000000 | bytes 2000000 | tf_op jit(solution)/shard_map/pallas_call | solution.py:569
  14.6 0.3 collective-permute-done.2
  15.0 1.4 %collective-permute-done.1 = bf16[55,4,256]{2,1,0:T(4,128)(2,1)S(1)} collective-permute-done((bf16[55,4,256]{2,1,0:T(4,128)(2,1)S(1)}, bf16[55,4,256]{2,1,0:T(4,128)(2,1)S(1)}, u32[]{:S(2)}, u32[]{:S(2)}) %collective-permute-start.1) | collective-permute-done | bytes 112672 | tf_op jit(solution)/shard_map/ppermute | solution.py:669
  16.4 0.1 broadcast_select_fusion
  16.5 0.0 copy-start.2
  16.5 2.2 %shard_map.148.mine_ref = f32[18,16,384]{2,1,0:T(8,128)S(1)} custom-call(s32[32]{0:T(128)S(1)} %broadcast_clamp_fusion.levels_ref, f32[18,8,384]{2,1,0:T(8,128)S(1)} %get-tuple-element.68.inner_ref, f32[2,32,8,384]{3,2,1,0:T(8,128)S(1)} %get-tuple-element.69.edge_ref, bf16[6,8,128]{2,1,0:T(8,128)(2,1)S(1)} %broadcast_select_fusion.2.side_ref, ...), custom_call_target="tpu_custom_call" | custom-call | flops 2000000 | bytes 2000000 | tf_op jit(solution)/shard_map/pallas_call | solution.py:569
  18.7 0.1 collective-permute-start.3
  18.8 0.0 copy-done.2
  18.8 2.7 %shard_map.147 = (f32[32,5376]{1,0:T(8,128)S(1)}, f32[32,4608]{1,0:T(8,128)S(1)}, f32[18,16,384]{2,1,0:T(8,128)S(1)}, f32[4,16,384]{2,1,0:T(8,128)S(1)}) custom-call(f32[4,8,256]{2,1,0:T(8,128)S(1)} %copy-done.2, bf16[6,8,128]{2,1,0:T(8,128)(2,1)S(1)} %broadcast_select_fusion.2.side_ref, bf16[55,4,256]{2,1,0:T(4,128)(2,1)S(1)} %get-tuple-element.60.below_ref, ...), custom_call_target="tpu_custom_call" | custom-call | flops 2000000 | bytes 2000000 | tf_op jit(solution)/shard_map/pallas_call | solution.py:569
  21.4 0.0 collective-permute-done.3.other_ref
  21.5 2.6 %shard_map.149 = (f32[96,128]{1,0:T(8,128)S(1)}, f32[32,3840]{1,0:T(8,128)S(1)}) custom-call(f32[18,16,384]{2,1,0:T(8,128)S(1)} %shard_map.148.mine_ref, f32[18,16,384]{2,1,0:T(8,128)S(1)} %collective-permute-done.3.other_ref, f32[4,16,384]{2,1,0:T(8,128)S(1)} %get-tuple-element.67.wind_ref, f32[1,384]{1,0:T(1,128)S(1)} %select_convert_fusion.inside_ref, ...), custom_call_target="tpu_custom_call" | custom-call | flops 2000000 | bytes 2000000 | tf_op jit(solution)/shard_map/pallas_call | solution.py:569
  24.1 1.6 %collective-permute-start.4 = (f32[96,128]{1,0:T(8,128)S(1)}, f32[96,128]{1,0:T(8,128)S(1)}, u32[]{:S(2)}, u32[]{:S(2)}) collective-permute-start(f32[96,128]{1,0:T(8,128)S(1)} %get-tuple-element.74), channel_id=1, source_target_pairs={{0,2},{2,0},{1,3},{3,1},{4,6},{6,4},{5,7},{7,5},{8,10},{10,8},{9,1... | collective-permute-start | bytes 147464 | tf_op jit(solution)/shard_map/ppermute | solution.py:597
  25.6 1.5 %shard_map.150 = f32[4,8,256]{2,1,0:T(8,128)} custom-call(f32[18,16,384]{2,1,0:T(8,128)S(1)} %shard_map.148.mine_ref, f32[18,16,384]{2,1,0:T(8,128)S(1)} %collective-permute-done.3.other_ref, f32[4,16,384]{2,1,0:T(8,128)S(1)} %get-tuple-element.67.wind_ref, f32[32,3840]{1,0:T(8,128)S(1)} %get-tuple-element.75.d1_ref, ...), custom_call_target="tpu_custom_call" | custom-call | flops 2000000 | bytes 2000000 | tf_op jit(solution)/shard_map/pallas_call | solution.py:569
  27.1 1.2 %collective-permute-done.4 = f32[96,128]{1,0:T(8,128)S(1)} collective-permute-done((f32[96,128]{1,0:T(8,128)S(1)}, f32[96,128]{1,0:T(8,128)S(1)}, u32[]{:S(2)}, u32[]{:S(2)}) %collective-permute-start.4) | collective-permute-done | bytes 49184 | tf_op jit(solution)/shard_map/ppermute | solution.py:597
  28.2 1.4 %collective-permute-start.5 = (f32[96,128]{1,0:T(8,128)S(1)}, f32[96,128]{1,0:T(8,128)S(1)}, u32[]{:S(2)}, u32[]{:S(2)}) collective-permute-start(f32[96,128]{1,0:T(8,128)S(1)} %add.29), channel_id=1, source_target_pairs={{0,4},{4,0},{8,12},{12,8},{1,5},{5,1},{9,13},{13,9},{2,6},{6,2},{1... | collective-permute-start | bytes 147464 | tf_op jit(solution)/shard_map/ppermute | solution.py:597
  29.6 2.8 %collective-permute-done.5 = f32[96,128]{1,0:T(8,128)S(1)} collective-permute-done((f32[96,128]{1,0:T(8,128)S(1)}, f32[96,128]{1,0:T(8,128)S(1)}, u32[]{:S(2)}, u32[]{:S(2)}) %collective-permute-start.5) | collective-permute-done | bytes 49184 | tf_op jit(solution)/shard_map/ppermute | solution.py:597
  32.4 0.6 %collective-permute-start.6 = (f32[96,128]{1,0:T(8,128)S(1)}, f32[96,128]{1,0:T(8,128)S(1)}, u32[]{:S(2)}, u32[]{:S(2)}) collective-permute-start(f32[96,128]{1,0:T(8,128)S(1)} %add.30.mine_ref), channel_id=1, source_target_pairs={{0,8},{4,12},{8,0},{12,4},{1,9},{5,13},{9,1},{13,5},{2,10},{6,14},... | collective-permute-start | bytes 147464 | tf_op jit(solution)/shard_map/ppermute | solution.py:597
  33.0 2.7 %shard_map.151 = bf16[32,8,256]{2,1,0:T(8,128)(2,1)} custom-call(s32[32]{0:T(128)S(1)} %broadcast_clamp_fusion.levels_ref, f32[4,16,384]{2,1,0:T(8,128)S(1)} %get-tuple-element.67.wind_ref, f32[18,16,384]{2,1,0:T(8,128)S(1)} %get-tuple-element.79.corr_ref, bf16[32,8,256]{2,1,0:T(8,128)(2,1)S(1)} %copy-done, ...), custom_call_target="tpu_custom_call" | custom-call | flops 2000000 | bytes 2000000 | tf_op jit(solution)/shard_map/pallas_call | solution.py:569
  35.7 1.8 %collective-permute-done.6.other_ref = f32[96,128]{1,0:T(8,128)S(1)} collective-permute-done((f32[96,128]{1,0:T(8,128)S(1)}, f32[96,128]{1,0:T(8,128)S(1)}, u32[]{:S(2)}, u32[]{:S(2)}) %collective-permute-start.6) | collective-permute-done | bytes 49184 | tf_op jit(solution)/shard_map/ppermute | solution.py:597
  37.5 1.0 %shard_map.152 = (f32[32,36]{1,0:T(8,128)}, f32[1,32]{1,0:T(1,128)}, f32[32,288]{1,0:T(8,128)}, f32[1,32]{1,0:T(1,128)}, f32[18,32]{1,0:T(8,128)}) custom-call(f32[96,128]{1,0:T(8,128)S(1)} %add.30.mine_ref, f32[96,128]{1,0:T(8,128)S(1)} %collective-permute-done.6.other_ref), custom_call_target="tpu_custom_call" | custom-call | flops 200000 | bytes 2000000 | tf_op jit(solution)/shard_map/pallas_call | solution.py:569
  (9 shorter events, 0.1 us)
Async XLA Ops:
  2.5 4.9 %collective-permute-start = (bf16[6,8,128]{2,1,0:T(8,128)(2,1)}, bf16[6,8,128]{2,1,0:T(8,128)(2,1)S(1)}, u32[]{:S(2)}, u32[]{:S(2)}) collective-permute-start(bf16[6,8,128]{2,1,0:T(8,128)(2,1)} %get-tuple-element.47), channel_id=1, source_target_pairs={{0,2},{2,0},{1,3},{3,1},{4,6},{6,4},{5,7},{7,5},{8,10},{10,8},{9,1... | collective-permute-start | bytes 36872 | tf_op jit(solution)/shard_map/ppermute | solution.py:626
  5.5 1.0 %copy-start.8 = (bf16[52,4,256]{2,1,0:T(4,128)(2,1)S(1)}, bf16[52,4,256]{2,1,0:T(4,128)(2,1)}, u32[]{:S(2)}) copy-start(bf16[52,4,256]{2,1,0:T(4,128)(2,1)} %get-tuple-element.49) | copy-start | bytes 319492
  6.5 5.1 %copy-start = (bf16[32,8,256]{2,1,0:T(8,128)(2,1)S(1)}, bf16[32,8,256]{2,1,0:T(8,128)(2,1)}, u32[]{:S(2)}) copy-start(bf16[32,8,256]{2,1,0:T(8,128)(2,1)} %cot_ref.3) | copy-start | bytes 393220
  6.5 5.1 %copy-start.1 = (bf16[32,8,256]{2,1,0:T(8,128)(2,1)S(1)}, bf16[32,8,256]{2,1,0:T(8,128)(2,1)}, u32[]{:S(2)}) copy-start(bf16[32,8,256]{2,1,0:T(8,128)(2,1)} %tracer_ref.1) | copy-start | bytes 393220
  7.4 4.2 %copy-start.9 = (s32[32]{0:T(128)S(1)}, s32[32]{0:T(128)}, u32[]{:S(2)}) copy-start(s32[32]{0:T(128)} %param.12) | copy-start | bytes 388
  7.4 7.6 %collective-permute-start.2 = (bf16[55,4,256]{2,1,0:T(4,128)(2,1)S(1)}, bf16[55,4,256]{2,1,0:T(4,128)(2,1)S(1)}, u32[]{:S(2)}, u32[]{:S(2)}) collective-permute-start(bf16[55,4,256]{2,1,0:T(4,128)(2,1)S(1)} %get-tuple-element.89), channel_id=1, source_target_pairs={{0,12},{4,8},{8,4},{12,0},{1,13},{5,9},{9,5},{13,1},{2,14},{6,10},... | collective-permute-start | bytes 337928 | tf_op jit(solution)/shard_map/ppermute | solution.py:669
  11.6 4.8 %collective-permute-start.1 = (bf16[55,4,256]{2,1,0:T(4,128)(2,1)S(1)}, bf16[55,4,256]{2,1,0:T(4,128)(2,1)S(1)}, u32[]{:S(2)}, u32[]{:S(2)}) collective-permute-start(bf16[55,4,256]{2,1,0:T(4,128)(2,1)S(1)} %get-tuple-element.90), channel_id=1, source_target_pairs={{0,4},{4,0},{8,12},{12,8},{1,5},{5,1},{9,13},{13,9},{2,6},{6,2},{1... | collective-permute-start | bytes 337928 | tf_op jit(solution)/shard_map/ppermute | solution.py:669
  11.6 2.3 %copy-start.3 = (f32[32,288]{1,0:T(8,128)S(1)}, f32[32,288]{1,0:T(8,128)}, u32[]{:S(2)}) copy-start(f32[32,288]{1,0:T(8,128)} %c2_hbm) | copy-start | bytes 110596
  11.7 2.3 %copy-start.4 = (f32[32,36]{1,0:T(8,128)S(1)}, f32[32,36]{1,0:T(8,128)}, u32[]{:S(2)}) copy-start(f32[32,36]{1,0:T(8,128)} %c1_hbm) | copy-start | bytes 13828
  11.7 2.3 %copy-start.5 = (f32[18,32]{1,0:T(8,128)S(1)}, f32[18,32]{1,0:T(8,128)}, u32[]{:S(2)}) copy-start(f32[18,32]{1,0:T(8,128)} %head_hbm) | copy-start | bytes 6916
  11.7 2.3 %copy-start.6 = (f32[32]{0:T(128)S(1)}, f32[32]{0:T(128)}, u32[]{:S(2)}) copy-start(f32[32]{0:T(128)} %param.14) | copy-start | bytes 388
  11.7 2.3 %copy-start.7 = (f32[32]{0:T(128)S(1)}, f32[32]{0:T(128)}, u32[]{:S(2)}) copy-start(f32[32]{0:T(128)} %param.16) | copy-start | bytes 388
  16.5 2.3 %copy-start.2 = (f32[4,8,256]{2,1,0:T(8,128)S(1)}, f32[4,8,256]{2,1,0:T(8,128)}, u32[]{:S(2)}) copy-start(f32[4,8,256]{2,1,0:T(8,128)} %own_ref.1) | copy-start | bytes 98308
  18.7 2.8 %collective-permute-start.3 = (f32[18,16,384]{2,1,0:T(8,128)S(1)}, f32[18,16,384]{2,1,0:T(8,128)S(1)}, u32[]{:S(2)}, u32[]{:S(2)}) collective-permute-start(f32[18,16,384]{2,1,0:T(8,128)S(1)} %shard_map.148.mine_ref), channel_id=1, source_target_pairs={{0,1},{1,0},{2,3},{3,2},{4,5},{5,4},{6,7},{7,6},{8,9},{9,8},{10,11... | collective-permute-start | bytes 1327112 | tf_op jit(solution)/shard_map/ppermute | solution.py:694
  24.1 4.2 %collective-permute-start.4 = (f32[96,128]{1,0:T(8,128)S(1)}, f32[96,128]{1,0:T(8,128)S(1)}, u32[]{:S(2)}, u32[]{:S(2)}) collective-permute-start(f32[96,128]{1,0:T(8,128)S(1)} %get-tuple-element.74), channel_id=1, source_target_pairs={{0,2},{2,0},{1,3},{3,1},{4,6},{6,4},{5,7},{7,5},{8,10},{10,8},{9,1... | collective-permute-start | bytes 147464 | tf_op jit(solution)/shard_map/ppermute | solution.py:597
  28.2 4.1 %collective-permute-start.5 = (f32[96,128]{1,0:T(8,128)S(1)}, f32[96,128]{1,0:T(8,128)S(1)}, u32[]{:S(2)}, u32[]{:S(2)}) collective-permute-start(f32[96,128]{1,0:T(8,128)S(1)} %add.29), channel_id=1, source_target_pairs={{0,4},{4,0},{8,12},{12,8},{1,5},{5,1},{9,13},{13,9},{2,6},{6,2},{1... | collective-permute-start | bytes 147464 | tf_op jit(solution)/shard_map/ppermute | solution.py:597
  32.4 5.0 %collective-permute-start.6 = (f32[96,128]{1,0:T(8,128)S(1)}, f32[96,128]{1,0:T(8,128)S(1)}, u32[]{:S(2)}, u32[]{:S(2)}) collective-permute-start(f32[96,128]{1,0:T(8,128)S(1)} %add.30.mine_ref), channel_id=1, source_target_pairs={{0,8},{4,12},{8,0},{12,4},{1,9},{5,13},{9,1},{13,5},{2,10},{6,14},... | collective-permute-start | bytes 147464 | tf_op jit(solution)/shard_map/ppermute | solution.py:597

commit v6 on v5

--- a/solution.py
+++ b/solution.py
@@ -326,17 +326,48 @@
     return dot3(weights, rows(high_ref), rows(low_ref))
 
 
-def put_winds(wind_ref, stack_ref, first_row, rows):
-    width = wind_ref.shape[2]
+def put_winds(wind_ref, stack_ref, pairs, keep):
     count = wind_ref.shape[0]
-    for row in range(rows):
-        value = wind_ref[:, first_row + row, :]
+    for row, place in pairs:
+        value = wind_ref[:, row, :]
         for b in range(3):
-            stack_ref[b * count : (b + 1) * count, row * width : (row + 1) * width] = turn(value, STEPS[b], 1)
+            moved = turn(value, STEPS[b], 1)[:, :keep]
+            stack_ref[b * count : (b + 1) * count, place * keep : (place + 1) * keep] = moved
+
+
+def network_rows(weights, bias, high_ref, low_ref, row, width):
+    starts = (row, row + 1, row + 2)
+    return jnp.tanh(convolved(weights, high_ref, low_ref, starts, width) + bias)
+
+
+def inner_forward_kernel(
+    own_ref, side_ref, inside_ref, w1_ref, b1_ref, w2_ref, b2_ref,
+    first_ref, high_ref, low_ref, second_ref,
+    wind_ref, stack_ref, wind_high, wind_low,
+):
+    count, tile, width = wind_ref.shape
+    cols = own_ref.shape[2]
+    side = side_ref[side_ref.shape[0] // 2 - 1].astype(F32)
+    for i in range(count):
+        wind_ref[i, :, :cols] = own_ref[i]
+        wind_ref[i, :, cols:] = sum(placed(side, part * count + i) for part in range(3))
+    stack_ref[...] = jnp.zeros(stack_ref.shape, F32)
+    put_winds(wind_ref, stack_ref, [(row, row) for row in range(tile)], width)
+    wind_high[...], wind_low[...] = halves(stack_ref[...])
+    bias1, bias2 = b1_ref[...], b2_ref[...]
+    inside = jnp.concatenate([inside_ref[...]] * 2, axis=1)
+    for row in range(0, tile - 2, 2):
+        value = network_rows(w1_ref[...], bias1, wind_high, wind_low, row, width) * inside
+        first_ref[:, row * width : (row + 2) * width] = value
+        for part in range(2):
+            put_moved(high_ref, low_ref, row + part, value[:, part * width : (part + 1) * width], 1)
+    for row in range(0, tile - 4, 2):
+        second_ref[:, row * width : (row + 2) * width] = network_rows(w2_ref[...], bias2, high_ref, low_ref, row, width)
 
 
 def forward_kernel(
     own_ref, side_ref, below_ref, above_ref, inside_ref, w1_ref, b1_ref, w2_ref, b2_ref, head_ref,
+    inner_first, inner_high, inner_low, inner_second,
     first_ref, second_ref, corr_ref, wind_ref,
     stack_ref, wind_high, wind_low, high_ref, low_ref,
 ):
@@ -359,19 +390,29 @@
             wind_ref[i, HALO + tile :, where] = value[:HALO]
             wind_ref[i, :HALO, where] = value[HALO:]
     stack_ref[...] = jnp.zeros(stack_ref.shape, F32)
-    put_winds(wind_ref, stack_ref, 0, rows)
+    edge = HALO + 2
+    put_winds(wind_ref, stack_ref, [(row, row) for row in range(rows) if row < edge or row >= rows - edge], width)
     wind_high[...], wind_low[...] = halves(stack_ref[...])
     bias1, bias2 = b1_ref[...], b2_ref[...]
     inside = jnp.concatenate([inside_ref[...]] * 2, axis=1)
+    first_ref[:, HALO * width : (rows - 2 - HALO) * width] = inner_first[...]
+    for row in list(range(2)) + list(range(tile - 4, tile - 2)):
+        source = slice(row * width, (row + 1) * width)
+        target = slice((HALO + row) * width, (HALO + row + 1) * width)
+        high_ref[:, target] = inner_high[:, source]
+        low_ref[:, target] = inner_low[:, source]
     for row in range(0, rows - 2, 2):
-        starts = (row, row + 1, row + 2)
-        value = jnp.tanh(convolved(w1_ref[...], wind_high, wind_low, starts, width) + bias1) * inside
+        if HALO <= row < rows - 2 - HALO:
+            continue
+        value = network_rows(w1_ref[...], bias1, wind_high, wind_low, row, width) * inside
         first_ref[:, row * width : (row + 2) * width] = value
         for part in range(2):
             put_moved(high_ref, low_ref, row + part, value[:, part * width : (part + 1) * width], 1)
     for row in range(0, rows - 4, 2):
-        starts = (row, row + 1, row + 2)
-        value = jnp.tanh(convolved(w2_ref[...], high_ref, low_ref, starts, width) + bias2)
+        if HALO <= row < rows - 4 - HALO:
+            value = inner_second[:, (row - HALO) * width : (row - HALO + 2) * width]
+        else:
+            value = network_rows(w2_ref[...], bias2, high_ref, low_ref, row, width)
         second_ref[:, row * width : (row + 2) * width] = value
         high, low = halves(value)
         corr = dot3(head_ref[...], high, low)
@@ -395,20 +436,19 @@
     g_ref[...] = jnp.zeros(g_ref.shape, F32)
     for row in range(ring):
         g_ref[:nine, row * width : (row + 1) * width] = sum_ref[:, (row - 2) % wrap, :]
-    own = lax.broadcasted_iota(jnp.int32, (1, width), 1) < cols
     inside = inside_ref[...]
     for ref in (own2_ref, own1_ref):
         ref[...] = jnp.zeros(ref.shape, BF16)
     wind_stack[...] = jnp.zeros(wind_stack.shape, F32)
-    put_winds(wind_ref, wind_stack, 3, tile + 2)
+    put_winds(wind_ref, wind_stack, [(row + 3, row) for row in range(tile + 2)], cols)
     wind_stack[12:13, :] = jnp.ones((1, wind_stack.shape[1]), F32)
-    bias2 = jnp.zeros((CH, width), F32)
+    bias2 = jnp.zeros((CH, cols), F32)
 
     def put_own(ref, x, value):
-        for half, part in enumerate(halves(jnp.where(own, value, 0.0))):
+        for half, part in enumerate(halves(value[:, :cols])):
             for a in range(3):
                 start = (3 * half + a) * CH
-                ref[start : start + CH, (x + a) * width : (x + a + 1) * width] = part
+                ref[start : start + CH, (x + a) * cols : (x + a + 1) * cols] = part
 
     for row in range(0, ring, 2):
         where = slice(row * width, (row + 2) * width)
@@ -422,9 +462,12 @@
             x = row + part - 2
             if 0 <= x < tile:
                 put_own(own2_ref, x, value)
-                bias2 = bias2 + jnp.where(own, value, 0.0)
+                bias2 = bias2 + value[:, :cols]
     for row in range(tile + 2):
-        put_moved(act_ref.at[: 3 * CH], act_ref.at[3 * CH :], row, first_ref[:, (row + 2) * width : (row + 3) * width], 1)
+        for half, part in enumerate(halves(first_ref[:, (row + 2) * width : (row + 3) * width])):
+            for b in range(3):
+                start = (3 * half + b) * CH
+                act_ref[start : start + CH, row * cols : (row + 1) * cols] = turn(part, STEPS[b], 1)[:, :cols]
     par_ref[...] = jnp.zeros(par_ref.shape, F32)
     par_ref[:, : 3 * CH] = dot3_nt(act_ref[...], own2_ref[...])
     par_ref[:CH, 3 * CH + 16 : 3 * CH + 17] = jnp.sum(bias2, axis=1, keepdims=True)
@@ -440,10 +483,12 @@
             if 0 <= x < tile:
                 put_own(own1_ref, x, value)
     par_ref[:, 3 * CH : 3 * CH + 16] = dot3_nt(own1_ref[...], jnp.concatenate(halves(wind_stack[...]), axis=0))
-    mid = slice(2 * width, (2 + tile) * width)
-    own_rows = jnp.concatenate([own] * tile, axis=1)
-    grads = jnp.concatenate(halves(jnp.where(own_rows, g_ref[:, mid], 0.0)), axis=0)
-    raw = dot3_nt(jnp.concatenate(halves(second_ref[:, mid]), axis=0), grads)
+
+    def own_cells(ref):
+        rows = [ref[:, row * width : row * width + cols] for row in range(2, 2 + tile)]
+        return jnp.concatenate(halves(jnp.concatenate(rows, axis=1)), axis=0)
+
+    raw = dot3_nt(own_cells(second_ref), own_cells(g_ref))
     for level in range(LEVELS):
         rows = slice((level + 1) * CH, (level + 2) * CH)
         par_ref[rows, 3 * CH + 16 : 3 * CH + 25] = raw[:, 9 * level : 9 * level + 9]
@@ -683,7 +728,18 @@
         (levels, tracers, cotangent, side),
         {0: pltpu.SMEM},
     )
-    above, below, w1, w2, inner = lax.optimization_barrier((above, below, w1, w2, inner))
+    inner_net = call(
+        inner_forward_kernel,
+        [
+            spec((CH, (tile - 2) * width), F32),
+            spec((3 * CH, (tile - 2) * width), BF16),
+            spec((3 * CH, (tile - 2) * width), BF16),
+            spec((CH, (tile - 4) * width), F32),
+        ],
+        [vmem((n_wind, tile, width), F32), vmem((16, tile * width), F32)] + [vmem((16, tile * width), BF16)] * 2,
+        (winds, side, inside, w1, bias1_col, w2, bias2_col),
+    )
+    above, below, inner_net, inner = lax.optimization_barrier((above, below, inner_net, inner))
     mine = call(
         border_kernel,
         spec((9 * LEVELS, rows, width), F32),
@@ -703,7 +759,7 @@
         [vmem((16, rows * width), F32)]
         + [vmem((16, rows * width), BF16)] * 2
         + [vmem((3 * CH, (rows - 2) * width), BF16)] * 2,
-        (winds, side, below, above, inside, w1, bias1_col, w2, bias2_col, head_w),
+        (winds, side, below, above, inside, w1, bias1_col, w2, bias2_col, head_w) + tuple(inner_net),
     )
     ring, own = (tile + 4) * width, (tile + 2) * width
     params, delta = call(
@@ -711,8 +767,8 @@
         [spec((3 * CH, LANES), F32), spec((CH, own), F32)],
         [vmem((9 * LEVELS, rows, width), F32), vmem((CH, ring), F32)]
         + [vmem((3 * CH, ring), BF16)] * 2
-        + [vmem((6 * CH, own), BF16)] * 3
-        + [vmem((16, own), F32)],
+        + [vmem((6 * CH, (tile + 2) * cols), BF16)] * 3
+        + [vmem((16, (tile + 2) * cols), F32)],
         (mine, other, wind_ext, inside, first, second, head_t, w2b),
     )
     wind_grad = call(

time: 38.6 us -> 37.5 us (0.972)
  waiting for transfers between devices: 8.28 us -> 6.44 us
  local copies, waits for them, and re-layouts: 1.09 us -> 1.84 us
    ppermute x2, waiting for transfers between devices: 1.75 us -> 0.78 us  [body(): one, two = (lax.ppermute(one, 'gx', ahead), lax.ppermute(two, 'gx', behind))]
    unnamed x20, local copies, waits for them, and re-layouts: 0.06 us -> 0.81 us
    ppermute x1, waiting for transfers between devices: 0.81 us -> 0.13 us  [body(): got = lax.ppermute(packed, 'gy', up + down)]
    pallas_call x9 -> x10, Pallas kernels: 17.3 us -> 17 us  [call(): pl.pallas_call(kernel, out_shape=outs, in_specs=specs, out_specs=[whole]...]
  transfers between devices with their start and end apart: 7 -> 7, of which waited for: 6 -> 5; matrix products, arithmetic and copies ran while one was open for 3% -> 3% of each run, Pallas kernels for 25% -> 27%
where the time goes in v6:
time: 37.5 us; the launch traced here: 37.3 us
  Pallas kernels  17 us (45%)
  starting transfers between devices  11 us (29%)
  waiting for transfers between devices  6.44 us (17%)
  local copies, waits for them, and re-layouts  1.84 us (5%)
  between operations  0.9 us (2%)
    pallas_call x10, Pallas kernels, call(): pl.pallas_call(kernel, out_shape=outs, in_specs=specs, out_specs=[whole]...  17 us
    ppermute x3, waiting for transfers between devices, sum_rounds(): lax.ppermute(value, axis, [(i, i ^ step) for i in range(lax.axis_size(axi...  5.53 us
    ppermute x2, starting transfers between devices, body(): one, two = (lax.ppermute(one, 'gx', ahead), lax.ppermute(two, 'gx', behind))  4.2 us
    ppermute x3, starting transfers between devices, sum_rounds(): lax.ppermute(value, axis, [(i, i ^ step) for i in range(lax.axis_size(axi...  3.71 us
    ppermute x1, starting transfers between devices, body(): got = lax.ppermute(packed, 'gy', up + down)  3 us
    pad x1, local copies, waits for them, and re-layouts, body(): jnp.pad(one, spare)  0.98 us
    unnamed x20, local copies, waits for them, and re-layouts  0.81 us
    ppermute x2, waiting for transfers between devices, body(): one, two = (lax.ppermute(one, 'gx', ahead), lax.ppermute(two, 'gx', behind))  0.78 us
  transfers between devices with their start and end apart: 7, of which 5 were waited for; matrix products, arithmetic and copies ran while one was open for 3% of the time, Pallas kernels for 27%

profile of v6, /device:TPU:0, one launch (start us, length us, event | category | flops | bytes accessed | tf_op | source)
XLA Modules:
  0.0 37.3 jit_solution(5571250995384388307)
XLA Ops:
  0.6 1.8 %shard_map.144 = (bf16[6,8,128]{2,1,0:T(8,128)(2,1)}, bf16[52,4,256]{2,1,0:T(4,128)(2,1)}, bf16[52,4,256]{2,1,0:T(4,128)(2,1)}) custom-call(s32[1]{0:T(128)} %bitcast.odd_ref, bf16[32,8,256]{2,1,0:T(8,128)(2,1)} %tracer_ref.1, bf16[32,8,256]{2,1,0:T(8,128)(2,1)} %cot_ref.3, f32[4,8,256]{2,1,0:T(8,128)} %own_ref.3), custom_call_target="tpu_custom_call" | custom-call | flops 2000000 | bytes 2000000 | tf_op jit(solution)/shard_map/pallas_call | solution.py:614
  2.5 3.0 %collective-permute-start = (bf16[6,8,128]{2,1,0:T(8,128)(2,1)}, bf16[6,8,128]{2,1,0:T(8,128)(2,1)S(1)}, u32[]{:S(2)}, u32[]{:S(2)}) collective-permute-start(bf16[6,8,128]{2,1,0:T(8,128)(2,1)} %get-tuple-element.53), channel_id=1, source_target_pairs={{0,2},{2,0},{1,3},{3,1},{4,6},{6,4},{5,7},{7,5},{8,10},{10,8},{9,1... | collective-permute-start | bytes 36872 | tf_op jit(solution)/shard_map/ppermute | solution.py:671
  5.5 0.0 copy-start.9
  5.5 0.7 %copy-done.9 = s32[32]{0:T(128)S(1)} copy-done((s32[32]{0:T(128)S(1)}, s32[32]{0:T(128)}, u32[]{:S(2)}) %copy-start.9) | copy-done | bytes 152
  6.2 0.0 copy-start.8
  6.2 1.0 %pad.7 = bf16[55,4,256]{2,1,0:T(4,128)(2,1)S(1)} pad(bf16[52,4,256]{2,1,0:T(4,128)(2,1)} %get-tuple-element.54, bf16[]{:T(256)} %constant.46.clone.1), padding=0_3x0_0x0_0 | pad | bytes 219138 | tf_op jit(solution)/shard_map/jit(_pad)/pad | solution.py:667
  7.2 0.0 copy-done.8
  7.2 0.0 copy-start
  7.2 0.0 copy-start.1
  7.2 0.1 collective-permute-done
  7.4 4.2 %collective-permute-start.2 = (bf16[55,4,256]{2,1,0:T(4,128)(2,1)S(1)}, bf16[55,4,256]{2,1,0:T(4,128)(2,1)S(1)}, u32[]{:S(2)}, u32[]{:S(2)}) collective-permute-start(bf16[55,4,256]{2,1,0:T(4,128)(2,1)S(1)} %get-tuple-element.101), channel_id=1, source_target_pairs={{0,12},{4,8},{8,4},{12,0},{1,13},{5,9},{9,5},{13,1},{2,14},{6,10},... | collective-permute-start | bytes 337928 | tf_op jit(solution)/shard_map/ppermute | solution.py:714
  11.6 0.0 collective-permute-start.1
  11.6 0.0 copy-done
  11.6 0.0 copy-done.1
  11.6 0.0 copy-start.3
  11.6 0.0 copy-start.4
  11.7 0.0 copy-start.5
  11.7 0.0 copy-start.6
  11.7 0.0 copy-start.7
  11.7 2.3 %shard_map.147 = (f32[18,8,384]{2,1,0:T(8,128)S(1)}, f32[2,32,8,384]{3,2,1,0:T(8,128)S(1)}) custom-call(s32[32]{0:T(128)S(1)} %broadcast_clamp_fusion.levels_ref, bf16[32,8,256]{2,1,0:T(8,128)(2,1)S(1)} %copy-done.1, bf16[32,8,256]{2,1,0:T(8,128)(2,1)S(1)} %copy-done, bf16[6,8,128]{2,1,0:T(8,128)(2,1)S(1)} %broadcast_select_fusion.2.side_ref), custom_call_target="tpu_custom_call" | custom-call | flops 2000000 | bytes 2000000 | tf_op jit(solution)/shard_map/pallas_call | solution.py:614
  14.0 0.0 copy-done.3
  14.0 0.0 copy-done.4
  14.0 0.0 copy-done.5
  14.0 0.0 copy-done.6
  14.0 0.0 copy-done.7
  14.0 0.0 copy-start.2
  14.0 0.6 %shard_map.145 = (bf16[64,96]{1,0:T(8,128)(2,1)S(1)}, bf16[64,576]{1,0:T(8,128)(2,1)S(1)}, bf16[64,576]{1,0:T(8,128)(2,1)S(1)}, bf16[32,576]{1,0:T(8,128)(2,1)S(...) custom-call(f32[32,36]{1,0:T(8,128)S(1)} %copy-done.4, ...), custom_call_target="tpu_custom_call" | custom-call | flops 2000000 | bytes 2000000 | tf_op jit(solution)/shard_map/pallas_call | solution.py:614
  14.7 0.1 copy-done.2
  14.8 0.9 %shard_map.146 = (f32[32,2304]{1,0:T(8,128)S(1)}, bf16[96,2304]{1,0:T(8,128)(2,1)S(1)}, bf16[96,2304]{1,0:T(8,128)(2,1)S(1)}, f32[32,1536]{1,0:T(8,128)S(1)}) custom-call(f32[4,8,256]{2,1,0:T(8,128)S(1)} %copy-done.2, bf16[6,8,128]{2,1,0:T(8,128)(2,1)S(1)} %broadcast_select_fusion.2.side_ref, f32[1,384]{1,0:T(1,128)S(1)} %select_convert_fusion.inside_ref, ...), custom_call_target="tpu_custom_call" | custom-call | flops 2000000 | bytes 2000000 | tf_op jit(solution)/shard_map/pallas_call | solution.py:614
  15.7 0.0 collective-permute-done.2
  15.7 0.8 %collective-permute-done.1 = bf16[55,4,256]{2,1,0:T(4,128)(2,1)S(1)} collective-permute-done((bf16[55,4,256]{2,1,0:T(4,128)(2,1)S(1)}, bf16[55,4,256]{2,1,0:T(4,128)(2,1)S(1)}, u32[]{:S(2)}, u32[]{:S(2)}) %collective-permute-start.1) | collective-permute-done | bytes 112672 | tf_op jit(solution)/shard_map/ppermute | solution.py:714
  16.5 0.1 broadcast_select_fusion
  16.6 2.2 %shard_map.149.mine_ref = f32[18,16,384]{2,1,0:T(8,128)S(1)} custom-call(s32[32]{0:T(128)S(1)} %broadcast_clamp_fusion.levels_ref, f32[18,8,384]{2,1,0:T(8,128)S(1)} %get-tuple-element.80.inner_ref, f32[2,32,8,384]{3,2,1,0:T(8,128)S(1)} %get-tuple-element.81.edge_ref, bf16[6,8,128]{2,1,0:T(8,128)(2,1)S(1)} %broadcast_select_fusion.2.side_ref, ...), custom_call_target="tpu_custom_call" | custom-call | flops 2000000 | bytes 2000000 | tf_op jit(solution)/shard_map/pallas_call | solution.py:614
  18.8 0.1 collective-permute-start.3
  18.8 2.0 %shard_map.148 = (f32[32,5376]{1,0:T(8,128)S(1)}, f32[32,4608]{1,0:T(8,128)S(1)}, f32[18,16,384]{2,1,0:T(8,128)S(1)}, f32[4,16,384]{2,1,0:T(8,128)S(1)}) custom-call(f32[4,8,256]{2,1,0:T(8,128)S(1)} %copy-done.2, bf16[6,8,128]{2,1,0:T(8,128)(2,1)S(1)} %broadcast_select_fusion.2.side_ref, bf16[55,4,256]{2,1,0:T(4,128)(2,1)S(1)} %get-tuple-element.72.below_ref, ...), custom_call_target="tpu_custom_call" | custom-call | flops 2000000 | bytes 2000000 | tf_op jit(solution)/shard_map/pallas_call | solution.py:614
  20.9 0.0 collective-permute-done.3.other_ref
  20.9 2.0 %shard_map.150 = (f32[96,128]{1,0:T(8,128)S(1)}, f32[32,3840]{1,0:T(8,128)S(1)}) custom-call(f32[18,16,384]{2,1,0:T(8,128)S(1)} %shard_map.149.mine_ref, f32[18,16,384]{2,1,0:T(8,128)S(1)} %collective-permute-done.3.other_ref, f32[4,16,384]{2,1,0:T(8,128)S(1)} %get-tuple-element.79.wind_ref, f32[1,384]{1,0:T(1,128)S(1)} %select_convert_fusion.inside_ref, ...), custom_call_target="tpu_custom_call" | custom-call | flops 2000000 | bytes 2000000 | tf_op jit(solution)/shard_map/pallas_call | solution.py:614
  22.9 1.5 %collective-permute-start.4 = (f32[96,128]{1,0:T(8,128)S(1)}, f32[96,128]{1,0:T(8,128)S(1)}, u32[]{:S(2)}, u32[]{:S(2)}) collective-permute-start(f32[96,128]{1,0:T(8,128)S(1)} %get-tuple-element.86), channel_id=1, source_target_pairs={{0,2},{2,0},{1,3},{3,1},{4,6},{6,4},{5,7},{7,5},{8,10},{10,8},{9,1... | collective-permute-start | bytes 147464 | tf_op jit(solution)/shard_map/ppermute | solution.py:642
  24.4 1.5 %shard_map.151 = f32[4,8,256]{2,1,0:T(8,128)} custom-call(f32[18,16,384]{2,1,0:T(8,128)S(1)} %shard_map.149.mine_ref, f32[18,16,384]{2,1,0:T(8,128)S(1)} %collective-permute-done.3.other_ref, f32[4,16,384]{2,1,0:T(8,128)S(1)} %get-tuple-element.79.wind_ref, f32[32,3840]{1,0:T(8,128)S(1)} %get-tuple-element.87.d1_ref, ...), custom_call_target="tpu_custom_call" | custom-call | flops 2000000 | bytes 2000000 | tf_op jit(solution)/shard_map/pallas_call | solution.py:614
  25.8 1.3 %collective-permute-done.4 = f32[96,128]{1,0:T(8,128)S(1)} collective-permute-done((f32[96,128]{1,0:T(8,128)S(1)}, f32[96,128]{1,0:T(8,128)S(1)}, u32[]{:S(2)}, u32[]{:S(2)}) %collective-permute-start.4) | collective-permute-done | bytes 49184 | tf_op jit(solution)/shard_map/ppermute | solution.py:642
  27.1 1.5 %collective-permute-start.5 = (f32[96,128]{1,0:T(8,128)S(1)}, f32[96,128]{1,0:T(8,128)S(1)}, u32[]{:S(2)}, u32[]{:S(2)}) collective-permute-start(f32[96,128]{1,0:T(8,128)S(1)} %add.29), channel_id=1, source_target_pairs={{0,4},{4,0},{8,12},{12,8},{1,5},{5,1},{9,13},{13,9},{2,6},{6,2},{1... | collective-permute-start | bytes 147464 | tf_op jit(solution)/shard_map/ppermute | solution.py:642
  28.7 2.6 %collective-permute-done.5 = f32[96,128]{1,0:T(8,128)S(1)} collective-permute-done((f32[96,128]{1,0:T(8,128)S(1)}, f32[96,128]{1,0:T(8,128)S(1)}, u32[]{:S(2)}, u32[]{:S(2)}) %collective-permute-start.5) | collective-permute-done | bytes 49184 | tf_op jit(solution)/shard_map/ppermute | solution.py:642
  31.3 0.7 %collective-permute-start.6 = (f32[96,128]{1,0:T(8,128)S(1)}, f32[96,128]{1,0:T(8,128)S(1)}, u32[]{:S(2)}, u32[]{:S(2)}) collective-permute-start(f32[96,128]{1,0:T(8,128)S(1)} %add.30.mine_ref), channel_id=1, source_target_pairs={{0,8},{4,12},{8,0},{12,4},{1,9},{5,13},{9,1},{13,5},{2,10},{6,14},... | collective-permute-start | bytes 147464 | tf_op jit(solution)/shard_map/ppermute | solution.py:642
  32.0 2.7 %shard_map.152 = bf16[32,8,256]{2,1,0:T(8,128)(2,1)} custom-call(s32[32]{0:T(128)S(1)} %broadcast_clamp_fusion.levels_ref, f32[4,16,384]{2,1,0:T(8,128)S(1)} %get-tuple-element.79.wind_ref, f32[18,16,384]{2,1,0:T(8,128)S(1)} %get-tuple-element.91.corr_ref, bf16[32,8,256]{2,1,0:T(8,128)(2,1)S(1)} %copy-done, ...), custom_call_target="tpu_custom_call" | custom-call | flops 2000000 | bytes 2000000 | tf_op jit(solution)/shard_map/pallas_call | solution.py:614
  34.7 1.6 %collective-permute-done.6.other_ref = f32[96,128]{1,0:T(8,128)S(1)} collective-permute-done((f32[96,128]{1,0:T(8,128)S(1)}, f32[96,128]{1,0:T(8,128)S(1)}, u32[]{:S(2)}, u32[]{:S(2)}) %collective-permute-start.6) | collective-permute-done | bytes 49184 | tf_op jit(solution)/shard_map/ppermute | solution.py:642
  36.3 1.0 %shard_map.153 = (f32[32,36]{1,0:T(8,128)}, f32[1,32]{1,0:T(1,128)}, f32[32,288]{1,0:T(8,128)}, f32[1,32]{1,0:T(1,128)}, f32[18,32]{1,0:T(8,128)}) custom-call(f32[96,128]{1,0:T(8,128)S(1)} %add.30.mine_ref, f32[96,128]{1,0:T(8,128)S(1)} %collective-permute-done.6.other_ref), custom_call_target="tpu_custom_call" | custom-call | flops 200000 | bytes 2000000 | tf_op jit(solution)/shard_map/pallas_call | solution.py:614
  (9 shorter events, 0.1 us)
Async XLA Ops:
  2.5 4.9 %collective-permute-start = (bf16[6,8,128]{2,1,0:T(8,128)(2,1)}, bf16[6,8,128]{2,1,0:T(8,128)(2,1)S(1)}, u32[]{:S(2)}, u32[]{:S(2)}) collective-permute-start(bf16[6,8,128]{2,1,0:T(8,128)(2,1)} %get-tuple-element.53), channel_id=1, source_target_pairs={{0,2},{2,0},{1,3},{3,1},{4,6},{6,4},{5,7},{7,5},{8,10},{10,8},{9,1... | collective-permute-start | bytes 36872 | tf_op jit(solution)/shard_map/ppermute | solution.py:671
  5.5 0.7 %copy-start.9 = (s32[32]{0:T(128)S(1)}, s32[32]{0:T(128)}, u32[]{:S(2)}) copy-start(s32[32]{0:T(128)} %param.12) | copy-start | bytes 388
  6.2 1.0 %copy-start.8 = (bf16[52,4,256]{2,1,0:T(4,128)(2,1)S(1)}, bf16[52,4,256]{2,1,0:T(4,128)(2,1)}, u32[]{:S(2)}) copy-start(bf16[52,4,256]{2,1,0:T(4,128)(2,1)} %get-tuple-element.55) | copy-start | bytes 319492
  7.2 4.4 %copy-start = (bf16[32,8,256]{2,1,0:T(8,128)(2,1)S(1)}, bf16[32,8,256]{2,1,0:T(8,128)(2,1)}, u32[]{:S(2)}) copy-start(bf16[32,8,256]{2,1,0:T(8,128)(2,1)} %cot_ref.3) | copy-start | bytes 393220
  7.2 4.4 %copy-start.1 = (bf16[32,8,256]{2,1,0:T(8,128)(2,1)S(1)}, bf16[32,8,256]{2,1,0:T(8,128)(2,1)}, u32[]{:S(2)}) copy-start(bf16[32,8,256]{2,1,0:T(8,128)(2,1)} %tracer_ref.1) | copy-start | bytes 393220
  7.4 8.3 %collective-permute-start.2 = (bf16[55,4,256]{2,1,0:T(4,128)(2,1)S(1)}, bf16[55,4,256]{2,1,0:T(4,128)(2,1)S(1)}, u32[]{:S(2)}, u32[]{:S(2)}) collective-permute-start(bf16[55,4,256]{2,1,0:T(4,128)(2,1)S(1)} %get-tuple-element.101), channel_id=1, source_target_pairs={{0,12},{4,8},{8,4},{12,0},{1,13},{5,9},{9,5},{13,1},{2,14},{6,10},... | collective-permute-start | bytes 337928 | tf_op jit(solution)/shard_map/ppermute | solution.py:714
  11.6 4.9 %collective-permute-start.1 = (bf16[55,4,256]{2,1,0:T(4,128)(2,1)S(1)}, bf16[55,4,256]{2,1,0:T(4,128)(2,1)S(1)}, u32[]{:S(2)}, u32[]{:S(2)}) collective-permute-start(bf16[55,4,256]{2,1,0:T(4,128)(2,1)S(1)} %get-tuple-element.102), channel_id=1, source_target_pairs={{0,4},{4,0},{8,12},{12,8},{1,5},{5,1},{9,13},{13,9},{2,6},{6,2},{1... | collective-permute-start | bytes 337928 | tf_op jit(solution)/shard_map/ppermute | solution.py:714
  11.6 2.3 %copy-start.3 = (f32[32,288]{1,0:T(8,128)S(1)}, f32[32,288]{1,0:T(8,128)}, u32[]{:S(2)}) copy-start(f32[32,288]{1,0:T(8,128)} %c2_hbm) | copy-start | bytes 110596
  11.6 2.3 %copy-start.4 = (f32[32,36]{1,0:T(8,128)S(1)}, f32[32,36]{1,0:T(8,128)}, u32[]{:S(2)}) copy-start(f32[32,36]{1,0:T(8,128)} %c1_hbm) | copy-start | bytes 13828
  11.7 2.3 %copy-start.5 = (f32[18,32]{1,0:T(8,128)S(1)}, f32[18,32]{1,0:T(8,128)}, u32[]{:S(2)}) copy-start(f32[18,32]{1,0:T(8,128)} %head_hbm) | copy-start | bytes 6916
  11.7 2.3 %copy-start.6 = (f32[32]{0:T(128)S(1)}, f32[32]{0:T(128)}, u32[]{:S(2)}) copy-start(f32[32]{0:T(128)} %param.14) | copy-start | bytes 388
  11.7 2.3 %copy-start.7 = (f32[32]{0:T(128)S(1)}, f32[32]{0:T(128)}, u32[]{:S(2)}) copy-start(f32[32]{0:T(128)} %param.16) | copy-start | bytes 388
  14.0 0.8 %copy-start.2 = (f32[4,8,256]{2,1,0:T(8,128)S(1)}, f32[4,8,256]{2,1,0:T(8,128)}, u32[]{:S(2)}) copy-start(f32[4,8,256]{2,1,0:T(8,128)} %own_ref.3) | copy-start | bytes 98308
  18.8 2.1 %collective-permute-start.3 = (f32[18,16,384]{2,1,0:T(8,128)S(1)}, f32[18,16,384]{2,1,0:T(8,128)S(1)}, u32[]{:S(2)}, u32[]{:S(2)}) collective-permute-start(f32[18,16,384]{2,1,0:T(8,128)S(1)} %shard_map.149.mine_ref), channel_id=1, source_target_pairs={{0,1},{1,0},{2,3},{3,2},{4,5},{5,4},{6,7},{7,6},{8,9},{9,8},{10,11... | collective-permute-start | bytes 1327112 | tf_op jit(solution)/shard_map/ppermute | solution.py:750
  22.9 4.2 %collective-permute-start.4 = (f32[96,128]{1,0:T(8,128)S(1)}, f32[96,128]{1,0:T(8,128)S(1)}, u32[]{:S(2)}, u32[]{:S(2)}) collective-permute-start(f32[96,128]{1,0:T(8,128)S(1)} %get-tuple-element.86), channel_id=1, source_target_pairs={{0,2},{2,0},{1,3},{3,1},{4,6},{6,4},{5,7},{7,5},{8,10},{10,8},{9,1... | collective-permute-start | bytes 147464 | tf_op jit(solution)/shard_map/ppermute | solution.py:642
  27.1 4.2 %collective-permute-start.5 = (f32[96,128]{1,0:T(8,128)S(1)}, f32[96,128]{1,0:T(8,128)S(1)}, u32[]{:S(2)}, u32[]{:S(2)}) collective-permute-start(f32[96,128]{1,0:T(8,128)S(1)} %add.29), channel_id=1, source_target_pairs={{0,4},{4,0},{8,12},{12,8},{1,5},{5,1},{9,13},{13,9},{2,6},{6,2},{1... | collective-permute-start | bytes 147464 | tf_op jit(solution)/shard_map/ppermute | solution.py:642
  31.3 5.0 %collective-permute-start.6 = (f32[96,128]{1,0:T(8,128)S(1)}, f32[96,128]{1,0:T(8,128)S(1)}, u32[]{:S(2)}, u32[]{:S(2)}) collective-permute-start(f32[96,128]{1,0:T(8,128)S(1)} %add.30.mine_ref), channel_id=1, source_target_pairs={{0,8},{4,12},{8,0},{12,4},{1,9},{5,13},{9,1},{13,5},{2,10},{6,14},... | collective-permute-start | bytes 147464 | tf_op jit(solution)/shard_map/ppermute | solution.py:642

commit v7 on v6

--- a/solution.py
+++ b/solution.py
@@ -69,9 +69,16 @@
 
 def cot_strip(strip, spare, part):
     slot = lax.broadcasted_iota(jnp.int32, strip.shape, 0)
-    value = jnp.where(slot == 0, turn(strip, 3, 0), jnp.where(slot == 6, turn(strip, -2, 0), 0.0))
+    value = jnp.where(slot == 0, turn(strip, 3, 0), jnp.where(slot == 7, turn(strip, -3, 0), 0.0))
     value = jnp.where(slot == 1, spare[part : part + 1], value)
-    return jnp.where(slot == 7, spare[HALO + part : HALO + part + 1], value)
+    return jnp.where(slot == 6, spare[HALO + part : HALO + part + 1], value)
+
+
+def in_slots(row, *pairs):
+    value = jnp.zeros(row.shape, F32)
+    for slot, part in pairs:
+        value = jnp.where(row == slot, part, value)
+    return value
 
 
 def run_copies(sources, targets, sems):
@@ -111,10 +118,10 @@
                 put(
                     t,
                     jnp.concatenate([tracer[:3], cot[:1]], axis=0),
-                    jnp.concatenate([cot[tile - 2 : tile - 1], tracer[tile - 3 :]], axis=0),
+                    jnp.concatenate([cot[tile - 1 :], tracer[tile - 3 :]], axis=0),
                 )
                 first.append(cot[1:2])
-                last.append(cot[tile - 1 :])
+                last.append(cot[tile - 2 : tile - 1])
             put(count + t // 4, jnp.concatenate(first, axis=0), jnp.concatenate(last, axis=0))
         out_ref[group] = totals[0].astype(BF16)
         out_ref[groups + 1 + group] = totals[1].astype(BF16)
@@ -263,10 +270,9 @@
     slot_sums(moved_ref, held_ref, lower, count, store)
 
 
-def border_kernel(levels_ref, inner_ref, edge_ref, side_ref, below_ref, above_ref, out_ref, moved_ref, held_ref):
+def border_kernel(levels_ref, edge_ref, side_ref, below_ref, above_ref, out_ref, moved_ref, held_ref):
     count = levels_ref.shape[0]
     slots, rows, width = moved_ref.shape[1:]
-    tile = inner_ref.shape[1]
     channels = below_ref.shape[0] - side_ref.shape[0] // 2
     groups = count // GROUP
     row = lax.broadcasted_iota(jnp.int32, (rows, width), 0)
@@ -285,31 +291,43 @@
                 strip = rows_of(below_ref[t], above_ref[t])
                 field = jnp.concatenate([strip, placed(near, j)], axis=1)
                 field = jnp.where((row == 3) | (row == 4), edge_ref[0, t], field)
-                cot = jnp.concatenate([cot_strip(strip, spare, part), placed(far, j)], axis=1)
                 edge = edge_ref[1, t]
                 for b in range(3):
                     moved_ref[b, slot] = turn(field, STEPS[b], 1)
-                held_ref[0, slot] = jnp.where(row == 7, edge, jnp.where(row == 3, turn(cot, -3, 0), turn(cot, 1, 0)))
-                held_ref[1, slot] = cot
-                held_ref[2, slot] = jnp.where(row == 0, edge, jnp.where(row == 4, turn(cot, 3, 0), turn(cot, -1, 0)))
+                next0, next1 = strip[3:4], spare[part : part + 1]
+                back1, back2 = strip[4:5], spare[HALO + part : HALO + part + 1]
+                where = row[:, : strip.shape[1]]
+                later = in_slots(where, (0, next1), (3, next0), (5, back2), (6, back1))
+                cot = in_slots(where, (0, next0), (1, next1), (6, back2), (7, back1))
+                sooner = in_slots(where, (1, next0), (2, next1), (4, back1), (7, back2))
+                tail, place = placed(far, j), row[:, :LANES]
+                tail_later = jnp.where(place == 3, turn(tail, -3, 0), turn(tail, 1, 0))
+                tail_sooner = jnp.where(place == 4, turn(tail, 3, 0), turn(tail, -1, 0))
+                later = jnp.concatenate([later, tail_later], axis=1)
+                sooner = jnp.concatenate([sooner, tail_sooner], axis=1)
+                held_ref[0, slot] = jnp.where(row == 7, edge, later)
+                held_ref[1, slot] = jnp.concatenate([cot, tail], axis=1)
+                held_ref[2, slot] = jnp.where(row == 0, edge, sooner)
             return lower
 
         lower = lax.fori_loop(0, GROUP // 4, fill, lower)
     gap_zeroed((moved_ref, held_ref), lower)
-    place = row[:, :LANES]
 
     def store(level, k, lanes, total):
-        index, step = 9 * level + k, STEPS[k // 3]
-        inner = inner_ref[index, :, lanes]
-        if step:
-            last = 7 if step == 1 else 0
-            shifted = turn(total, step, 0)
-            inner = inner + jnp.where(place == last, shifted, 0.0)
-            total = jnp.where(place == last, turn(total, 5 if step == 1 else 3, 0), shifted)
-        out_ref[index, :tile, lanes] = inner
-        out_ref[index, tile:, lanes] = total
+        out_ref[9 * level + k, :, lanes] = total
 
     slot_sums(moved_ref, held_ref, lower, count, store)
+
+
+def merged(inner, border, k):
+    step = STEPS[k // 3]
+    if not step:
+        return inner, border
+    place = lax.broadcasted_iota(jnp.int32, border.shape, 0)
+    last = place == (7 if step == 1 else 0)
+    shifted = turn(border, step, 0)
+    strip = jnp.where(last, turn(border, 5 if step == 1 else 3, 0), shifted)
+    return inner + jnp.where(last, shifted, 0.0), strip
 
 
 def put_moved(high_ref, low_ref, row, value, sign):
@@ -366,9 +384,9 @@
 
 
 def forward_kernel(
-    own_ref, side_ref, below_ref, above_ref, inside_ref, w1_ref, b1_ref, w2_ref, b2_ref, head_ref,
+    own_ref, side_ref, below_ref, above_ref, inside_ref, w1_ref, b1_ref, w2_ref, b2_ref,
     inner_first, inner_high, inner_low, inner_second,
-    first_ref, second_ref, corr_ref, wind_ref,
+    first_ref, second_ref, wind_ref,
     stack_ref, wind_high, wind_low, high_ref, low_ref,
 ):
     count, rows, width = wind_ref.shape
@@ -414,14 +432,10 @@
         else:
             value = network_rows(w2_ref[...], bias2, high_ref, low_ref, row, width)
         second_ref[:, row * width : (row + 2) * width] = value
-        high, low = halves(value)
-        corr = dot3(head_ref[...], high, low)
-        for part in range(2):
-            corr_ref[:, 2 + row + part, :] = corr[: corr_ref.shape[0], part * width : (part + 1) * width]
 
 
 def backward_kernel(
-    mine_ref, other_ref, wind_ref, inside_ref, first_ref, second_ref, headt_ref, w2b_ref,
+    inner_ref, inner_other, border_ref, border_other, wind_ref, inside_ref, first_ref, second_ref, headt_ref, w2b_ref,
     par_ref, d1_ref,
     sum_ref, g_ref, d2_high, d2_low, own2_ref, act_ref, own1_ref, wind_stack,
 ):
@@ -430,9 +444,11 @@
     cols = width - LANES
     ring = cells // width
     tile = ring - 4
-    sum_ref[...] = mine_ref[...] + other_ref[...]
     wrap = sum_ref.shape[1]
     nine = sum_ref.shape[0]
+    for index in range(nine):
+        inner, border = inner_ref[index] + inner_other[index], border_ref[index] + border_other[index]
+        sum_ref[index, :tile], sum_ref[index, tile:] = merged(inner, border, index % 9)
     g_ref[...] = jnp.zeros(g_ref.shape, F32)
     for row in range(ring):
         g_ref[:nine, row * width : (row + 1) * width] = sum_ref[:, (row - 2) % wrap, :]
@@ -494,7 +510,7 @@
         par_ref[rows, 3 * CH + 16 : 3 * CH + 25] = raw[:, 9 * level : 9 * level + 9]
 
 
-def wind_kernel(mine_ref, other_ref, wind_ref, d1_ref, w1b_ref, wgrad_ref, d1_high, d1_low, net_ref):
+def wind_kernel(inner_ref, inner_other, border_ref, border_other, wind_ref, d1_ref, w1b_ref, wgrad_ref, d1_high, d1_low, net_ref):
     tile, cols = wgrad_ref.shape[1:]
     width = wind_ref.shape[2]
     for row in range(tile + 2):
@@ -513,7 +529,9 @@
         for a in range(3):
             for b in range(3):
                 k = 9 * level + 3 * a + b
-                grad = mine_ref[k, :tile, :cols] + other_ref[k, :tile, :cols]
+                inner = inner_ref[k, :, :cols] + inner_other[k, :, :cols]
+                border = border_ref[k, :, :cols] + border_other[k, :, :cols]
+                grad = merged(inner, border, k % 9)[0]
                 gx_sum = gx_sum + grad * (dx[a] * py[b])
                 gy_sum = gy_sum + grad * (px[a] * dy[b])
         wgrad_ref[2 * level] = COURANT * gx_sum + net_ref[2 * level]
@@ -572,8 +590,14 @@
     )
 
 
-def tracer_kernel(levels_ref, wind_ref, corr_ref, cot_ref, side_ref, below_ref, above_ref, out_ref, coef_ref):
+def tracer_kernel(levels_ref, wind_ref, second_ref, head_ref, cot_ref, side_ref, below_ref, above_ref, out_ref, coef_ref, corr_ref):
     count, tile, cols = out_ref.shape
+    width = wind_ref.shape[2]
+    for row in range(0, tile + 4, 2):
+        high, low = halves(second_ref[:, row * width : (row + 2) * width])
+        corr = dot3(head_ref[...], high, low)
+        for part in range(2):
+            corr_ref[:, 2 + row + part, :] = corr[: corr_ref.shape[0], part * width : (part + 1) * width]
     for level in range(LEVELS):
         px = lax_wendroff(COURANT * wind_ref[2 * level])
         py = lax_wendroff(COURANT * wind_ref[2 * level + 1])
@@ -739,27 +763,28 @@
         [vmem((n_wind, tile, width), F32), vmem((16, tile * width), F32)] + [vmem((16, tile * width), BF16)] * 2,
         (winds, side, inside, w1, bias1_col, w2, bias2_col),
     )
-    above, below, inner_net, inner = lax.optimization_barrier((above, below, inner_net, inner))
-    mine = call(
+    cores = [(i, i ^ 1) for i in range(lax.axis_size("tracer"))]
+    inner_other = lax.ppermute(inner, "tracer", cores)
+    above, below, inner_net, inner, inner_other = lax.optimization_barrier((above, below, inner_net, inner, inner_other))
+    border = call(
         border_kernel,
-        spec((9 * LEVELS, rows, width), F32),
+        spec((9 * LEVELS, 2 * HALO, width), F32),
         [vmem((3, count + 8, 2 * HALO, width), F32)] * 2,
-        (levels, inner, edge, side, below, above),
+        (levels, edge, side, below, above),
         {0: pltpu.SMEM},
     )
-    other = lax.ppermute(mine, "tracer", [(i, i ^ 1) for i in range(lax.axis_size("tracer"))])
-    first, second, corr, wind_ext = call(
+    totals = (inner, inner_other, border, lax.ppermute(border, "tracer", cores))
+    first, second, wind_ext = call(
         forward_kernel,
         [
             spec((CH, (rows - 2) * width), F32),
             spec((CH, (rows - 4) * width), F32),
-            spec((9 * LEVELS, rows, width), F32),
             spec((n_wind, rows, width), F32),
         ],
         [vmem((16, rows * width), F32)]
         + [vmem((16, rows * width), BF16)] * 2
         + [vmem((3 * CH, (rows - 2) * width), BF16)] * 2,
-        (winds, side, below, above, inside, w1, bias1_col, w2, bias2_col, head_w) + tuple(inner_net),
+        (winds, side, below, above, inside, w1, bias1_col, w2, bias2_col) + tuple(inner_net),
     )
     ring, own = (tile + 4) * width, (tile + 2) * width
     params, delta = call(
@@ -769,20 +794,20 @@
         + [vmem((3 * CH, ring), BF16)] * 2
         + [vmem((6 * CH, (tile + 2) * cols), BF16)] * 3
         + [vmem((16, (tile + 2) * cols), F32)],
-        (mine, other, wind_ext, inside, first, second, head_t, w2b),
+        totals + (wind_ext, inside, first, second, head_t, w2b),
     )
     wind_grad = call(
         wind_kernel,
         spec((n_wind, tile, cols), F32),
         [vmem((3 * CH, own), BF16)] * 2 + [vmem((n_wind, tile, cols), F32)],
-        (mine, other, wind_ext, delta, w1b),
-    )
-    mine, other, wind_grad, corr = sum_rounds(params, ("gy", "gx"), wind_grad, corr)
+        totals + (wind_ext, delta, w1b),
+    )
+    mine, other, wind_grad, second = sum_rounds(params, ("gy", "gx"), wind_grad, second)
     tracer_grad = call(
         tracer_kernel,
         spec((count, tile, cols), BF16),
-        [vmem((LEVELS, 9, tile, cols), F32)],
-        (levels, wind_ext, corr, cotangent, side, below, above),
+        [vmem((LEVELS, 9, tile, cols), F32), vmem((9 * LEVELS, rows, width), F32)],
+        (levels, wind_ext, second, head_w, cotangent, side, below, above),
         {0: pltpu.SMEM},
     )
     conv1_grad, bias1_grad, conv2_grad, bias2_grad, head_grad = call(

time: 37.5 us -> 36.9 us (0.984)
  waiting for transfers between devices: 6.44 us -> 5.59 us
  Pallas kernels: 17 us -> 16.5 us
  local copies, waits for them, and re-layouts: 1.84 us -> 2.26 us
    ppermute x3, waiting for transfers between devices: 5.53 us -> 4.96 us  [sum_rounds(): lax.ppermute(value, axis, [(i, i ^ step) for i in range(lax.axis_size(axi...]
    pallas_call x10, Pallas kernels: 17 us -> 16.5 us  [call(): pl.pallas_call(kernel, out_shape=outs, in_specs=specs, out_specs=[whole]...]
    ppermute x2, waiting for transfers between devices: 0.78 us -> 0.36 us  [body(): one, two = (lax.ppermute(one, 'gx', ahead), lax.ppermute(two, 'gx', behind))]
    unnamed x20, local copies, waits for them, and re-layouts: 0.81 us -> 1.23 us
  transfers between devices with their start and end apart: 7 -> 8, of which waited for: 5 -> 6; matrix products, arithmetic and copies ran while one was open for 3% -> 3% of each run, Pallas kernels for 27% -> 26%
where the time goes in v7:
time: 36.9 us; the launch traced here: 36.6 us
  Pallas kernels  16.5 us (45%)
  starting transfers between devices  11.3 us (31%)
  waiting for transfers between devices  5.59 us (15%)
  local copies, waits for them, and re-layouts  2.26 us (6%)
  between operations  0.9 us (2%)
    pallas_call x10, Pallas kernels, call(): pl.pallas_call(kernel, out_shape=outs, in_specs=specs, out_specs=[whole]...  16.5 us
    ppermute x3, waiting for transfers between devices, sum_rounds(): lax.ppermute(value, axis, [(i, i ^ step) for i in range(lax.axis_size(axi...  4.96 us
    ppermute x2, starting transfers between devices, body(): one, two = (lax.ppermute(one, 'gx', ahead), lax.ppermute(two, 'gx', behind))  4.2 us
    ppermute x3, starting transfers between devices, sum_rounds(): lax.ppermute(value, axis, [(i, i ^ step) for i in range(lax.axis_size(axi...  3.91 us
    ppermute x1, starting transfers between devices, body(): got = lax.ppermute(packed, 'gy', up + down)  3 us
    unnamed x20, local copies, waits for them, and re-layouts  1.23 us
    pad x1, local copies, waits for them, and re-layouts, body(): jnp.pad(one, spare)  0.98 us
  transfers between devices with their start and end apart: 8, of which 6 were waited for; matrix products, arithmetic and copies ran while one was open for 3% of the time, Pallas kernels for 26%

profile of v7, /device:TPU:0, one launch (start us, length us, event | category | flops | bytes accessed | tf_op | source)
XLA Modules:
  0.0 36.6 jit_solution(2853732236354885170)
XLA Ops:
  0.6 1.8 %shard_map.144 = (bf16[6,8,128]{2,1,0:T(8,128)(2,1)}, bf16[52,4,256]{2,1,0:T(4,128)(2,1)}, bf16[52,4,256]{2,1,0:T(4,128)(2,1)}) custom-call(s32[1]{0:T(128)} %bitcast.odd_ref, bf16[32,8,256]{2,1,0:T(8,128)(2,1)} %tracer_ref.1, bf16[32,8,256]{2,1,0:T(8,128)(2,1)} %cot_ref.3, f32[4,8,256]{2,1,0:T(8,128)} %own_ref.3), custom_call_target="tpu_custom_call" | custom-call | flops 2000000 | bytes 2000000 | tf_op jit(solution)/shard_map/pallas_call | solution.py:638
  2.5 3.0 %collective-permute-start = (bf16[6,8,128]{2,1,0:T(8,128)(2,1)}, bf16[6,8,128]{2,1,0:T(8,128)(2,1)S(1)}, u32[]{:S(2)}, u32[]{:S(2)}) collective-permute-start(bf16[6,8,128]{2,1,0:T(8,128)(2,1)} %get-tuple-element.53), channel_id=1, source_target_pairs={{0,2},{2,0},{1,3},{3,1},{4,6},{6,4},{5,7},{7,5},{8,10},{10,8},{9,1... | collective-permute-start | bytes 36872 | tf_op jit(solution)/shard_map/ppermute | solution.py:695
  5.5 0.0 copy-start.9
  5.5 0.7 %copy-done.9 = s32[32]{0:T(128)S(1)} copy-done((s32[32]{0:T(128)S(1)}, s32[32]{0:T(128)}, u32[]{:S(2)}) %copy-start.9) | copy-done | bytes 152
  6.2 0.0 copy-start.8
  6.2 1.0 %pad.7 = bf16[55,4,256]{2,1,0:T(4,128)(2,1)S(1)} pad(bf16[52,4,256]{2,1,0:T(4,128)(2,1)} %get-tuple-element.54, bf16[]{:T(256)} %constant.46.clone.1), padding=0_3x0_0x0_0 | pad | bytes 219138 | tf_op jit(solution)/shard_map/jit(_pad)/pad | solution.py:691
  7.2 0.0 copy-done.8
  7.2 0.0 copy-start
  7.2 0.0 copy-start.1
  7.3 0.1 collective-permute-done
  7.4 4.2 %collective-permute-start.2 = (bf16[55,4,256]{2,1,0:T(4,128)(2,1)S(1)}, bf16[55,4,256]{2,1,0:T(4,128)(2,1)S(1)}, u32[]{:S(2)}, u32[]{:S(2)}) collective-permute-start(bf16[55,4,256]{2,1,0:T(4,128)(2,1)S(1)} %get-tuple-element.101), channel_id=1, source_target_pairs={{0,12},{4,8},{8,4},{12,0},{1,13},{5,9},{9,5},{13,1},{2,14},{6,10},... | collective-permute-start | bytes 337928 | tf_op jit(solution)/shard_map/ppermute | solution.py:738
  11.6 0.0 collective-permute-start.1
  11.6 0.0 copy-done
  11.6 0.0 copy-done.1
  11.6 0.0 copy-start.3
  11.7 0.0 copy-start.4
  11.7 0.0 copy-start.5
  11.7 2.2 %shard_map.147 = (f32[18,8,384]{2,1,0:T(8,128)S(1)}, f32[2,32,8,384]{3,2,1,0:T(8,128)S(1)}) custom-call(s32[32]{0:T(128)S(1)} %broadcast_clamp_fusion.levels_ref, bf16[32,8,256]{2,1,0:T(8,128)(2,1)S(1)} %copy-done.1, bf16[32,8,256]{2,1,0:T(8,128)(2,1)S(1)} %copy-done, bf16[6,8,128]{2,1,0:T(8,128)(2,1)S(1)} %broadcast_select_fusion.2.side_ref), custom_call_target="tpu_custom_call" | custom-call | flops 2000000 | bytes 2000000 | tf_op jit(solution)/shard_map/pallas_call | solution.py:638
  13.9 0.0 copy-start.6
  13.9 0.0 copy-start.7
  13.9 0.0 copy-start.2
  13.9 0.1 collective-permute-start.3
  14.0 0.0 copy-done.3
  14.0 0.0 copy-done.4
  14.0 0.0 copy-done.5
  14.0 0.5 %copy-done.6 = f32[32]{0:T(128)S(1)} copy-done((f32[32]{0:T(128)S(1)}, f32[32]{0:T(128)}, u32[]{:S(2)}) %copy-start.6) | copy-done | bytes 152
  14.6 0.0 copy-done.7
  14.6 0.6 %shard_map.145 = (bf16[64,96]{1,0:T(8,128)(2,1)S(1)}, bf16[64,576]{1,0:T(8,128)(2,1)S(1)}, bf16[64,576]{1,0:T(8,128)(2,1)S(1)}, bf16[32,576]{1,0:T(8,128)(2,1)S(...) custom-call(f32[32,36]{1,0:T(8,128)S(1)} %copy-done.4, ...), custom_call_target="tpu_custom_call" | custom-call | flops 2000000 | bytes 2000000 | tf_op jit(solution)/shard_map/pallas_call | solution.py:638
  15.2 0.0 copy-done.2
  15.2 0.9 %shard_map.146 = (f32[32,2304]{1,0:T(8,128)S(1)}, bf16[96,2304]{1,0:T(8,128)(2,1)S(1)}, bf16[96,2304]{1,0:T(8,128)(2,1)S(1)}, f32[32,1536]{1,0:T(8,128)S(1)}) custom-call(f32[4,8,256]{2,1,0:T(8,128)S(1)} %copy-done.2, bf16[6,8,128]{2,1,0:T(8,128)(2,1)S(1)} %broadcast_select_fusion.2.side_ref, f32[1,384]{1,0:T(1,128)S(1)} %select_convert_fusion.inside_ref, ...), custom_call_target="tpu_custom_call" | custom-call | flops 2000000 | bytes 2000000 | tf_op jit(solution)/shard_map/pallas_call | solution.py:638
  16.1 0.0 collective-permute-done.2
  16.1 0.4 collective-permute-done.1
  16.5 0.1 broadcast_select_fusion
  16.6 0.0 collective-permute-done.3.inner_other
  16.6 2.1 %shard_map.149.border_ref = f32[18,8,384]{2,1,0:T(8,128)S(1)} custom-call(s32[32]{0:T(128)S(1)} %broadcast_clamp_fusion.levels_ref, f32[2,32,8,384]{3,2,1,0:T(8,128)S(1)} %get-tuple-element.81.edge_ref, bf16[6,8,128]{2,1,0:T(8,128)(2,1)S(1)} %broadcast_select_fusion.2.side_ref, bf16[55,4,256]{2,1,0:T(4,128)(2,1)S(1)} %get-tuple-element.72.below_ref, ...), custom_call_target="tpu_custom_call" | custom-call | flops 2000000 | bytes 2000000 | tf_op jit(solution)/shard_map/pallas_call | solution.py:638
  18.7 0.1 collective-permute-start.4
  18.8 1.3 %shard_map.148 = (f32[32,5376]{1,0:T(8,128)S(1)}, f32[32,4608]{1,0:T(8,128)S(1)}, f32[4,16,384]{2,1,0:T(8,128)S(1)}) custom-call(f32[4,8,256]{2,1,0:T(8,128)S(1)} %copy-done.2, bf16[6,8,128]{2,1,0:T(8,128)(2,1)S(1)} %broadcast_select_fusion.2.side_ref, bf16[55,4,256]{2,1,0:T(4,128)(2,1)S(1)} %get-tuple-element.72.below_ref, ...), custom_call_target="tpu_custom_call" | custom-call | flops 2000000 | bytes 2000000 | tf_op jit(solution)/shard_map/pallas_call | solution.py:638
  20.1 0.1 collective-permute-done.4.border_other
  20.3 2.0 %shard_map.150 = (f32[96,128]{1,0:T(8,128)S(1)}, f32[32,3840]{1,0:T(8,128)S(1)}) custom-call(f32[18,8,384]{2,1,0:T(8,128)S(1)} %get-tuple-element.79.inner_ref, f32[18,8,384]{2,1,0:T(8,128)S(1)} %collective-permute-done.3.inner_other, f32[18,8,384]{2,1,0:T(8,128)S(1)} %shard_map.149.border_ref, f32[18,8,384]{2,1,0:T(8,128)S(1)} %collective-permute-done.4.border_other, ...), custom_call_target="tpu_custom_call" | custom-call | flops 2000000 | bytes 2000000 | tf_op jit(solution)/shard_map/pallas_call | solution.py:638
  22.3 1.5 %collective-permute-start.5 = (f32[96,128]{1,0:T(8,128)S(1)}, f32[96,128]{1,0:T(8,128)S(1)}, u32[]{:S(2)}, u32[]{:S(2)}) collective-permute-start(f32[96,128]{1,0:T(8,128)S(1)} %get-tuple-element.86), channel_id=1, source_target_pairs={{0,2},{2,0},{1,3},{3,1},{4,6},{6,4},{5,7},{7,5},{8,10},{10,8},{9,1... | collective-permute-start | bytes 147464 | tf_op jit(solution)/shard_map/ppermute | solution.py:666
  23.7 1.5 %shard_map.151 = f32[4,8,256]{2,1,0:T(8,128)} custom-call(f32[18,8,384]{2,1,0:T(8,128)S(1)} %get-tuple-element.79.inner_ref, f32[18,8,384]{2,1,0:T(8,128)S(1)} %collective-permute-done.3.inner_other, f32[18,8,384]{2,1,0:T(8,128)S(1)} %shard_map.149.border_ref, f32[18,8,384]{2,1,0:T(8,128)S(1)} %collective-permute-done.4.border_other, ...), custom_call_target="tpu_custom_call" | custom-call | flops 2000000 | bytes 2000000 | tf_op jit(solution)/shard_map/pallas_call | solution.py:638
  25.2 1.2 %collective-permute-done.5 = f32[96,128]{1,0:T(8,128)S(1)} collective-permute-done((f32[96,128]{1,0:T(8,128)S(1)}, f32[96,128]{1,0:T(8,128)S(1)}, u32[]{:S(2)}, u32[]{:S(2)}) %collective-permute-start.5) | collective-permute-done | bytes 49184 | tf_op jit(solution)/shard_map/ppermute | solution.py:666
  26.4 1.7 %collective-permute-start.6 = (f32[96,128]{1,0:T(8,128)S(1)}, f32[96,128]{1,0:T(8,128)S(1)}, u32[]{:S(2)}, u32[]{:S(2)}) collective-permute-start(f32[96,128]{1,0:T(8,128)S(1)} %add.29), channel_id=1, source_target_pairs={{0,4},{4,0},{8,12},{12,8},{1,5},{5,1},{9,13},{13,9},{2,6},{6,2},{1... | collective-permute-start | bytes 147464 | tf_op jit(solution)/shard_map/ppermute | solution.py:666
  28.2 2.4 %collective-permute-done.6 = f32[96,128]{1,0:T(8,128)S(1)} collective-permute-done((f32[96,128]{1,0:T(8,128)S(1)}, f32[96,128]{1,0:T(8,128)S(1)}, u32[]{:S(2)}, u32[]{:S(2)}) %collective-permute-start.6) | collective-permute-done | bytes 49184 | tf_op jit(solution)/shard_map/ppermute | solution.py:666
  30.6 0.7 %collective-permute-start.7 = (f32[96,128]{1,0:T(8,128)S(1)}, f32[96,128]{1,0:T(8,128)S(1)}, u32[]{:S(2)}, u32[]{:S(2)}) collective-permute-start(f32[96,128]{1,0:T(8,128)S(1)} %add.30.mine_ref), channel_id=1, source_target_pairs={{0,8},{4,12},{8,0},{12,4},{1,9},{5,13},{9,1},{13,5},{2,10},{6,14},... | collective-permute-start | bytes 147464 | tf_op jit(solution)/shard_map/ppermute | solution.py:666
  31.3 3.0 %shard_map.152 = bf16[32,8,256]{2,1,0:T(8,128)(2,1)} custom-call(s32[32]{0:T(128)S(1)} %broadcast_clamp_fusion.levels_ref, f32[4,16,384]{2,1,0:T(8,128)S(1)} %get-tuple-element.78.wind_ref, f32[32,4608]{1,0:T(8,128)S(1)} %get-tuple-element.90.second_ref, bf16[64,64]{1,0:T(8,128)(2,1)S(1)} %get-tuple-element.91.head_ref, bf16[32,8,256]{2,1,0:T(8,128)(2,1)S(1)} %copy-done, ...), custom_call_target="tpu_custom_call" | custom-call | flops 2000000 | bytes 2000000 | tf_op jit(solution)/shard_map/pallas_call | solution.py:638
  34.3 1.3 %collective-permute-done.7.other_ref = f32[96,128]{1,0:T(8,128)S(1)} collective-permute-done((f32[96,128]{1,0:T(8,128)S(1)}, f32[96,128]{1,0:T(8,128)S(1)}, u32[]{:S(2)}, u32[]{:S(2)}) %collective-permute-start.7) | collective-permute-done | bytes 49184 | tf_op jit(solution)/shard_map/ppermute | solution.py:666
  35.6 1.0 %shard_map.153 = (f32[32,36]{1,0:T(8,128)}, f32[1,32]{1,0:T(1,128)}, f32[32,288]{1,0:T(8,128)}, f32[1,32]{1,0:T(1,128)}, f32[18,32]{1,0:T(8,128)}) custom-call(f32[96,128]{1,0:T(8,128)S(1)} %add.30.mine_ref, f32[96,128]{1,0:T(8,128)S(1)} %collective-permute-done.7.other_ref), custom_call_target="tpu_custom_call" | custom-call | flops 200000 | bytes 2000000 | tf_op jit(solution)/shard_map/pallas_call | solution.py:638
  (9 shorter events, 0.1 us)
Async XLA Ops:
  2.5 4.9 %collective-permute-start = (bf16[6,8,128]{2,1,0:T(8,128)(2,1)}, bf16[6,8,128]{2,1,0:T(8,128)(2,1)S(1)}, u32[]{:S(2)}, u32[]{:S(2)}) collective-permute-start(bf16[6,8,128]{2,1,0:T(8,128)(2,1)} %get-tuple-element.53), channel_id=1, source_target_pairs={{0,2},{2,0},{1,3},{3,1},{4,6},{6,4},{5,7},{7,5},{8,10},{10,8},{9,1... | collective-permute-start | bytes 36872 | tf_op jit(solution)/shard_map/ppermute | solution.py:695
  5.5 0.7 %copy-start.9 = (s32[32]{0:T(128)S(1)}, s32[32]{0:T(128)}, u32[]{:S(2)}) copy-start(s32[32]{0:T(128)} %param.12) | copy-start | bytes 388
  6.2 1.0 %copy-start.8 = (bf16[52,4,256]{2,1,0:T(4,128)(2,1)S(1)}, bf16[52,4,256]{2,1,0:T(4,128)(2,1)}, u32[]{:S(2)}) copy-start(bf16[52,4,256]{2,1,0:T(4,128)(2,1)} %get-tuple-element.55) | copy-start | bytes 319492
  7.2 4.4 %copy-start = (bf16[32,8,256]{2,1,0:T(8,128)(2,1)S(1)}, bf16[32,8,256]{2,1,0:T(8,128)(2,1)}, u32[]{:S(2)}) copy-start(bf16[32,8,256]{2,1,0:T(8,128)(2,1)} %cot_ref.3) | copy-start | bytes 393220
  7.2 4.4 %copy-start.1 = (bf16[32,8,256]{2,1,0:T(8,128)(2,1)S(1)}, bf16[32,8,256]{2,1,0:T(8,128)(2,1)}, u32[]{:S(2)}) copy-start(bf16[32,8,256]{2,1,0:T(8,128)(2,1)} %tracer_ref.1) | copy-start | bytes 393220
  7.4 8.7 %collective-permute-start.2 = (bf16[55,4,256]{2,1,0:T(4,128)(2,1)S(1)}, bf16[55,4,256]{2,1,0:T(4,128)(2,1)S(1)}, u32[]{:S(2)}, u32[]{:S(2)}) collective-permute-start(bf16[55,4,256]{2,1,0:T(4,128)(2,1)S(1)} %get-tuple-element.101), channel_id=1, source_target_pairs={{0,12},{4,8},{8,4},{12,0},{1,13},{5,9},{9,5},{13,1},{2,14},{6,10},... | collective-permute-start | bytes 337928 | tf_op jit(solution)/shard_map/ppermute | solution.py:738
  11.6 4.9 %collective-permute-start.1 = (bf16[55,4,256]{2,1,0:T(4,128)(2,1)S(1)}, bf16[55,4,256]{2,1,0:T(4,128)(2,1)S(1)}, u32[]{:S(2)}, u32[]{:S(2)}) collective-permute-start(bf16[55,4,256]{2,1,0:T(4,128)(2,1)S(1)} %get-tuple-element.102), channel_id=1, source_target_pairs={{0,4},{4,0},{8,12},{12,8},{1,5},{5,1},{9,13},{13,9},{2,6},{6,2},{1... | collective-permute-start | bytes 337928 | tf_op jit(solution)/shard_map/ppermute | solution.py:738
  11.6 2.4 %copy-start.3 = (f32[32,288]{1,0:T(8,128)S(1)}, f32[32,288]{1,0:T(8,128)}, u32[]{:S(2)}) copy-start(f32[32,288]{1,0:T(8,128)} %c2_hbm) | copy-start | bytes 110596
  11.7 2.4 %copy-start.4 = (f32[32,36]{1,0:T(8,128)S(1)}, f32[32,36]{1,0:T(8,128)}, u32[]{:S(2)}) copy-start(f32[32,36]{1,0:T(8,128)} %c1_hbm) | copy-start | bytes 13828
  11.7 2.4 %copy-start.5 = (f32[18,32]{1,0:T(8,128)S(1)}, f32[18,32]{1,0:T(8,128)}, u32[]{:S(2)}) copy-start(f32[18,32]{1,0:T(8,128)} %head_hbm) | copy-start | bytes 6916
  13.9 0.7 %copy-start.6 = (f32[32]{0:T(128)S(1)}, f32[32]{0:T(128)}, u32[]{:S(2)}) copy-start(f32[32]{0:T(128)} %param.14) | copy-start | bytes 388
  13.9 0.7 %copy-start.7 = (f32[32]{0:T(128)S(1)}, f32[32]{0:T(128)}, u32[]{:S(2)}) copy-start(f32[32]{0:T(128)} %param.16) | copy-start | bytes 388
  13.9 1.3 %copy-start.2 = (f32[4,8,256]{2,1,0:T(8,128)S(1)}, f32[4,8,256]{2,1,0:T(8,128)}, u32[]{:S(2)}) copy-start(f32[4,8,256]{2,1,0:T(8,128)} %own_ref.3) | copy-start | bytes 98308
  13.9 2.6 %collective-permute-start.3 = (f32[18,8,384]{2,1,0:T(8,128)S(1)}, f32[18,8,384]{2,1,0:T(8,128)S(1)}, u32[]{:S(2)}, u32[]{:S(2)}) collective-permute-start(f32[18,8,384]{2,1,0:T(8,128)S(1)} %get-tuple-element.79.inner_ref), channel_id=1, source_target_pairs={{0,1},{1,0},{2,3},{3,2},{4,5},{5,4},{6,7},{7,6},{8,9},{9,8},{10,11... | collective-permute-start | bytes 663560 | tf_op jit(solution)/shard_map/ppermute | solution.py:767
  18.7 1.5 %collective-permute-start.4 = (f32[18,8,384]{2,1,0:T(8,128)S(1)}, f32[18,8,384]{2,1,0:T(8,128)S(1)}, u32[]{:S(2)}, u32[]{:S(2)}) collective-permute-start(f32[18,8,384]{2,1,0:T(8,128)S(1)} %shard_map.149.border_ref), channel_id=1, source_target_pairs={{0,1},{1,0},{2,3},{3,2},{4,5},{5,4},{6,7},{7,6},{8,9},{9,8},{10,11... | collective-permute-start | bytes 663560 | tf_op jit(solution)/shard_map/ppermute | solution.py:776
  22.3 4.2 %collective-permute-start.5 = (f32[96,128]{1,0:T(8,128)S(1)}, f32[96,128]{1,0:T(8,128)S(1)}, u32[]{:S(2)}, u32[]{:S(2)}) collective-permute-start(f32[96,128]{1,0:T(8,128)S(1)} %get-tuple-element.86), channel_id=1, source_target_pairs={{0,2},{2,0},{1,3},{3,1},{4,6},{6,4},{5,7},{7,5},{8,10},{10,8},{9,1... | collective-permute-start | bytes 147464 | tf_op jit(solution)/shard_map/ppermute | solution.py:666
  26.4 4.2 %collective-permute-start.6 = (f32[96,128]{1,0:T(8,128)S(1)}, f32[96,128]{1,0:T(8,128)S(1)}, u32[]{:S(2)}, u32[]{:S(2)}) collective-permute-start(f32[96,128]{1,0:T(8,128)S(1)} %add.29), channel_id=1, source_target_pairs={{0,4},{4,0},{8,12},{12,8},{1,5},{5,1},{9,13},{13,9},{2,6},{6,2},{1... | collective-permute-start | bytes 147464 | tf_op jit(solution)/shard_map/ppermute | solution.py:666
  30.6 5.0 %collective-permute-start.7 = (f32[96,128]{1,0:T(8,128)S(1)}, f32[96,128]{1,0:T(8,128)S(1)}, u32[]{:S(2)}, u32[]{:S(2)}) collective-permute-start(f32[96,128]{1,0:T(8,128)S(1)} %add.30.mine_ref), channel_id=1, source_target_pairs={{0,8},{4,12},{8,0},{12,4},{1,9},{5,13},{9,1},{13,5},{2,10},{6,14},... | collective-permute-start | bytes 147464 | tf_op jit(solution)/shard_map/ppermute | solution.py:666

commit v8 on v7

--- a/solution.py
+++ b/solution.py
@@ -510,7 +510,20 @@
         par_ref[rows, 3 * CH + 16 : 3 * CH + 25] = raw[:, 9 * level : 9 * level + 9]
 
 
-def wind_kernel(inner_ref, inner_other, border_ref, border_other, wind_ref, d1_ref, w1b_ref, wgrad_ref, d1_high, d1_low, net_ref):
+def wind_kernel(inner_ref, inner_other, border_ref, border_other, wind_ref, d1_ref, w1b_ref, wgrad_ref, pick2_ref, pick1_ref, d1_high, d1_low, net_ref):
+    n_wind = wgrad_ref.shape[0]
+    def wanted2(row):
+        r = row & (LANES - 1)
+        return jnp.where(r < 3 * CH, 9 * (r & (CH - 1)) + 3 * (row >> 7) + (r >> 5), -1)
+
+    pick2_ref[...] = picker(pick2_ref.shape, 1, wanted2)
+
+    def wanted1(row):
+        a, r = row >> 7, (row & (LANES - 1)) - 3 * CH
+        b = (r >= n_wind).astype(jnp.int32) + (r >= 2 * n_wind).astype(jnp.int32)
+        return jnp.where((r >= 0) & (r < 3 * n_wind), 9 * (r - n_wind * b) + 3 * a + b, -1)
+
+    pick1_ref[...] = picker(pick1_ref.shape, 1, wanted1)
     tile, cols = wgrad_ref.shape[1:]
     width = wind_ref.shape[2]
     for row in range(tile + 2):
@@ -538,42 +551,22 @@
         wgrad_ref[2 * level + 1] = COURANT * gy_sum + net_ref[2 * level + 1]
 
 
-def final_kernel(mine_ref, other_ref, c1_ref, b1_ref, c2_ref, b2_ref, head_ref):
+def final_kernel(mine_ref, other_ref, pick2_ref, pick1_ref, c1_ref, b1_ref, c2_ref, b2_ref, head_ref):
     total = mine_ref[...] + other_ref[...]
     across = jnp.concatenate([total, jnp.zeros((LANES - total.shape[0], LANES), F32)], axis=0).T
-    size2, size1 = c2_ref.shape[1], c1_ref.shape[1]
-    n_wind = size1 // 9
-    split, rest = [], total
-    turned, rest_t = [], across[: 3 * CH, : 3 * CH]
-    for _ in range(3):
-        high = rest.astype(BF16)
-        split.append(high)
-        rest = rest - high.astype(F32)
-        high = rest_t.astype(BF16)
-        turned.append(high)
-        rest_t = rest_t - high.astype(F32)
-    source = lax.broadcasted_iota(jnp.int32, (3 * CH, size2), 0)
-    target = lax.broadcasted_iota(jnp.int32, (3 * CH, size2), 1)
-    source1 = lax.broadcasted_iota(jnp.int32, (LANES, size1), 0) - 3 * CH
-    target1 = lax.broadcasted_iota(jnp.int32, (LANES, size1), 1)
-    out2 = jnp.zeros((CH, size2), F32)
-    out1 = jnp.zeros((CH, size1), F32)
-    for a in range(3):
-        rows = slice(a * CH, (a + 1) * CH)
-        pick2 = jnp.zeros((3 * CH, size2), F32)
-        pick1 = jnp.zeros((LANES, size1), F32)
-        for b in range(3):
-            shift = 3 * a + b
-            lies = (source >= b * CH) & (source < (b + 1) * CH)
-            pick2 = jnp.where(lies & (target == 9 * (source - b * CH) + shift), 1.0, pick2)
-            lies = (source1 >= b * n_wind) & (source1 < (b + 1) * n_wind)
-            pick1 = jnp.where(lies & (target1 == 9 * (source1 - b * n_wind) + shift), 1.0, pick1)
-        pick2, pick1 = pick2.astype(BF16), pick1.astype(BF16)
-        for part in range(3):
-            out2 = out2 + jnp.dot(turned[part][rows], pick2, preferred_element_type=F32)
-            out1 = out1 + jnp.dot(split[part][rows], pick1, preferred_element_type=F32)
-    c2_ref[...] = out2
-    c1_ref[...] = out1
+    n_wind = c1_ref.shape[1] // 9
+
+    def moved(value, pick_ref):
+        parts = []
+        for _ in range(3):
+            high = value.astype(BF16)
+            parts.append(jnp.concatenate([high[a * CH : (a + 1) * CH] for a in range(3)], axis=1))
+            value = value - high.astype(F32)
+        out = jnp.dot(jnp.concatenate(parts, axis=0), pick_ref[...], preferred_element_type=F32)
+        return out[:CH] + out[CH : 2 * CH] + out[2 * CH :]
+
+    c2_ref[...] = moved(across[: 3 * CH], pick2_ref)
+    c1_ref[...] = moved(total, pick1_ref)
     b1_ref[...] = across[3 * CH + 3 * n_wind : 3 * CH + 3 * n_wind + 1, CH : 2 * CH]
     b2_ref[...] = across[3 * CH + 16 : 3 * CH + 17, :CH]
     for level in range(LEVELS):
@@ -796,13 +789,14 @@
         + [vmem((16, (tile + 2) * cols), F32)],
         totals + (wind_ext, inside, first, second, head_t, w2b),
     )
-    wind_grad = call(
+    early = call(
         wind_kernel,
-        spec((n_wind, tile, cols), F32),
+        [spec((n_wind, tile, cols), F32), spec((3 * LANES, 9 * CH), BF16), spec((3 * LANES, conv1.shape[1]), BF16)],
         [vmem((3 * CH, own), BF16)] * 2 + [vmem((n_wind, tile, cols), F32)],
         totals + (wind_ext, delta, w1b),
     )
-    mine, other, wind_grad, second = sum_rounds(params, ("gy", "gx"), wind_grad, second)
+    mine, other, early, second = sum_rounds(params, ("gy", "gx"), early, second)
+    wind_grad, pick2, pick1 = early
     tracer_grad = call(
         tracer_kernel,
         spec((count, tile, cols), BF16),
@@ -814,7 +808,7 @@
         final_kernel,
         [spec(conv1.shape, F32), spec((1, CH), F32), spec(conv2.shape, F32), spec((1, CH), F32), spec(head.shape, F32)],
         [],
-        (mine, other),
+        (mine, other, pick2, pick1),
         flops=200_000,
     )
     return (tracer_grad, wind_grad, conv1_grad, bias1_grad[0], conv2_grad, bias2_grad[0], head_grad)

time: 36.9 us -> 36.8 us (level)
  no operation moved by 1% of the time
where the time goes in v8:
time: 36.8 us; the launch traced here: 36.6 us
  Pallas kernels  16.6 us (45%)
  starting transfers between devices  11.3 us (31%)
  waiting for transfers between devices  5.41 us (15%)
  local copies, waits for them, and re-layouts  2.26 us (6%)
  between operations  0.9 us (2%)
    pallas_call x10, Pallas kernels, call(): pl.pallas_call(kernel, out_shape=outs, in_specs=specs, out_specs=[whole]...  16.6 us
    ppermute x3, waiting for transfers between devices, sum_rounds(): lax.ppermute(value, axis, [(i, i ^ step) for i in range(lax.axis_size(axi...  4.82 us
    ppermute x2, starting transfers between devices, body(): one, two = (lax.ppermute(one, 'gx', ahead), lax.ppermute(two, 'gx', behind))  4.2 us
    ppermute x3, starting transfers between devices, sum_rounds(): lax.ppermute(value, axis, [(i, i ^ step) for i in range(lax.axis_size(axi...  3.96 us
    ppermute x1, starting transfers between devices, body(): got = lax.ppermute(packed, 'gy', up + down)  3 us
    unnamed x20, local copies, waits for them, and re-layouts  1.23 us
    pad x1, local copies, waits for them, and re-layouts, body(): jnp.pad(one, spare)  0.98 us
  transfers between devices with their start and end apart: 8, of which 6 were waited for; matrix products, arithmetic and copies ran while one was open for 3% of the time, Pallas kernels for 26%

profile of v8, /device:TPU:0, one launch (start us, length us, event | category | flops | bytes accessed | tf_op | source)
XLA Modules:
  0.0 36.6 jit_solution(12236410790054262193)
XLA Ops:
  0.6 1.8 %shard_map.144 = (bf16[6,8,128]{2,1,0:T(8,128)(2,1)}, bf16[52,4,256]{2,1,0:T(4,128)(2,1)}, bf16[52,4,256]{2,1,0:T(4,128)(2,1)}) custom-call(s32[1]{0:T(128)} %bitcast.odd_ref, bf16[32,8,256]{2,1,0:T(8,128)(2,1)} %tracer_ref.1, bf16[32,8,256]{2,1,0:T(8,128)(2,1)} %cot_ref.3, f32[4,8,256]{2,1,0:T(8,128)} %own_ref.3), custom_call_target="tpu_custom_call" | custom-call | flops 2000000 | bytes 2000000 | tf_op jit(solution)/shard_map/pallas_call | solution.py:631
  2.5 3.0 %collective-permute-start = (bf16[6,8,128]{2,1,0:T(8,128)(2,1)}, bf16[6,8,128]{2,1,0:T(8,128)(2,1)S(1)}, u32[]{:S(2)}, u32[]{:S(2)}) collective-permute-start(bf16[6,8,128]{2,1,0:T(8,128)(2,1)} %get-tuple-element.58), channel_id=1, source_target_pairs={{0,2},{2,0},{1,3},{3,1},{4,6},{6,4},{5,7},{7,5},{8,10},{10,8},{9,1... | collective-permute-start | bytes 36872 | tf_op jit(solution)/shard_map/ppermute | solution.py:688
  5.5 0.0 copy-start.9
  5.5 0.7 %copy-done.9 = s32[32]{0:T(128)S(1)} copy-done((s32[32]{0:T(128)S(1)}, s32[32]{0:T(128)}, u32[]{:S(2)}) %copy-start.9) | copy-done | bytes 152
  6.2 0.0 copy-start.8
  6.2 1.0 %pad.7 = bf16[55,4,256]{2,1,0:T(4,128)(2,1)S(1)} pad(bf16[52,4,256]{2,1,0:T(4,128)(2,1)} %get-tuple-element.59, bf16[]{:T(256)} %constant.46.clone.1), padding=0_3x0_0x0_0 | pad | bytes 219138 | tf_op jit(solution)/shard_map/jit(_pad)/pad | solution.py:684
  7.2 0.0 copy-done.8
  7.2 0.0 copy-start
  7.2 0.0 copy-start.1
  7.3 0.1 collective-permute-done
  7.4 4.2 %collective-permute-start.2 = (bf16[55,4,256]{2,1,0:T(4,128)(2,1)S(1)}, bf16[55,4,256]{2,1,0:T(4,128)(2,1)S(1)}, u32[]{:S(2)}, u32[]{:S(2)}) collective-permute-start(bf16[55,4,256]{2,1,0:T(4,128)(2,1)S(1)} %get-tuple-element.111), channel_id=1, source_target_pairs={{0,12},{4,8},{8,4},{12,0},{1,13},{5,9},{9,5},{13,1},{2,14},{6,10},... | collective-permute-start | bytes 337928 | tf_op jit(solution)/shard_map/ppermute | solution.py:731
  11.6 0.0 collective-permute-start.1
  11.6 0.0 copy-done
  11.6 0.0 copy-done.1
  11.6 0.0 copy-start.3
  11.7 0.0 copy-start.4
  11.7 0.0 copy-start.5
  11.7 2.3 %shard_map.147 = (f32[18,8,384]{2,1,0:T(8,128)S(1)}, f32[2,32,8,384]{3,2,1,0:T(8,128)S(1)}) custom-call(s32[32]{0:T(128)S(1)} %broadcast_clamp_fusion.levels_ref, bf16[32,8,256]{2,1,0:T(8,128)(2,1)S(1)} %copy-done.1, bf16[32,8,256]{2,1,0:T(8,128)(2,1)S(1)} %copy-done, bf16[6,8,128]{2,1,0:T(8,128)(2,1)S(1)} %broadcast_select_fusion.2.side_ref), custom_call_target="tpu_custom_call" | custom-call | flops 2000000 | bytes 2000000 | tf_op jit(solution)/shard_map/pallas_call | solution.py:631
  13.9 0.0 copy-start.6
  14.0 0.0 copy-start.7
  14.0 0.0 copy-start.2
  14.0 0.1 collective-permute-start.3
  14.1 0.0 copy-done.3
  14.1 0.0 copy-done.4
  14.1 0.0 copy-done.5
  14.1 0.5 %copy-done.6 = f32[32]{0:T(128)S(1)} copy-done((f32[32]{0:T(128)S(1)}, f32[32]{0:T(128)}, u32[]{:S(2)}) %copy-start.6) | copy-done | bytes 152
  14.6 0.0 copy-done.7
  14.6 0.6 %shard_map.145 = (bf16[64,96]{1,0:T(8,128)(2,1)S(1)}, bf16[64,576]{1,0:T(8,128)(2,1)S(1)}, bf16[64,576]{1,0:T(8,128)(2,1)S(1)}, bf16[32,576]{1,0:T(8,128)(2,1)S(...) custom-call(f32[32,36]{1,0:T(8,128)S(1)} %copy-done.4, ...), custom_call_target="tpu_custom_call" | custom-call | flops 2000000 | bytes 2000000 | tf_op jit(solution)/shard_map/pallas_call | solution.py:631
  15.2 0.0 copy-done.2
  15.2 0.9 %shard_map.146 = (f32[32,2304]{1,0:T(8,128)S(1)}, bf16[96,2304]{1,0:T(8,128)(2,1)S(1)}, bf16[96,2304]{1,0:T(8,128)(2,1)S(1)}, f32[32,1536]{1,0:T(8,128)S(1)}) custom-call(f32[4,8,256]{2,1,0:T(8,128)S(1)} %copy-done.2, bf16[6,8,128]{2,1,0:T(8,128)(2,1)S(1)} %broadcast_select_fusion.2.side_ref, f32[1,384]{1,0:T(1,128)S(1)} %select_convert_fusion.inside_ref, ...), custom_call_target="tpu_custom_call" | custom-call | flops 2000000 | bytes 2000000 | tf_op jit(solution)/shard_map/pallas_call | solution.py:631
  16.2 0.0 collective-permute-done.2
  16.2 0.3 collective-permute-done.1
  16.5 0.1 broadcast_select_fusion
  16.6 0.0 collective-permute-done.3.inner_other
  16.6 2.2 %shard_map.149.border_ref = f32[18,8,384]{2,1,0:T(8,128)S(1)} custom-call(s32[32]{0:T(128)S(1)} %broadcast_clamp_fusion.levels_ref, f32[2,32,8,384]{3,2,1,0:T(8,128)S(1)} %get-tuple-element.86.edge_ref, bf16[6,8,128]{2,1,0:T(8,128)(2,1)S(1)} %broadcast_select_fusion.2.side_ref, bf16[55,4,256]{2,1,0:T(4,128)(2,1)S(1)} %get-tuple-element.77.below_ref, ...), custom_call_target="tpu_custom_call" | custom-call | flops 2000000 | bytes 2000000 | tf_op jit(solution)/shard_map/pallas_call | solution.py:631
  18.8 0.1 collective-permute-start.4
  18.9 1.3 %shard_map.148 = (f32[32,5376]{1,0:T(8,128)S(1)}, f32[32,4608]{1,0:T(8,128)S(1)}, f32[4,16,384]{2,1,0:T(8,128)S(1)}) custom-call(f32[4,8,256]{2,1,0:T(8,128)S(1)} %copy-done.2, bf16[6,8,128]{2,1,0:T(8,128)(2,1)S(1)} %broadcast_select_fusion.2.side_ref, bf16[55,4,256]{2,1,0:T(4,128)(2,1)S(1)} %get-tuple-element.77.below_ref, ...), custom_call_target="tpu_custom_call" | custom-call | flops 2000000 | bytes 2000000 | tf_op jit(solution)/shard_map/pallas_call | solution.py:631
  20.2 0.1 collective-permute-done.4.border_other
  20.3 2.0 %shard_map.150 = (f32[96,128]{1,0:T(8,128)S(1)}, f32[32,3840]{1,0:T(8,128)S(1)}) custom-call(f32[18,8,384]{2,1,0:T(8,128)S(1)} %get-tuple-element.84.inner_ref, f32[18,8,384]{2,1,0:T(8,128)S(1)} %collective-permute-done.3.inner_other, f32[18,8,384]{2,1,0:T(8,128)S(1)} %shard_map.149.border_ref, f32[18,8,384]{2,1,0:T(8,128)S(1)} %collective-permute-done.4.border_other, ...), custom_call_target="tpu_custom_call" | custom-call | flops 2000000 | bytes 2000000 | tf_op jit(solution)/shard_map/pallas_call | solution.py:631
  22.3 1.5 %collective-permute-start.5 = (f32[96,128]{1,0:T(8,128)S(1)}, f32[96,128]{1,0:T(8,128)S(1)}, u32[]{:S(2)}, u32[]{:S(2)}) collective-permute-start(f32[96,128]{1,0:T(8,128)S(1)} %get-tuple-element.91), channel_id=1, source_target_pairs={{0,2},{2,0},{1,3},{3,1},{4,6},{6,4},{5,7},{7,5},{8,10},{10,8},{9,1... | collective-permute-start | bytes 147464 | tf_op jit(solution)/shard_map/ppermute | solution.py:659
  23.8 1.6 %shard_map.151 = (f32[4,8,256]{2,1,0:T(8,128)}, bf16[384,288]{1,0:T(8,128)(2,1)S(1)}, bf16[384,36]{1,0:T(8,128)(2,1)S(1)}) custom-call(f32[18,8,384]{2,1,0:T(8,128)S(1)} %get-tuple-element.84.inner_ref, f32[18,8,384]{2,1,0:T(8,128)S(1)} %collective-permute-done.3.inner_other, f32[18,8,384]{2,1,0:T(8,128)S(1)} %shard_map.149.border_ref, ...), custom_call_target="tpu_custom_call" | custom-call | flops 2000000 | bytes 2000000 | tf_op jit(solution)/shard_map/pallas_call | solution.py:631
  25.3 1.1 %collective-permute-done.5 = f32[96,128]{1,0:T(8,128)S(1)} collective-permute-done((f32[96,128]{1,0:T(8,128)S(1)}, f32[96,128]{1,0:T(8,128)S(1)}, u32[]{:S(2)}, u32[]{:S(2)}) %collective-permute-start.5) | collective-permute-done | bytes 49184 | tf_op jit(solution)/shard_map/ppermute | solution.py:659
  26.5 1.8 %collective-permute-start.6 = (f32[96,128]{1,0:T(8,128)S(1)}, f32[96,128]{1,0:T(8,128)S(1)}, u32[]{:S(2)}, u32[]{:S(2)}) collective-permute-start(f32[96,128]{1,0:T(8,128)S(1)} %add.29), channel_id=1, source_target_pairs={{0,4},{4,0},{8,12},{12,8},{1,5},{5,1},{9,13},{13,9},{2,6},{6,2},{1... | collective-permute-start | bytes 147464 | tf_op jit(solution)/shard_map/ppermute | solution.py:659
  28.3 2.4 %collective-permute-done.6 = f32[96,128]{1,0:T(8,128)S(1)} collective-permute-done((f32[96,128]{1,0:T(8,128)S(1)}, f32[96,128]{1,0:T(8,128)S(1)}, u32[]{:S(2)}, u32[]{:S(2)}) %collective-permute-start.6) | collective-permute-done | bytes 49184 | tf_op jit(solution)/shard_map/ppermute | solution.py:659
  30.6 0.7 %collective-permute-start.7 = (f32[96,128]{1,0:T(8,128)S(1)}, f32[96,128]{1,0:T(8,128)S(1)}, u32[]{:S(2)}, u32[]{:S(2)}) collective-permute-start(f32[96,128]{1,0:T(8,128)S(1)} %add.30.mine_ref), channel_id=1, source_target_pairs={{0,8},{4,12},{8,0},{12,4},{1,9},{5,13},{9,1},{13,5},{2,10},{6,14},... | collective-permute-start | bytes 147464 | tf_op jit(solution)/shard_map/ppermute | solution.py:659
  31.4 3.0 %shard_map.152 = bf16[32,8,256]{2,1,0:T(8,128)(2,1)} custom-call(s32[32]{0:T(128)S(1)} %broadcast_clamp_fusion.levels_ref, f32[4,16,384]{2,1,0:T(8,128)S(1)} %get-tuple-element.83.wind_ref, f32[32,4608]{1,0:T(8,128)S(1)} %get-tuple-element.98.second_ref, bf16[64,64]{1,0:T(8,128)(2,1)S(1)} %get-tuple-element.99.head_ref, bf16[32,8,256]{2,1,0:T(8,128)(2,1)S(1)} %copy-done, ...), custom_call_target="tpu_custom_call" | custom-call | flops 2000000 | bytes 2000000 | tf_op jit(solution)/shard_map/pallas_call | solution.py:631
  34.4 1.3 %collective-permute-done.7.other_ref = f32[96,128]{1,0:T(8,128)S(1)} collective-permute-done((f32[96,128]{1,0:T(8,128)S(1)}, f32[96,128]{1,0:T(8,128)S(1)}, u32[]{:S(2)}, u32[]{:S(2)}) %collective-permute-start.7) | collective-permute-done | bytes 49184 | tf_op jit(solution)/shard_map/ppermute | solution.py:659
  35.7 0.9 %shard_map.153 = (f32[32,36]{1,0:T(8,128)}, f32[1,32]{1,0:T(1,128)}, f32[32,288]{1,0:T(8,128)}, f32[1,32]{1,0:T(1,128)}, f32[18,32]{1,0:T(8,128)}) custom-call(f32[96,128]{1,0:T(8,128)S(1)} %add.30.mine_ref, f32[96,128]{1,0:T(8,128)S(1)} %collective-permute-done.7.other_ref, bf16[384,288]{1,0:T(8,128)(2,1)S(1)} %get-tuple-element.102.pick2_ref, ...), custom_call_target="tpu_custom_call" | custom-call | flops 200000 | bytes 2000000 | tf_op jit(solution)/shard_map/pallas_call | solution.py:631
  (9 shorter events, 0.1 us)
Async XLA Ops:
  2.5 4.9 %collective-permute-start = (bf16[6,8,128]{2,1,0:T(8,128)(2,1)}, bf16[6,8,128]{2,1,0:T(8,128)(2,1)S(1)}, u32[]{:S(2)}, u32[]{:S(2)}) collective-permute-start(bf16[6,8,128]{2,1,0:T(8,128)(2,1)} %get-tuple-element.58), channel_id=1, source_target_pairs={{0,2},{2,0},{1,3},{3,1},{4,6},{6,4},{5,7},{7,5},{8,10},{10,8},{9,1... | collective-permute-start | bytes 36872 | tf_op jit(solution)/shard_map/ppermute | solution.py:688
  5.5 0.7 %copy-start.9 = (s32[32]{0:T(128)S(1)}, s32[32]{0:T(128)}, u32[]{:S(2)}) copy-start(s32[32]{0:T(128)} %param.12) | copy-start | bytes 388
  6.2 1.0 %copy-start.8 = (bf16[52,4,256]{2,1,0:T(4,128)(2,1)S(1)}, bf16[52,4,256]{2,1,0:T(4,128)(2,1)}, u32[]{:S(2)}) copy-start(bf16[52,4,256]{2,1,0:T(4,128)(2,1)} %get-tuple-element.60) | copy-start | bytes 319492
  7.2 4.4 %copy-start = (bf16[32,8,256]{2,1,0:T(8,128)(2,1)S(1)}, bf16[32,8,256]{2,1,0:T(8,128)(2,1)}, u32[]{:S(2)}) copy-start(bf16[32,8,256]{2,1,0:T(8,128)(2,1)} %cot_ref.3) | copy-start | bytes 393220
  7.2 4.4 %copy-start.1 = (bf16[32,8,256]{2,1,0:T(8,128)(2,1)S(1)}, bf16[32,8,256]{2,1,0:T(8,128)(2,1)}, u32[]{:S(2)}) copy-start(bf16[32,8,256]{2,1,0:T(8,128)(2,1)} %tracer_ref.1) | copy-start | bytes 393220
  7.4 8.7 %collective-permute-start.2 = (bf16[55,4,256]{2,1,0:T(4,128)(2,1)S(1)}, bf16[55,4,256]{2,1,0:T(4,128)(2,1)S(1)}, u32[]{:S(2)}, u32[]{:S(2)}) collective-permute-start(bf16[55,4,256]{2,1,0:T(4,128)(2,1)S(1)} %get-tuple-element.111), channel_id=1, source_target_pairs={{0,12},{4,8},{8,4},{12,0},{1,13},{5,9},{9,5},{13,1},{2,14},{6,10},... | collective-permute-start | bytes 337928 | tf_op jit(solution)/shard_map/ppermute | solution.py:731
  11.6 4.9 %collective-permute-start.1 = (bf16[55,4,256]{2,1,0:T(4,128)(2,1)S(1)}, bf16[55,4,256]{2,1,0:T(4,128)(2,1)S(1)}, u32[]{:S(2)}, u32[]{:S(2)}) collective-permute-start(bf16[55,4,256]{2,1,0:T(4,128)(2,1)S(1)} %get-tuple-element.112), channel_id=1, source_target_pairs={{0,4},{4,0},{8,12},{12,8},{1,5},{5,1},{9,13},{13,9},{2,6},{6,2},{1... | collective-permute-start | bytes 337928 | tf_op jit(solution)/shard_map/ppermute | solution.py:731
  11.6 2.4 %copy-start.3 = (f32[32,288]{1,0:T(8,128)S(1)}, f32[32,288]{1,0:T(8,128)}, u32[]{:S(2)}) copy-start(f32[32,288]{1,0:T(8,128)} %c2_hbm) | copy-start | bytes 110596
  11.7 2.4 %copy-start.4 = (f32[32,36]{1,0:T(8,128)S(1)}, f32[32,36]{1,0:T(8,128)}, u32[]{:S(2)}) copy-start(f32[32,36]{1,0:T(8,128)} %c1_hbm) | copy-start | bytes 13828
  11.7 2.4 %copy-start.5 = (f32[18,32]{1,0:T(8,128)S(1)}, f32[18,32]{1,0:T(8,128)}, u32[]{:S(2)}) copy-start(f32[18,32]{1,0:T(8,128)} %head_hbm) | copy-start | bytes 6916
  13.9 0.7 %copy-start.6 = (f32[32]{0:T(128)S(1)}, f32[32]{0:T(128)}, u32[]{:S(2)}) copy-start(f32[32]{0:T(128)} %param.14) | copy-start | bytes 388
  14.0 0.7 %copy-start.7 = (f32[32]{0:T(128)S(1)}, f32[32]{0:T(128)}, u32[]{:S(2)}) copy-start(f32[32]{0:T(128)} %param.16) | copy-start | bytes 388
  14.0 1.3 %copy-start.2 = (f32[4,8,256]{2,1,0:T(8,128)S(1)}, f32[4,8,256]{2,1,0:T(8,128)}, u32[]{:S(2)}) copy-start(f32[4,8,256]{2,1,0:T(8,128)} %own_ref.3) | copy-start | bytes 98308
  14.0 2.6 %collective-permute-start.3 = (f32[18,8,384]{2,1,0:T(8,128)S(1)}, f32[18,8,384]{2,1,0:T(8,128)S(1)}, u32[]{:S(2)}, u32[]{:S(2)}) collective-permute-start(f32[18,8,384]{2,1,0:T(8,128)S(1)} %get-tuple-element.84.inner_ref), channel_id=1, source_target_pairs={{0,1},{1,0},{2,3},{3,2},{4,5},{5,4},{6,7},{7,6},{8,9},{9,8},{10,11... | collective-permute-start | bytes 663560 | tf_op jit(solution)/shard_map/ppermute | solution.py:760
  18.8 1.5 %collective-permute-start.4 = (f32[18,8,384]{2,1,0:T(8,128)S(1)}, f32[18,8,384]{2,1,0:T(8,128)S(1)}, u32[]{:S(2)}, u32[]{:S(2)}) collective-permute-start(f32[18,8,384]{2,1,0:T(8,128)S(1)} %shard_map.149.border_ref), channel_id=1, source_target_pairs={{0,1},{1,0},{2,3},{3,2},{4,5},{5,4},{6,7},{7,6},{8,9},{9,8},{10,11... | collective-permute-start | bytes 663560 | tf_op jit(solution)/shard_map/ppermute | solution.py:769
  22.3 4.2 %collective-permute-start.5 = (f32[96,128]{1,0:T(8,128)S(1)}, f32[96,128]{1,0:T(8,128)S(1)}, u32[]{:S(2)}, u32[]{:S(2)}) collective-permute-start(f32[96,128]{1,0:T(8,128)S(1)} %get-tuple-element.91), channel_id=1, source_target_pairs={{0,2},{2,0},{1,3},{3,1},{4,6},{6,4},{5,7},{7,5},{8,10},{10,8},{9,1... | collective-permute-start | bytes 147464 | tf_op jit(solution)/shard_map/ppermute | solution.py:659
  26.5 4.1 %collective-permute-start.6 = (f32[96,128]{1,0:T(8,128)S(1)}, f32[96,128]{1,0:T(8,128)S(1)}, u32[]{:S(2)}, u32[]{:S(2)}) collective-permute-start(f32[96,128]{1,0:T(8,128)S(1)} %add.29), channel_id=1, source_target_pairs={{0,4},{4,0},{8,12},{12,8},{1,5},{5,1},{9,13},{13,9},{2,6},{6,2},{1... | collective-permute-start | bytes 147464 | tf_op jit(solution)/shard_map/ppermute | solution.py:659
  30.6 5.0 %collective-permute-start.7 = (f32[96,128]{1,0:T(8,128)S(1)}, f32[96,128]{1,0:T(8,128)S(1)}, u32[]{:S(2)}, u32[]{:S(2)}) collective-permute-start(f32[96,128]{1,0:T(8,128)S(1)} %add.30.mine_ref), channel_id=1, source_target_pairs={{0,8},{4,12},{8,0},{12,4},{1,9},{5,13},{9,1},{13,5},{2,10},{6,14},... | collective-permute-start | bytes 147464 | tf_op jit(solution)/shard_map/ppermute | solution.py:659
